TPU v7x, 32 devices: a whole 2x2x4 slice. The times are simulated.
32 devices in a mesh: dp: 8 (over y, x, core), tp: 4 (over z).
Axes of the slice: x: 2, y: 2, z: 4, core: 2. Of those that a mesh axis runs over, the one named last changes fastest.
Arguments:
- tokens: bfloat16 [25088, 768], P(('dp', 'tp')), may hold values from -6 to 6
- heights: int32 [8], P('dp'), may hold values from 43 to 56, as said below
- widths: int32 [8], P('dp'), may hold values from 15 to 56
- norm_gain: bfloat16 [2, 768], replicated, may hold values from 0.25 to 1.75
- norm_bias: bfloat16 [2, 768], replicated, may hold values from -1.796875 to 1.796875
- w_qkv: bfloat16 [3, 768, 768], P(None, None, 'tp'), may hold values from -0.21875 to 0.21875
- b_qv: bfloat16 [2, 768], P(None, 'tp'), may hold values from -1.796875 to 1.796875
- rel_pos: bfloat16 [2, 27, 64], replicated, may hold values from -0.8984375 to 0.8984375
- w_proj: bfloat16 [768, 768], P('tp'), may hold values from -1.75 to 1.75
- b_proj: bfloat16 [768], replicated, may hold values from -1.796875 to 1.796875
- w_fc1: bfloat16 [768, 3072], P(None, 'tp'), may hold values from -0.21875 to 0.21875
- b_fc1: bfloat16 [3072], P('tp'), may hold values from -1.796875 to 1.796875
- w_fc2: bfloat16 [3072, 768], P('tp'), may hold values from -0.21875 to 0.21875
- b_fc2: bfloat16 [768], replicated, may hold values from -1.796875 to 1.796875
- cotangent: bfloat16 [25088, 768], P(('dp', 'tp')), may hold values from -6 to 6
Outputs:
- out: bfloat16 [25088, 768], P(('dp', 'tp'))
- grad_tokens: float32 [25088, 768], P(('dp', 'tp'))
- grad_norm_gain: float32 [2, 768], replicated
- grad_norm_bias: float32 [2, 768], replicated
- grad_qkv: float32 [3, 768, 768], P(None, None, 'tp')
- grad_b_qv: float32 [2, 768], P(None, 'tp')
- grad_rel_pos: float32 [2, 27, 64], replicated
- grad_proj: float32 [768, 768], P('tp')
- grad_b_proj: float32 [768], replicated
- grad_fc1: float32 [768, 3072], P(None, 'tp')
- grad_b_fc1: float32 [3072], P('tp')
- grad_fc2: float32 [3072, 768], P('tp')
- grad_b_fc2: float32 [768], replicated
Inputs may be any that keep to these rules, and one draw needn't show every extreme that they name: `heights`: patch rows of each image; the last row of windows always holds patches.
All inputs are finite; a program needn't handle non-finite values.
Results may differ from a plain program's by a relative error of at most 0.018.
Values may be sent and summed in bfloat16 or wider, within the bound.
A program may use at most 192 MiB of HBM per device.

v0:
```python
from functools import partial
import math

import jax
import jax.numpy as jnp
from jax import lax
from jax.sharding import PartitionSpec as P

HEAD_DIM = 64
WIN = 14
GRID = 4


highest = lax.Precision.HIGHEST
neg_fill = -30000.0


def layer_norm(values, norm_gains, shifts):
    centre = jnp.mean(values, axis=-1, keepdims=True)
    centred = values - centre
    spread = jnp.mean(centred * centred, axis=-1, keepdims=True)
    return centred * lax.rsqrt(spread + 1e-06) * norm_gains + shifts


def valid_slots(height, breadth, start, slot_count):
    index = start + jnp.arange(slot_count, dtype=jnp.int32)
    window = index // (WIN * WIN)
    inside = index % (WIN * WIN)
    row_at = window // GRID * WIN + inside // WIN
    column_at = window % GRID * WIN + inside % WIN
    return (row_at < height) & (column_at < breadth)


def offset_onehot():
    offsets = (
        jnp.arange(WIN, dtype=jnp.int32)[:, None]
        - jnp.arange(WIN, dtype=jnp.int32)[None, :]
        + (WIN - 1)
    )
    return (offsets[:, :, None] == jnp.arange(2 * WIN - 1, dtype=jnp.int32)[None, None, :]).astype(
        jnp.float32
    )


def relative_tables(rel_table):
    return jnp.einsum("ykj,tjc->tykc", offset_onehot(), rel_table, precision=highest)


def window_block():
    return 4


def window_scores(queries, key_rows, tables):
    leading = queries.shape[:2]
    grid_q = queries.reshape(leading + (WIN, WIN, HEAD_DIM))
    direct = jnp.einsum(
        "nhqc,nhkc->nhqk", queries, key_rows, preferred_element_type=jnp.float32
    ) / math.sqrt(HEAD_DIM)
    along_h = jnp.einsum("nhyxc,ykc->nhyxk", grid_q, tables[0], preferred_element_type=jnp.float32)
    along_w = jnp.einsum("nhyxc,xkc->nhyxk", grid_q, tables[1], preferred_element_type=jnp.float32)
    combined = (
        direct.reshape(leading + (WIN, WIN, WIN, WIN))
        + along_h[..., :, None]
        + along_w[..., None, :]
    )
    return combined.reshape(leading + (WIN * WIN, WIN * WIN))


def attend_forward(pieces, tables):
    q_block, k_block, v_block, keep_block = pieces
    scores = window_scores(q_block, k_block, tables)
    scores = jnp.where(keep_block[:, None, None, :], scores, neg_fill)
    summit = jnp.max(scores, axis=-1, keepdims=True)
    weights = jnp.exp(scores - summit)
    denominator = jnp.sum(weights, axis=-1, keepdims=True)
    attention = (weights / denominator).astype(jnp.bfloat16)
    mixture = jnp.einsum("nhqk,nhkc->nhqc", attention, v_block, preferred_element_type=jnp.float32)
    return (mixture.astype(jnp.bfloat16), summit + jnp.log(denominator))


def attend_backward(pieces, tables):
    q_block, k_block, v_block, keep_block, log_total, d_block = pieces
    leading = q_block.shape[:2]
    scores = window_scores(q_block, k_block, tables)
    scores = jnp.where(keep_block[:, None, None, :], scores, neg_fill)
    attention = jnp.exp(scores - log_total)
    d_attn = jnp.einsum("nhqc,nhkc->nhqk", d_block, v_block, preferred_element_type=jnp.float32)
    inner = jnp.sum(d_attn * attention, axis=-1, keepdims=True)
    d_scores = (attention * (d_attn - inner)).astype(jnp.bfloat16)
    d_values = jnp.einsum(
        "nhqk,nhqc->nhkc",
        attention.astype(jnp.bfloat16),
        d_block,
        preferred_element_type=jnp.float32,
    )
    d_keys = jnp.einsum(
        "nhqk,nhqc->nhkc", d_scores, q_block, preferred_element_type=jnp.float32
    ) / math.sqrt(HEAD_DIM)
    d_queries = jnp.einsum(
        "nhqk,nhkc->nhqc", d_scores, k_block, preferred_element_type=jnp.float32
    ) / math.sqrt(HEAD_DIM)
    grid_d = d_scores.astype(jnp.float32).reshape(leading + (WIN, WIN, WIN, WIN))
    d_rows = jnp.sum(grid_d, axis=5)
    d_cols = jnp.sum(grid_d, axis=4)
    tables_wide = tables.astype(jnp.float32)
    extra = jnp.einsum("nhyxk,ykc->nhyxc", d_rows, tables_wide[0], precision=highest)
    extra = extra + jnp.einsum("nhyxk,xkc->nhyxc", d_cols, tables_wide[1], precision=highest)
    d_queries = d_queries + extra.reshape(leading + (WIN * WIN, HEAD_DIM))
    grid_q = q_block.astype(jnp.float32).reshape(leading + (WIN, WIN, HEAD_DIM))
    table_rows = jnp.einsum("nhyxk,nhyxc->ykc", d_rows, grid_q, precision=highest)
    table_cols = jnp.einsum("nhyxk,nhyxc->xkc", d_cols, grid_q, precision=highest)
    return (d_queries, d_keys, d_values, jnp.stack([table_rows, table_cols]))


def body(
    tokens,
    heights,
    widths,
    norm_gain,
    norm_bias,
    w_qkv,
    b_qv,
    rel_pos,
    w_proj,
    b_proj,
    w_fc1,
    b_fc1,
    w_fc2,
    b_fc2,
    cotangent,
):
    local_rows = tokens.shape[0]
    local_start = lax.axis_index("tp") * local_rows
    height = heights[0]
    breadth = widths[0]
    weights = (w_qkv, b_qv, w_proj, w_fc1, b_fc1, w_fc2)
    compute_start = 0
    compute_rows = local_rows * lax.axis_size("tp")
    qkv_weight, qv_bias, proj_weight, fc1_weight, fc1_bias, fc2_weight = weights
    inputs_wide = tokens.astype(jnp.float32)
    norm_gains = norm_gain.astype(jnp.float32)
    shifts = norm_bias.astype(jnp.float32)
    masking = valid_slots(height, breadth, local_start, local_rows)[:, None].astype(jnp.float32)
    keep_all = valid_slots(height, breadth, compute_start, compute_rows)
    tables = relative_tables(rel_pos.astype(jnp.float32)).astype(jnp.bfloat16)
    normed_one, first_back = jax.vjp(layer_norm, inputs_wide, norm_gains[0], shifts[0])
    normed = lax.all_gather(normed_one.astype(jnp.bfloat16), "tp", axis=0, tiled=True)
    projected = jnp.einsum("rd,tde->tre", normed, qkv_weight, preferred_element_type=jnp.float32)
    bias_wide = qv_bias.astype(jnp.float32)
    queries = (projected[0] + bias_wide[0]).astype(jnp.bfloat16)
    key_rows = projected[1].astype(jnp.bfloat16)
    values = (projected[2] + bias_wide[1]).astype(jnp.bfloat16)
    head_count = queries.shape[1] // HEAD_DIM
    windows = compute_rows // (WIN * WIN)
    per_block = window_block()
    blocks = windows // per_block

    def to_heads(flat):
        return flat.reshape(blocks, per_block, WIN * WIN, head_count, HEAD_DIM).transpose(
            0, 1, 3, 2, 4
        )

    def from_heads(grouped):
        return grouped.transpose(0, 1, 3, 2, 4).reshape(compute_rows, head_count * HEAD_DIM)

    grouped_inputs = (
        to_heads(queries),
        to_heads(key_rows),
        to_heads(values),
        keep_all.reshape(blocks, per_block, WIN * WIN),
    )
    mixed_heads, log_totals = lax.map(partial(attend_forward, tables=tables), grouped_inputs)
    mixture = from_heads(mixed_heads)
    branch = lax.psum_scatter(
        jnp.dot(mixture, proj_weight, preferred_element_type=jnp.float32).astype(jnp.bfloat16),
        "tp",
        scatter_dimension=0,
        tiled=True,
    ).astype(jnp.float32)
    middle = inputs_wide + masking * (branch + b_proj.astype(jnp.float32))
    normed_mid, second_back = jax.vjp(layer_norm, middle, norm_gains[1], shifts[1])
    normed_two = lax.all_gather(normed_mid.astype(jnp.bfloat16), "tp", axis=0, tiled=True)
    before = jnp.dot(normed_two, fc1_weight, preferred_element_type=jnp.float32) + fc1_bias.astype(
        jnp.float32
    )
    activated, gelu_back = jax.vjp(partial(jax.nn.gelu, approximate=False), before)
    hidden = activated.astype(jnp.bfloat16)
    branch_two = lax.psum_scatter(
        jnp.dot(
            lax.dynamic_slice_in_dim(hidden, jnp.int32(0), lax.axis_size("tp") * local_rows, 0),
            fc2_weight,
            preferred_element_type=jnp.float32,
        ).astype(jnp.bfloat16),
        "tp",
        scatter_dimension=0,
        tiled=True,
    ).astype(jnp.float32)
    result = (middle + masking * (branch_two + b_fc2.astype(jnp.float32))).astype(jnp.bfloat16)
    d_output = cotangent.astype(jnp.float32)
    masked_out = masking * d_output
    grad_bias_two = jnp.sum(masked_out, axis=0)
    d_second = lax.all_gather(masked_out.astype(jnp.bfloat16), "tp", axis=0, tiled=True)
    grad_second = jnp.einsum("rf,rd->fd", hidden, d_second, preferred_element_type=jnp.float32)
    d_hidden = jnp.einsum("rd,fd->rf", d_second, fc2_weight, preferred_element_type=jnp.float32)
    d_before = gelu_back(d_hidden)[0].astype(jnp.bfloat16)
    grad_bias_one = jnp.sum(d_before.astype(jnp.float32), axis=0)
    grad_first = jnp.einsum("rd,rf->df", normed_two, d_before, preferred_element_type=jnp.float32)
    d_normed_two = lax.psum_scatter(
        jnp.einsum("rf,df->rd", d_before, fc1_weight, preferred_element_type=jnp.float32).astype(
            jnp.bfloat16
        ),
        "tp",
        scatter_dimension=0,
        tiled=True,
    ).astype(jnp.float32)
    d_mid_norm, gain_two, shift_two = second_back(d_normed_two)
    d_middle = d_output + d_mid_norm
    masked_mid = masking * d_middle
    grad_bias_proj = jnp.sum(masked_mid, axis=0)
    d_first = lax.all_gather(masked_mid.astype(jnp.bfloat16), "tp", axis=0, tiled=True)
    grad_projection = jnp.einsum("re,rd->ed", mixture, d_first, preferred_element_type=jnp.float32)
    d_mixture = jnp.einsum(
        "rd,ed->re", d_first, proj_weight, preferred_element_type=jnp.float32
    ).astype(jnp.bfloat16)
    back_inputs = grouped_inputs + (log_totals, to_heads(d_mixture))
    dq_heads, dk_heads, dv_heads, table_grads = lax.map(
        partial(attend_backward, tables=tables), back_inputs
    )
    d_queries = from_heads(dq_heads).astype(jnp.bfloat16)
    d_keys = from_heads(dk_heads).astype(jnp.bfloat16)
    d_values = from_heads(dv_heads).astype(jnp.bfloat16)
    d_stack = jnp.stack([d_queries, d_keys, d_values])
    grad_attention_in = jnp.einsum(
        "rd,tre->tde", normed, d_stack, preferred_element_type=jnp.float32
    )
    grad_qv_bias = jnp.stack(
        [
            jnp.sum(d_queries.astype(jnp.float32), axis=0),
            jnp.sum(d_values.astype(jnp.float32), axis=0),
        ]
    )
    d_normed_one = lax.psum_scatter(
        jnp.einsum("tre,tde->rd", d_stack, qkv_weight, preferred_element_type=jnp.float32).astype(
            jnp.bfloat16
        ),
        "tp",
        scatter_dimension=0,
        tiled=True,
    ).astype(jnp.float32)
    d_input_norm, gain_one, shift_one = first_back(d_normed_one)
    grad_inputs = d_middle + d_input_norm
    table_total = jnp.sum(table_grads, axis=0)
    grad_table = jnp.einsum("ykj,tykc->tjc", offset_onehot(), table_total, precision=highest)
    shared = lax.psum(
        (
            jnp.stack([gain_one, gain_two]),
            jnp.stack([shift_one, shift_two]),
            grad_table,
            grad_bias_proj,
            grad_bias_two,
        ),
        ("dp", "tp"),
    )
    weight_grads = (
        grad_attention_in,
        grad_qv_bias,
        grad_projection,
        grad_first,
        grad_bias_one,
        grad_second,
    )
    summed = lax.psum(
        (
            weight_grads[0],
            weight_grads[1],
            weight_grads[2],
            weight_grads[3],
            weight_grads[4],
            weight_grads[5],
        ),
        "dp",
    )
    return (
        result,
        grad_inputs,
        shared[0],
        shared[1],
        summed[0],
        summed[1],
        shared[2],
        summed[2],
        shared[3],
        summed[3],
        summed[4],
        summed[5],
        shared[4],
    )


def solution(mesh):
    placed = (
        P(("dp", "tp"), None),
        P("dp"),
        P("dp"),
        P(),
        P(),
        P(None, None, "tp"),
        P(None, "tp"),
        P(),
        P("tp", None),
        P(),
        P(None, "tp"),
        P("tp"),
        P("tp", None),
        P(),
        P(("dp", "tp"), None),
    )
    return jax.shard_map(
        body,
        mesh=mesh,
        in_specs=placed,
        out_specs=(
            P(("dp", "tp"), None),
            P(("dp", "tp"), None),
            P(),
            P(),
            P(None, None, "tp"),
            P(None, "tp"),
            P(),
            P("tp", None),
            P(),
            P(None, "tp"),
            P("tp"),
            P("tp", None),
            P(),
        ),
        check_vma=False,
    )
```

profile of v0, /device:TPU:0, one launch (start us, length us, event | category | flops | bytes accessed | tf_op | source)
XLA Modules:
  0.0 1623.8 jit_solution(9236804614198621510)
XLA Ops:
  16.5 91.6 %all-gather.5.cloned.1.call-done = bf16[3136,768]{1,0:T(8,128)(2,1)} async-done(((bf16[784,768]{1,0:T(8,128)(2,1)}), bf16[3136,768]{1,0:T(8,128)(2,1)}) %all-gather.5.cloned.1.call-update) | async-done | bytes 4816912 | tf_op jit(solution)/shard_map/all_gather | solution.py:147
  151.7 233.8 %while.28 = (s32[]{:T(128)}, bf16[4,4,3,196,64]{3,4,2,1,0:T(8,128)(2,1)}, f32[4,4,3,196,1]{3,2,1,4,0:T(4,128)}, pred[4,4,196]{2,1,0:T(4,128)(4,1)S(1)}, bf16[4,4...) while((s32[]{:T(128)}, ...), condition=%wide.region_5.6_spmd, body=%wide.region_2.5_spmd.sunk | while | flops 131201616 | bytes 34155604 | solution.py:172
  156.4 8.1 add.620
  164.6 12.7 add.621
  187.7 12.7 add.623
  214.9 8.1 add.620
  223.0 12.7 add.621
  246.1 12.7 add.623
  273.3 8.1 add.620
  281.4 12.7 add.621
  304.5 12.7 add.623
  331.7 8.1 add.620
  339.8 12.7 add.621
  362.9 12.7 add.623
  397.7 84.7 %reduce-scatter.5.cloned.1.call-done = bf16[784,768]{1,0:T(8,128)(2,1)} async-done(((bf16[3136,768]{1,0:T(8,128)(2,1)}), bf16[784,768]{1,0:T(8,128)(2,1)}) %reduce-scatter.5.cloned.1.call-update) | async-done | bytes 1204240 | tf_op jit(solution)/shard_map/reduce_scatter | solution.py:174
  488.6 91.1 %all-gather.7.cloned.1.call-done = bf16[3136,768]{1,0:T(8,128)(2,1)} async-done(((bf16[784,768]{1,0:T(8,128)(2,1)}), bf16[3136,768]{1,0:T(8,128)(2,1)}) %all-gather.7.cloned.1.call-update) | async-done | bytes 4816912 | tf_op jit(solution)/shard_map/all_gather | solution.py:182
  579.6 10.8 fusion.144
  590.4 80.7 %all-gather.9.cloned.1.call-done = bf16[3136,768]{1,0:T(8,128)(2,1)} async-done(((bf16[784,768]{1,0:T(8,128)(2,1)}), bf16[3136,768]{1,0:T(8,128)(2,1)}) %all-gather.9.cloned.1.call-update) | async-done | bytes 4816912 | tf_op jit(solution)/shard_map/all_gather | solution.py:202
  671.1 29.1 %convert_reduce_fusion = (f32[768]{0:T(1024)}, bf16[3136,768]{1,0:T(8,128)(2,1)S(1)}, f32[3136,768]{1,0:T(8,128)}) fusion(f32[3136,768]{1,0:T(8,128)} %fusion.144, f32[768]{0:T(1024)S(1)} %convert_element_type.197, bf16[3136,768]{1,0:T(8,128)(2,1)} %all-gather.9.cloned.1.call-done, bf16[768,768]{1,0:T(8,128)(2,1)S(1)} %copy-done), kind=kOutput, calls=%fused_computation.88 | convolution fusion | flops 3880008960 | bytes 30087168 | tf_op jit(solution)/shard_map/rd,fd->rf/dot_general | solution.py:204
  708.2 10.9 multiply_convert_fusion.1
  727.7 65.9 %reduce-scatter.9.cloned.1.call-done = bf16[784,768]{1,0:T(8,128)(2,1)} async-done(((bf16[3136,768]{1,0:T(8,128)(2,1)}), bf16[784,768]{1,0:T(8,128)(2,1)}) %reduce-scatter.9.cloned.1.call-update) | async-done | bytes 1204240 | tf_op jit(solution)/shard_map/reduce_scatter | solution.py:208
  797.3 85.8 %reduce-scatter.7.cloned.1.call-done = bf16[784,768]{1,0:T(8,128)(2,1)} async-done(((bf16[3136,768]{1,0:T(8,128)(2,1)}), bf16[784,768]{1,0:T(8,128)(2,1)}) %reduce-scatter.7.cloned.1.call-update) | async-done | bytes 1204240 | tf_op jit(solution)/shard_map/reduce_scatter | solution.py:188
  890.3 91.6 %all-gather.11.cloned.1.call-done = bf16[3136,768]{1,0:T(8,128)(2,1)} async-done(((bf16[784,768]{1,0:T(8,128)(2,1)}), bf16[3136,768]{1,0:T(8,128)(2,1)}) %all-gather.11.cloned.1.call-update) | async-done | bytes 4816912 | tf_op jit(solution)/shard_map/all_gather | solution.py:220
  995.1 377.8 %while.29 = (s32[]{:T(128)}, bf16[4,4,3,196,64]{3,4,2,1,0:T(8,128)(2,1)}, bf16[4,4,3,196,64]{3,4,2,1,0:T(8,128)(2,1)}, bf16[4,4,3,196,64]{3,4,2,1,0:T(8,128)(2,1...) while((s32[]{:T(128)}, ...), condition=%wide.region_17.18_spmd, body=%wide.region_13.17_spmd.sunk | while | flops 411171136 | bytes 79734752 | solution.py:226
  999.9 8.1 add.629
  1008.0 12.7 add.630
  1031.1 12.7 add.632
  1056.6 12.7 reshape.337
  1069.3 9.3 fusion.239
  1094.2 8.1 add.629
  1102.3 12.7 add.630
  1125.4 12.7 add.632
  1150.9 12.7 reshape.337
  1163.6 9.3 fusion.239
  1196.6 12.7 add.630
  1219.7 12.7 add.632
  1245.2 12.7 reshape.337
  1257.9 9.3 fusion.239
  1291.0 12.7 add.630
  1314.1 12.7 add.632
  1339.5 12.7 reshape.337
  1352.2 9.3 fusion.239
  1404.5 9.6 fusion.146
  1414.1 9.6 fusion.147
  1434.8 15.7 all-reduce.1
  1450.8 38.9 %reduce-scatter.11.cloned.1.call-done = bf16[784,768]{1,0:T(8,128)(2,1)} async-done(((bf16[3136,768]{1,0:T(8,128)(2,1)}), bf16[784,768]{1,0:T(8,128)(2,1)}) %reduce-scatter.11.cloned.1.call-update) | async-done | bytes 1204240 | tf_op jit(solution)/shard_map/reduce_scatter | solution.py:242
  1493.5 42.6 %all-reduce = (f32[2,768]{1,0:T(2,128)}, f32[2,768]{1,0:T(2,128)}, f32[2,27,64]{2,1,0:T(8,128)S(1)}, f32[768]{0:T(1024)}, f32[768]{0:T(1024)}) all-reduce(f32[2,768]{1,0:T(2,128)S(1)} %pad_maximum_fusion, f32[2,768]{1,0:T(2,128)S(1)} %pad_maximum_fusion.1, ...), channel_id=1, replica_groups=mesh['dp'=8,'tp'=4] {'dp','tp'}, use_global_device_ids=true, to_apply=%region_23.24 | all-reduce | flops 8064 | bytes 64512 | tf_op jit(solution)/shard_map/psum | solution.py:254
  1540.9 68.4 %all-reduce.5.cloned.1.call-done = (f32[3,768,192]{1,2,0:T(8,128)}, f32[192,768]{1,0:T(8,128)}, f32[768,768]{1,0:T(8,128)}, f32[768,768]{1,0:T(8,128)}) async-done(((f32[3,768,192]{1,2,0:T(8,128)}, f32[192,768]{1,0:T(8,128)}, f32[768,768]{1,0:T(8,128)}, f32[768,768]{1,0:T(8,128)}), (f32[3,768,192]{1,2,0:T(8,128)}, f32[192,768]{1,0:T(8,128)}, f32[768,768]{1,0:T(8,128)}, ...) | async-done | bytes 7077904 | tf_op jit(solution)/shard_map/psum | solution.py:272
  (441 shorter events, 439.1 us)
Async XLA Ops:
  7.2 663.9 %copy-start = (bf16[768,768]{1,0:T(8,128)(2,1)S(1)}, bf16[768,768]{1,0:T(8,128)(2,1)}, u32[]{:S(2)}) copy-start(bf16[768,768]{1,0:T(8,128)(2,1)} %param.31) | copy-start | bytes 3538948
  7.2 5.5 copy-start.2
  7.2 3.7 copy-start.52
  7.2 4.3 copy-start.53
  7.2 100.9 %all-gather.5.cloned.1.call-start = ((), (), s32[]{:S(2)}) async-start(), calls=%async_computation.4 | async-start | bytes 6021120 | tf_op jit(solution)/shard_map/all_gather | solution.py:147
  9.0 6.6 copy-start.57
  9.0 6.8 copy-start.45
  9.0 99.1 %copy-start.59 = (bf16[3,768,192]{1,2,0:T(8,128)(2,1)S(1)}, bf16[3,768,192]{1,2,0:T(8,128)(2,1)}, u32[]{:S(2)}) copy-start(bf16[3,768,192]{1,2,0:T(8,128)(2,1)} %param.24) | copy-start | bytes 2654212
  14.2 468.2 %reduce-scatter.5.cloned.1.call-start = ((), (), s32[]{:S(2)}) async-start(), calls=%async_computation.5 | async-start | bytes 6021120 | tf_op jit(solution)/shard_map/reduce_scatter | solution.py:174
  385.6 7.7 copy-start.8
  385.6 7.7 copy-start.29
  393.3 3.7 copy-start.15
  396.9 85.5 %copy-start.3 = (bf16[784,768]{1,0:T(8,128)(2,1)S(1)}, bf16[784,768]{1,0:T(8,128)(2,1)}, u32[]{:S(2)}) copy-start(bf16[784,768]{1,0:T(8,128)(2,1)} %param.19) | copy-start | bytes 3612676
  397.0 182.6 %all-gather.7.cloned.1.call-start = ((), (), s32[]{:S(2)}) async-start(), calls=%async_computation.6 | async-start | bytes 6021120 | tf_op jit(solution)/shard_map/all_gather | solution.py:182
  397.7 87.9 %copy-start.36 = (f32[768]{0:T(1024)S(1)}, f32[768]{0:T(1024)}, u32[]{:S(2)}) copy-start(f32[768]{0:T(1024)} %get-tuple-element.375) | copy-start | bytes 9220
  397.7 87.8 %copy-start.50 = (f32[768]{0:T(1024)S(1)}, f32[768]{0:T(1024)}, u32[]{:S(2)}) copy-start(f32[768]{0:T(1024)} %get-tuple-element.306) | copy-start | bytes 9220
  487.9 183.2 %all-gather.9.cloned.1.call-start = ((), (), s32[]{:S(2)}) async-start(), calls=%async_computation.8 | async-start | bytes 6021120 | tf_op jit(solution)/shard_map/all_gather | solution.py:202
  488.5 305.1 %reduce-scatter.9.cloned.1.call-start = ((), (), s32[]{:S(2)}) async-start(), calls=%async_computation.9 | async-start | bytes 6021120 | tf_op jit(solution)/shard_map/reduce_scatter | solution.py:208
  671.1 31.3 %copy-start.58 = (bf16[768,768]{1,0:T(8,128)(2,1)S(1)}, bf16[768,768]{1,0:T(8,128)(2,1)}, u32[]{:S(2)}) copy-start(bf16[768,768]{1,0:T(8,128)(2,1)} %param.29) | copy-start | bytes 3538948
  708.1 175.0 %reduce-scatter.7.cloned.1.call-start = ((), (), s32[]{:S(2)}) async-start(), calls=%async_computation.7 | async-start | bytes 6021120 | tf_op jit(solution)/shard_map/reduce_scatter | solution.py:188
  727.0 254.9 %all-gather.11.cloned.1.call-start = ((), (), s32[]{:S(2)}) async-start(), calls=%async_computation.10 | async-start | bytes 6021120 | tf_op jit(solution)/shard_map/all_gather | solution.py:220
  883.2 4.7 copy-start.14
  890.2 599.5 %reduce-scatter.11.cloned.1.call-start = ((), (), s32[]{:S(2)}) async-start(), calls=%async_computation.11 | async-start | bytes 6021120 | tf_op jit(solution)/shard_map/reduce_scatter | solution.py:242
  987.1 8.0 copy-start.9
  1047.1 3.6 copy-start.17
  1141.4 3.6 copy-start.17
  1372.9 8.2 copy-start.19
  1383.5 4.4 copy-start.20
  1390.3 5.9 copy-start.21
  1404.2 205.0 %all-reduce.5.cloned.1.call-start = ((), (), s32[]{:S(2)}) async-start(), calls=%async_computation.12 | async-start | bytes 14155776 | tf_op jit(solution)/shard_map/psum | solution.py:272
  1404.5 19.2 %slice-start.2 = ((s8[4816896]{0:T(1024)(128)(4,1)}), s8[4194304]{0:T(1024)(128)(4,1)S(1)}, s32[]{:S(2)}) async-start(s8[4816896]{0:T(1024)(128)(4,1)} %bitcast.316), calls=%async_computation.15 | async-start | bytes 8388608
  1404.5 21.2 %slice-start = ((s8[4816896]{0:T(1024)(128)(4,1)}), s8[4194304]{0:T(1024)(128)(4,1)S(1)}, s32[]{:S(2)}) async-start(s8[4816896]{0:T(1024)(128)(4,1)} %bitcast.314), calls=%async_computation.13 | async-start | bytes 8388608
  1414.1 9.6 copy-start.16
  1414.1 9.6 slice-start.3
  1414.1 11.6 slice-start.1
  1430.2 4.4 copy-start.25
  1430.2 4.5 copy-start.51
  1430.2 20.2 %copy-start.35 = (s32[14,14]{1,0:T(8,128)S(1)}, s32[14,14]{1,0:T(8,128)}, u32[]{:S(2)}) copy-start(s32[14,14]{1,0:T(8,128)} %copy-done.34) | copy-start | bytes 2356
  1430.2 59.5 %copy-start.4 = (bf16[784,768]{1,0:T(8,128)(2,1)S(1)}, bf16[784,768]{1,0:T(8,128)(2,1)}, u32[]{:S(2)}) copy-start(bf16[784,768]{1,0:T(8,128)(2,1)} %param.19) | copy-start | bytes 3612676
  1430.3 59.4 %copy-start.31 = (f32[784]{0:T(1024)S(1)}, f32[784]{0:T(1024)}, u32[]{:S(2)}) copy-start(f32[784]{0:T(1024)} %copy-done.30) | copy-start | bytes 9412
  1430.3 59.4 %copy-start.33 = (f32[768]{0:T(1024)S(1)}, f32[768]{0:T(1024)}, u32[]{:S(2)}) copy-start(f32[768]{0:T(1024)} %copy-done.32) | copy-start | bytes 9220
  1432.8 59.2 %copy-start.44 = (f32[784]{0:T(1024)S(1)}, f32[784]{0:T(1024)}, u32[]{:S(2)}) copy-start(f32[784]{0:T(1024)} %copy-done.43) | copy-start | bytes 9412
  1432.8 59.2 %copy-start.38 = (f32[784]{0:T(1024)S(1)}, f32[784]{0:T(1024)}, u32[]{:S(2)}) copy-start(f32[784]{0:T(1024)} %copy-done.37) | copy-start | bytes 9412
  1450.7 42.8 %copy-start.48 = (f32[768]{0:T(1024)S(1)}, f32[768]{0:T(1024)}, u32[]{:S(2)}) copy-start(f32[768]{0:T(1024)} %get-tuple-element.298) | copy-start | bytes 9220
  1450.8 42.8 %copy-start.49 = (f32[768]{0:T(1024)S(1)}, f32[768]{0:T(1024)}, u32[]{:S(2)}) copy-start(f32[768]{0:T(1024)} %get-tuple-element.299) | copy-start | bytes 9220
  1450.8 86.0 %copy-start.42 = (f32[784]{0:T(1024)S(1)}, f32[784]{0:T(1024)}, u32[]{:S(2)}) copy-start(f32[784]{0:T(1024)} %copy-done.41) | copy-start | bytes 9412
  1609.3 3.8 copy-start.24
  1613.0 3.9 copy-start.1
  (48 other events, 104.1 us)
Sparse Core Ops, SparseCore 0:
  14.4 93.7 all-gather.4
  397.1 85.2 reduce-scatter.4
  488.0 91.5 all-gather.6
  581.6 89.4 all-gather.8
  708.3 85.2 reduce-scatter.8
  795.7 87.3 reduce-scatter.6
  890.4 91.5 all-gather.10
  1404.4 85.2 reduce-scatter.10
  1494.5 114.6 all-reduce.4
where the time goes:
time: 1630 us; the launch traced here: 1620 us
  waiting for transfers between devices  699 us (43%)
  local copies, waits for them, and re-layouts  561 us (34%)
  matrix products  188 us (12%)
  other arithmetic  98.3 us (6%)
  blocking collectives  58.3 us (4%)
    add x48, local copies, waits for them, and re-layouts, window_scores(): direct.reshape(leading + (WIN, WIN, WIN, WIN)) + along_h[..., :, None]  377 us
    all_gather x1, waiting for transfers between devices, body(): lax.all_gather(masked_mid.astype(jnp.bfloat16), 'tp', axis=0, tiled=True)  91.6 us
    all_gather x1, waiting for transfers between devices, body(): lax.all_gather(normed_one.astype(jnp.bfloat16), 'tp', axis=0, tiled=True)  91.6 us
    all_gather x1, waiting for transfers between devices, body(): lax.all_gather(normed_mid.astype(jnp.bfloat16), 'tp', axis=0, tiled=True)  91.1 us
    reduce_scatter x1, waiting for transfers between devices, body(): lax.psum_scatter(jnp.dot(lax.dynamic_slice_in_dim(hidden, jnp.int32(0), l...  85.8 us
    reduce_scatter x1, waiting for transfers between devices, body(): lax.psum_scatter(jnp.dot(mixture, proj_weight, preferred_element_type=jnp...  84.7 us
    all_gather x1, waiting for transfers between devices, body(): lax.all_gather(masked_out.astype(jnp.bfloat16), 'tp', axis=0, tiled=True)  80.7 us
    psum x1, waiting for transfers between devices, body(): lax.psum((weight_grads[0], weight_grads[1], weight_grads[2], weight_grads...  68.4 us
  transfers between devices with their start and end apart: 9, of which 9 were waited for; matrix products, arithmetic and copies ran while one was open for 4% of the time, Pallas kernels for 0%

commit v1 on v0

v1 whole, which is shorter than its diff:
```python
import jax
import jax.numpy as jnp
from jax import lax
from jax.experimental import pallas as pl
from jax.experimental.pallas import tpu as pltpu
from jax.sharding import PartitionSpec as P

HEAD_DIM = 64
WIN = 14
GRID = 4
SLOTS = WIN * WIN
PAD = 208
LANES = 128
HALF = 64

bf16 = jnp.bfloat16
f32 = jnp.float32
neg_fill = -30000.0
pad_fill = -1e30


def dot(a, b, dims=((1,), (0,))):
    return lax.dot_general(a, b, (dims, ((), ())), preferred_element_type=f32)


def window_constants():
    slot = jnp.arange(PAD, dtype=jnp.int32)[:, None]
    lane = jnp.arange(LANES, dtype=jnp.int32)[None, :]
    real = slot < SLOTS
    y, x = slot // WIN, slot % WIN
    shift = jnp.where(real, (WIN - 1) - jnp.where(lane < HALF, y, x), 0)
    bits = jnp.stack([(shift >> b) & 1 for b in range(4)]).astype(jnp.int32)
    inner = lane % HALF
    place = jnp.where(lane < HALF, y, x)
    hot = real & ((inner == place) | (inner - 32 == place)) & ((inner < WIN) | ((inner >= 32) & (inner < 32 + WIN)))
    return bits, hot.astype(bf16)


def position_matrix(rel_pos):
    flipped = rel_pos[:, ::-1, :]
    rows = jnp.pad(flipped, ((0, 0), (0, HALF - flipped.shape[1]), (0, 0))).reshape(LANES, HEAD_DIM)
    return jnp.concatenate([rows, rows], axis=1)


def shift_lanes(values, bits_ref, left):
    for b in range(4):
        amount = LANES - (1 << b) if left else (1 << b)
        moved = pltpu.roll(values, amount, 1)
        mask = bits_ref[b] != 0
        values = jnp.where(jnp.concatenate([mask, mask], axis=0), moved, values)
    return values


def split_heads(pair):
    lane = lax.broadcasted_iota(jnp.int32, pair.shape, 1)
    zero = jnp.zeros_like(pair)
    return jnp.concatenate(
        [jnp.where(lane < HALF, pair, zero), jnp.where(lane < HALF, zero, pair)], axis=0
    )


def merge_heads(stacked):
    top, bottom = stacked[:PAD], stacked[PAD:]
    lane = lax.broadcasted_iota(jnp.int32, top.shape, 1)
    return jnp.where(lane < HALF, top, bottom)


def attend_forward_kernel(q_ref, k_ref, v_ref, fill_ref, rel_ref, hot_ref, bits_ref, mix_ref, p_ref):
    pairs = q_ref.shape[1] // LANES
    fill = fill_ref[0]
    for pair in range(pairs):
        columns = slice(pair * LANES, (pair + 1) * LANES)
        queries = split_heads(q_ref[:, columns])
        bias = shift_lanes(dot(queries, rel_ref[...], ((1,), (1,))), bits_ref, True)
        high = bias.astype(bf16).astype(f32)
        low = pltpu.roll(bias - high, 32, 1)
        lane = lax.broadcasted_iota(jnp.int32, bias.shape, 1)
        bias = jnp.where((lane & 32) == 0, high, low).astype(bf16)
        wide_q = jnp.concatenate([queries * jnp.asarray(0.125, bf16), bias], axis=1)
        wide_k = jnp.concatenate([k_ref[:, columns], hot_ref[...]], axis=1)
        scores = dot(wide_q, wide_k, ((1,), (1,)))
        scores = jnp.where(fill == 0.0, scores, fill)
        summit = jnp.max(scores, axis=1, keepdims=True)
        weights = jnp.exp(scores - summit)
        total = jnp.sum(weights, axis=1, keepdims=True)
        attention = (weights * (1.0 / total)).astype(bf16)
        p_ref[0, pair] = attention
        mix_ref[:, columns] = merge_heads(dot(attention, v_ref[:, columns])).astype(bf16)


def attend_backward_kernel(
    q_ref, k_ref, v_ref, p_ref, d_ref, rel_ref, hot_ref, bits_ref, dq_ref, dk_ref, dv_ref, table_ref
):
    pairs = q_ref.shape[1] // LANES

    @pl.when(pl.program_id(0) == 0)
    def _():
        table_ref[...] = jnp.zeros_like(table_ref)

    for pair in range(pairs):
        columns = slice(pair * LANES, (pair + 1) * LANES)
        attention = p_ref[0, pair]
        d_mix = split_heads(d_ref[:, columns])
        queries = split_heads(q_ref[:, columns])
        eighth = jnp.asarray(0.125, bf16)
        d_attn = dot(d_mix, v_ref[:, columns], ((1,), (1,)))
        soft = attention.astype(f32)
        weighted = d_attn * soft
        inner = jnp.sum(weighted, axis=1, keepdims=True)
        d_scores = (weighted - soft * inner).astype(bf16)
        dv_ref[:, columns] = dot(attention, d_mix, ((0,), (0,))).astype(bf16)
        dk_ref[:, columns] = dot(d_scores, queries * eighth, ((0,), (0,))).astype(bf16)
        wide_k = jnp.concatenate([k_ref[:, columns] * eighth, hot_ref[...]], axis=1)
        both = dot(d_scores, wide_k)
        d_offsets = shift_lanes(both[:, LANES:], bits_ref, False)
        high = d_offsets.astype(bf16)
        low = (d_offsets - high.astype(f32)).astype(bf16)
        parts = jnp.concatenate([high, low], axis=1)
        rel = jnp.concatenate([rel_ref[...], rel_ref[...]], axis=0)
        dq_ref[:, columns] = merge_heads(both[:, :LANES] + dot(parts, rel)).astype(bf16)
        table_ref[...] += dot(parts, queries, ((0,), (0,)))


def attend_forward(q, k, v, fill, rel, hot, bits):
    rows, width = q.shape
    windows = rows // PAD
    pairs = width // LANES
    block = pl.BlockSpec((PAD, width), lambda i: (i, 0))
    whole = lambda a: pl.BlockSpec(a.shape, lambda i: (0,) * a.ndim)
    return pl.pallas_call(
        attend_forward_kernel,
        grid=(windows,),
        in_specs=[block, block, block, pl.BlockSpec((1, 1, PAD), lambda i: (i, 0, 0)), whole(rel), whole(hot), whole(bits)],
        out_specs=[block, pl.BlockSpec((1, pairs, 2 * PAD, PAD), lambda i: (i, 0, 0, 0))],
        out_shape=[
            jax.ShapeDtypeStruct((rows, width), bf16),
            jax.ShapeDtypeStruct((windows, pairs, 2 * PAD, PAD), bf16),
        ],
        compiler_params=pltpu.CompilerParams(vmem_limit_bytes=50 << 20),
    )(q, k, v, fill, rel, hot, bits)


def attend_backward(q, k, v, p, d_mixture, rel, hot, bits):
    rows, width = q.shape
    windows = rows // PAD
    pairs = width // LANES
    block = pl.BlockSpec((PAD, width), lambda i: (i, 0))
    whole = lambda a: pl.BlockSpec(a.shape, lambda i: (0,) * a.ndim)
    return pl.pallas_call(
        attend_backward_kernel,
        grid=(windows,),
        in_specs=[
            block,
            block,
            block,
            pl.BlockSpec((1, pairs, 2 * PAD, PAD), lambda i: (i, 0, 0, 0)),
            block,
            whole(rel),
            whole(hot),
            whole(bits),
        ],
        out_specs=[block, block, block, pl.BlockSpec((2 * LANES, LANES), lambda i: (0, 0))],
        out_shape=[jax.ShapeDtypeStruct((rows, width), bf16)] * 3
        + [jax.ShapeDtypeStruct((2 * LANES, LANES), f32)],
        compiler_params=pltpu.CompilerParams(vmem_limit_bytes=50 << 20),
    )(q, k, v, p, d_mixture, rel, hot, bits)


def normalize(values):
    centre = jnp.mean(values, axis=-1, keepdims=True)
    centred = values - centre
    scale = lax.rsqrt(jnp.mean(centred * centred, axis=-1, keepdims=True) + 1e-06)
    return centred * scale, scale


def normalize_back(gradient, normal, scale, gain):
    e = gradient * gain
    return scale * (
        e - jnp.mean(e, axis=-1, keepdims=True) - normal * jnp.mean(e * normal, axis=-1, keepdims=True)
    )


def gather_shards(weight, split):
    dp = lax.axis_size("dp")
    size = weight.shape[split] // dp
    piece = lax.dynamic_slice_in_dim(weight, lax.axis_index("dp") * size, size, split)
    pieces = lax.all_gather(piece, ("dp", "tp"), axis=0, tiled=False)
    pieces = pieces.reshape((dp, -1) + piece.shape)
    return jnp.moveaxis(pieces, 0, split + 1).reshape((-1,) + weight.shape)


def spread_sum(gradient, split):
    dp = lax.axis_size("dp")
    tp = gradient.shape[0]
    shape = gradient.shape[1:]
    cut = gradient.reshape((tp,) + shape[:split] + (dp, shape[split] // dp) + shape[split + 1 :])
    cut = jnp.moveaxis(cut, split + 1, 0).astype(bf16)
    mine = lax.psum_scatter(cut.reshape((dp * tp,) + cut.shape[2:]), ("dp", "tp"), scatter_dimension=0, tiled=True)
    return lax.all_gather(mine[0], "dp", axis=split, tiled=True).astype(f32)


def pad_windows(rows):
    windows = rows.shape[0] // SLOTS
    cut = rows.reshape((windows, SLOTS) + rows.shape[1:])
    return jnp.pad(cut, ((0, 0), (0, PAD - SLOTS), (0, 0))).reshape((windows * PAD,) + rows.shape[1:])


def cut_windows(rows):
    windows = rows.shape[0] // PAD
    return rows.reshape((windows, PAD) + rows.shape[1:])[:, :SLOTS].reshape((windows * SLOTS,) + rows.shape[1:])


def keep_slots(height, breadth, windows):
    first = lax.axis_index("tp") * windows
    window = (first + jnp.arange(windows, dtype=jnp.int32))[:, None]
    inside = jnp.arange(PAD, dtype=jnp.int32)[None, :]
    row_at = window // GRID * WIN + inside // WIN
    column_at = window % GRID * WIN + inside % WIN
    real = inside < SLOTS
    return (row_at < height) & (column_at < breadth) & real, real


def body(
    tokens,
    heights,
    widths,
    norm_gain,
    norm_bias,
    w_qkv,
    b_qv,
    rel_pos,
    w_proj,
    b_proj,
    w_fc1,
    b_fc1,
    w_fc2,
    b_fc2,
    cotangent,
):
    tp = lax.axis_size("tp")
    width = tokens.shape[1]
    windows = tokens.shape[0] // SLOTS
    heads_part = w_qkv.shape[2]

    full_qkv = gather_shards(w_qkv, 1).transpose(1, 2, 0, 3).reshape(3, width, width)
    full_proj = gather_shards(w_proj, 0).reshape(width, width)
    full_fc1 = gather_shards(w_fc1, 0).transpose(1, 0, 2).reshape(width, -1)
    full_fc2 = gather_shards(w_fc2, 0).reshape(-1, width)
    full_b_qv = lax.all_gather(b_qv, "tp", axis=1, tiled=True).astype(f32)
    full_b_fc1 = lax.all_gather(b_fc1, "tp", axis=0, tiled=True).astype(f32)

    keep, real = keep_slots(heights[0], widths[0], windows)
    fill = jnp.where(keep, 0.0, jnp.where(real, neg_fill, pad_fill)).astype(f32)[:, None, :]
    masking = keep.reshape(-1, 1).astype(f32)
    gains = norm_gain.astype(f32)
    shifts = norm_bias.astype(f32)
    bits, hot = window_constants()
    rel = position_matrix(rel_pos)

    inputs = pad_windows(tokens).astype(f32)
    d_output = pad_windows(cotangent).astype(f32)
    normal_one, scale_one = normalize(inputs)
    normed = (normal_one * gains[0] + shifts[0]).astype(bf16)
    queries = (dot(normed, full_qkv[0]) + full_b_qv[0]).astype(bf16)
    key_rows = dot(normed, full_qkv[1]).astype(bf16)
    values = (dot(normed, full_qkv[2]) + full_b_qv[1]).astype(bf16)
    mixture, attention = attend_forward(queries, key_rows, values, fill, rel, hot, bits)
    middle = inputs + masking * (dot(mixture, full_proj) + b_proj.astype(f32))
    normal_two, scale_two = normalize(middle)
    normed_two = (normal_two * gains[1] + shifts[1]).astype(bf16)
    before = dot(normed_two, full_fc1) + full_b_fc1
    phi = 0.5 * (1.0 + lax.erf(before * 0.7071067811865476))
    hidden = (before * phi).astype(bf16)
    slope = phi + before * (jnp.exp(-0.5 * before * before) * 0.3989422804014327)
    result = (middle + masking * (dot(hidden, full_fc2) + b_fc2.astype(f32))).astype(bf16)

    masked_out = masking * d_output
    grad_bias_two = jnp.sum(masked_out, axis=0)
    d_second = masked_out.astype(bf16)
    grad_second = dot(hidden, d_second, ((0,), (0,)))
    d_hidden = dot(d_second, full_fc2, ((1,), (1,)))
    d_before = (slope * d_hidden).astype(bf16)
    grad_bias_one = jnp.sum(d_before.astype(f32), axis=0)
    grad_first = dot(normed_two, d_before, ((0,), (0,)))
    d_normed_two = dot(d_before, full_fc1, ((1,), (1,)))
    d_middle = d_output + normalize_back(d_normed_two, normal_two, scale_two, gains[1])
    masked_mid = masking * d_middle
    grad_bias_proj = jnp.sum(masked_mid, axis=0)
    d_first = masked_mid.astype(bf16)
    grad_projection = dot(mixture, d_first, ((0,), (0,)))
    d_mixture = dot(d_first, full_proj, ((1,), (1,))).astype(bf16)
    d_queries, d_keys, d_values, table = attend_backward(
        queries, key_rows, values, attention, d_mixture, rel, hot, bits
    )
    grad_qkv = jnp.stack(
        [dot(normed, part, ((0,), (0,))) for part in (d_queries, d_keys, d_values)]
    )
    grad_qv_bias = jnp.stack(
        [jnp.sum(d_queries.astype(f32), axis=0), jnp.sum(d_values.astype(f32), axis=0)]
    )
    d_normed = (
        dot(d_queries, full_qkv[0], ((1,), (1,)))
        + dot(d_keys, full_qkv[1], ((1,), (1,)))
        + dot(d_values, full_qkv[2], ((1,), (1,)))
    )
    grad_inputs = d_middle + normalize_back(d_normed, normal_one, scale_one, gains[0])

    offsets = 2 * WIN - 1
    table = table[:LANES] + table[LANES:]
    table = table[:, :HALF] + table[:, HALF:]
    grad_table = jnp.stack([table[:offsets], table[HALF : HALF + offsets]])[:, ::-1, :]

    small = lax.psum(
        (
            jnp.stack([jnp.sum(d_normed * normal_one, axis=0), jnp.sum(d_normed_two * normal_two, axis=0)]),
            jnp.stack([jnp.sum(d_normed, axis=0), jnp.sum(d_normed_two, axis=0)]),
            grad_table,
            grad_bias_proj,
            grad_bias_two,
            grad_qv_bias,
            grad_bias_one,
        ),
        ("dp", "tp"),
    )
    me = lax.axis_index("tp")
    grad_qkv = spread_sum(grad_qkv.reshape(3, width, tp, heads_part).transpose(2, 0, 1, 3), 1)
    grad_projection = spread_sum(grad_projection.reshape(tp, heads_part, width), 0)
    grad_first = spread_sum(grad_first.reshape(width, tp, -1).transpose(1, 0, 2), 0)
    grad_second = spread_sum(grad_second.reshape(tp, -1, width), 0)
    return (
        cut_windows(result),
        cut_windows(grad_inputs),
        small[0],
        small[1],
        grad_qkv,
        lax.dynamic_slice_in_dim(small[5], me * heads_part, heads_part, 1),
        small[2],
        grad_projection,
        small[3],
        grad_first,
        lax.dynamic_slice_in_dim(small[6], me * w_fc1.shape[1], w_fc1.shape[1], 0),
        grad_second,
        small[4],
    )


def solution(mesh):
    rows = P(("dp", "tp"), None)
    return jax.shard_map(
        body,
        mesh=mesh,
        in_specs=(
            rows,
            P("dp"),
            P("dp"),
            P(),
            P(),
            P(None, None, "tp"),
            P(None, "tp"),
            P(),
            P("tp", None),
            P(),
            P(None, "tp"),
            P("tp"),
            P("tp", None),
            P(),
            rows,
        ),
        out_specs=(
            rows,
            rows,
            P(),
            P(),
            P(None, None, "tp"),
            P(None, "tp"),
            P(),
            P("tp", None),
            P(),
            P(None, "tp"),
            P("tp"),
            P("tp", None),
            P(),
        ),
        check_vma=False,
    )
```

time: 1630 us -> 773 us (0.47)
  local copies, waits for them, and re-layouts: 561 us -> 110 us
  waiting for transfers between devices: 699 us -> 353 us
  matrix products: 188 us -> 84.7 us
  other arithmetic: 98.3 us -> 23.5 us
  Pallas kernels: 0 us -> 69 us
  blocking collectives: 58.3 us -> 91.5 us
    add x54 -> x0, local copies, waits for them, and re-layouts: 384 us -> none  [the longest x48 377 us: window_scores(): direct.reshape(leading + (WIN, WIN, WIN, WIN)) + along_h[..., :, None]]
    all_gather x4 -> x6, waiting for transfers between devices: 355 us -> 132 us  [the longest x4 101 us: gather_shards(): pieces = lax.all_gather(piece, ('dp', 'tp'), axis=0, tiled=False)]
    dot_general x73 -> x18, matrix products: 183 us -> 84.7 us  [dot(): return lax.dot_general(a, b, (dims, ((), ())), preferred_element_type=f32)]
    pallas_call x0 -> x2, Pallas kernels: none -> 69 us  [the longest x1 39.3 us: attend_forward(): pl.pallas_call(attend_forward_kernel, grid=(windows,), in_specs=[block, b...]
    psum x1 -> x0, waiting for transfers between devices: 68.4 us -> none  [body(): lax.psum((weight_grads[0], weight_grads[1], weight_grads[2], weight_grads...]
    reduce_sum x19 -> x6, other arithmetic: 61.3 us -> 4.29 us  [the longest x1 1.57 us: body(): jnp.sum(d_values.astype(f32), axis=0)]
    reshape x19 -> x6, local copies, waits for them, and re-layouts: 76.7 us -> 21.9 us  [the longest x1 8.23 us: gather_shards(): return jnp.moveaxis(pieces, 0, split + 1).reshape((-1,) + weight.shape)]
    reduce_scatter x4, waiting for transfers between devices: 275 us -> 221 us  [spread_sum(): lax.psum_scatter(cut.reshape((dp * tp,) + cut.shape[2:]), ('dp', 'tp'), s...]
  transfers between devices with their start and end apart: 9 -> 10, of which waited for: 9 -> 8; matrix products, arithmetic and copies ran while one was open for 4% -> 27% of each run, Pallas kernels for 0% -> 9%
where the time goes in v1:
time: 773 us; the launch traced here: 761 us
  waiting for transfers between devices  353 us (46%)
  local copies, waits for them, and re-layouts  110 us (14%)
  blocking collectives  91.5 us (12%)
  matrix products  84.7 us (11%)
  Pallas kernels  69 us (9%)
  other arithmetic  23.5 us (3%)
  between operations  16.6 us (2%)
  starting transfers between devices  12.9 us (2%)
    reduce_scatter x4, waiting for transfers between devices, spread_sum(): lax.psum_scatter(cut.reshape((dp * tp,) + cut.shape[2:]), ('dp', 'tp'), s...  221 us
    all_gather x4, waiting for transfers between devices, gather_shards(): pieces = lax.all_gather(piece, ('dp', 'tp'), axis=0, tiled=False)  101 us
    dot_general x18, matrix products, dot(): return lax.dot_general(a, b, (dims, ((), ())), preferred_element_type=f32)  84.7 us
    psum x1, blocking collectives, body(): lax.psum((jnp.stack([jnp.sum(d_normed * normal_one, axis=0), jnp.sum(d_no...  41.8 us
    pallas_call x1, Pallas kernels, attend_forward(): pl.pallas_call(attend_forward_kernel, grid=(windows,), in_specs=[block, b...  39.3 us
    convert_element_type x6, local copies, waits for them, and re-layouts, spread_sum(): cut = jnp.moveaxis(cut, split + 1, 0).astype(bf16)  35.4 us
    all_gather x2, waiting for transfers between devices, spread_sum(): return lax.all_gather(mine[0], 'dp', axis=split, tiled=True).astype(f32)  30.3 us
    pallas_call x1, Pallas kernels, attend_backward(): pl.pallas_call(attend_backward_kernel, grid=(windows,), in_specs=[block,...  29.8 us
  transfers between devices with their start and end apart: 10, of which 8 were waited for; matrix products, arithmetic and copies ran while one was open for 27% of the time, Pallas kernels for 9%

profile of v1, /device:TPU:0, one launch (start us, length us, event | category | flops | bytes accessed | tf_op | source)
XLA Modules:
  0.0 761.1 jit_solution(7755647720576757417)
XLA Ops:
  15.4 12.8 %all-gather.8 = bf16[4,192,2]{1,2,0:T(2,128)(2,1)S(1)} all-gather(bf16[1,192,2]{1,2,0:T(2,128)(2,1)} %bitcast.199), channel_id=1, replica_groups=mesh['dp'=8,'tp'=4] {'tp'}, dimensions={0}, use_global_device_ids=true | all-gather | bytes 3840 | tf_op jit(solution)/shard_map/all_gather | solution.py:249
  30.3 13.0 %all-gather.9 = bf16[4,1,768]{2,1,0:T(2,128)(2,1)S(1)} all-gather(bf16[1,1,768]{2,1,0:T(2,128)(2,1)S(1)} %reshape.1059), channel_id=1, replica_groups=mesh['dp'=8,'tp'=4] {'tp'}, dimensions={0}, use_global_device_ids=true | all-gather | bytes 7680 | tf_op jit(solution)/shard_map/all_gather | solution.py:250
  52.7 15.6 %all-gather.19.cloned.1.call-done = bf16[768,768]{1,0:T(8,128)(2,1)} async-done(((bf16[24,768]{1,0:T(8,128)(2,1)}), bf16[768,768]{1,0:T(8,128)(2,1)}) %all-gather.19.cloned.1.call-update) | async-done | bytes 1179664 | tf_op jit(solution)/shard_map/all_gather | solution.py:187
  68.2 2.4 copy.107
  70.6 63.5 %all-gather.17.cloned.1.call-done = bf16[96,96,192]{2,1,0:T(8,128)(2,1)} async-done(((bf16[3,96,192]{2,1,0:T(8,128)(2,1)}), bf16[96,96,192]{2,1,0:T(8,128)(2,1)}) %all-gather.17.cloned.1.call-update) | async-done | bytes 3538960 | tf_op jit(solution)/shard_map/all_gather | solution.py:187
  134.1 7.1 copy.104
  141.2 8.2 %reshape.1022 = bf16[4,3,768,192]{2,3,1,0:T(8,128)(2,1)} reshape(bf16[4,3,8,96,192]{3,2,4,1,0:T(8,128)(2,1)} %bitcast.158) | data formatting | bytes 7077888 | tf_op jit(solution)/shard_map/reshape | solution.py:189
  151.7 2.2 convolution_convert_fusion.2.k_ref
  153.9 2.2 add_convert_fusion.2.v_ref
  156.2 2.5 add_convert_fusion.3.q_ref
  158.7 39.3 %shard_map.246 = (bf16[832,768]{1,0:T(8,128)(2,1)S(1)}, bf16[4,6,416,208]{3,2,1,0:T(8,128)(2,1)}) custom-call(bf16[832,768]{1,0:T(8,128)(2,1)S(1)} %add_convert_fusion.3.q_ref, bf16[832,768]{1,0:T(8,128)(2,1)} %convolution_convert_fusion.2.k_ref, bf16[832,768]{1,0:T(8,128)(2,1)} %add_convert_fusion.2.v_ref, f32[4,1,208]{2,1,0:T(1,128)S(1)} %and_select_fusion.fill_ref, ...), custom_call_target="tpu_custom_call" | custom-call | tf_op jit(solution)/shard_map/pallas_call | solution.py:130
  201.2 4.8 copy.108
  206.1 6.6 copy.109
  212.7 10.7 %fusion.9 = (bf16[3072,832]{0,1:T(8,128)(2,1)}, f32[832,3072]{1,0:T(8,128)}) fusion(f32[3072]{0:T(1024)S(1)} %bitcast.196, bf16[768,3072]{0,1:T(8,128)(2,1)} %bitcast.171, f32[832,768]{1,0:T(8,128)} %copy-done.11, f32[768]{0:T(1024)S(1)} %get-tuple-element.113, f32[768]{0:T(1024)S(1)} %get-tuple-element.146, f32[832]{0:T(1024)S(1)} %add_rsqrt_fusion, ...), kind=kOutput, calls=%fused_computation.15 | convolution fusion | flops 3944398848 | bytes 22635008 | tf_op jit(solution)/shard_map/dot_general | solution.py:23
  223.4 8.0 %copy.118 = bf16[3072,832]{1,0:T(8,128)(2,1)} copy(bf16[3072,832]{0,1:T(8,128)(2,1)} %get-tuple-element.143) | data formatting | bytes 10223616 | tf_op jit(solution)/shard_map/convert_element_type | solution.py:273
  231.5 8.0 %convert_bitcast_fusion = bf16[8,4,96,768]{3,2,0,1:T(8,128)(2,1)S(1)} fusion(bf16[4,8,96,832]{3,2,1,0:T(8,128)(2,1)} %bitcast.163, bf16[832,768,1,1]{1,0,3,2:T(8,128)(2,1)S(1)} %bitcast.183), kind=kOutput, calls=%fused_computation.19 | convolution fusion | flops 3928227840 | bytes 11108352 | tf_op jit(solution)/shard_map/dot_general | solution.py:23
  239.5 2.5 copy.119
  242.1 22.3 %all-gather.23.cloned.1.call-done = bf16[3072,768]{1,0:T(8,128)(2,1)} async-done(((bf16[96,768]{1,0:T(8,128)(2,1)}), bf16[3072,768]{1,0:T(8,128)(2,1)}) %all-gather.23.cloned.1.call-update) | async-done | bytes 4718608 | tf_op jit(solution)/shard_map/all_gather | solution.py:187
  264.4 2.7 copy.110
  267.1 11.5 %convert_reduce_fusion = (f32[3072]{0:T(1024)S(1)}, bf16[832,3072]{1,0:T(8,128)(2,1)S(1)}) fusion(bf16[832,768]{1,0:T(8,128)(2,1)S(1)} %bitcast.184, bf16[3072,768]{1,0:T(8,128)(2,1)S(1)} %bitcast.169, f32[832,3072]{1,0:T(8,128)} %get-tuple-element.144, f32[3072]{0:T(1024)S(1)} %bitcast.197), kind=kOutput, calls=%fused_computation.12 | convolution fusion | flops 3959092224 | bytes 21356544 | tf_op jit(solution)/shard_map/dot_general | solution.py:23
  278.6 2.3 copy-done.30
  280.9 7.7 %convolution_convert_fusion = bf16[768,3072]{1,0:T(8,128)(2,1)} fusion(bf16[832,3072]{1,0:T(8,128)(2,1)S(1)} %get-tuple-element.142, f32[832,768]{1,0:T(8,128)S(1)} %copy-done.12, f32[768]{0:T(1024)S(1)} %get-tuple-element.113, f32[768]{0:T(1024)S(1)} %get-tuple-element.146, f32[832]{0:T(1024)S(1)} %add_rsqrt_fusion, f32[832]{0:T(1024)S(1)} %broadcast_multiply_fusion.4), kind=kOutput, calls=%fused_computation.18 | convolution fusion | flops 3931422720 | bytes 12399104 | tf_op jit(solution)/shard_map/dot_general | solution.py:23
  288.6 9.8 %convert_element_type.214 = bf16[768,4,768]{2,1,0:T(4,128)(2,1)} reshape(bf16[768,3072]{1,0:T(8,128)(2,1)} %convolution_convert_fusion) | data formatting | bytes 9437184 | tf_op jit(solution)/shard_map/convert_element_type | solution.py:197
  298.5 5.6 copy.117
  304.1 12.5 %reduce-scatter.7.cloned.1.call-start = ((), (), s32[]{:S(2)}) async-start(), calls=%async_computation.5 | async-start | bytes 1216512 | tf_op jit(solution)/shard_map/reduce_scatter | solution.py:198
  316.6 10.0 %multiply_reduce_fusion = (f32[768]{0:T(1024)S(1)}, f32[832]{0:T(1024)S(1)}, f32[832]{0:T(1024)S(1)}, f32[768]{0:T(1024)S(1)}, f32[832,768]{1,0:T(8,128)S(1)}) fusion(f32[832,768]{1,0:T(8,128)} %copy-done.11, f32[832]{0:T(1024)S(1)} %add_rsqrt_fusion, f32[832]{0:T(1024)S(1)} %broadcast_multiply_fusion.4, f32[768]{0:T(1024)S(1)} %get-tuple-element.146, ...), kind=kOutput, calls=%fused_computation.24 | convolution fusion | flops 3931616256 | bytes 14964736 | tf_op jit(solution)/shard_map/dot_general | solution.py:23
  331.3 4.0 convolution_convert_fusion.1.d_ref
  335.3 29.8 %shard_map.247 = (bf16[832,768]{1,0:T(8,128)(2,1)S(1)}, bf16[832,768]{1,0:T(8,128)(2,1)S(1)}, bf16[832,768]{1,0:T(8,128)(2,1)}, f32[256,128]{1,0:T(8,128)S(1)}) custom-call(bf16[832,768]{1,0:T(8,128)(2,1)} %copy-done.2, bf16[832,768]{1,0:T(8,128)(2,1)} %convolution_convert_fusion.2.k_ref, bf16[832,768]{1,0:T(8,128)(2,1)} %add_convert_fusion.2.v_ref, ...), custom_call_target="tpu_custom_call" | custom-call | tf_op jit(solution)/shard_map/pallas_call | solution.py:149
  365.1 2.5 copy.113
  370.7 3.3 fusion.14
  379.0 9.1 %convert_element_type.204 = bf16[4,3,8,96,192]{3,2,4,0,1:T(8,128)(2,1)} reshape(bf16[4,3,768,192]{2,3,0,1:T(8,128)(2,1)} %maximum_bitcast_fusion) | data formatting | bytes 7077888 | tf_op jit(solution)/shard_map/convert_element_type | solution.py:197
  388.1 7.3 copy.114
  396.1 9.8 %add_convert_fusion = bf16[832,768]{1,0:T(8,128)(2,1)S(1)} fusion(f32[832,768]{1,0:T(8,128)} %copy-done.11, bf16[3072,768]{1,0:T(8,128)(2,1)} %bitcast.170, f32[832,3072]{1,0:T(8,128)} %get-tuple-element.144, f32[3072]{0:T(1024)S(1)} %bitcast.198, f32[768]{0:T(1024)S(1)} %convert_element_type.192, f32[832]{0:T(1024)S(1)} %reshape.1039), kind=kOutput, calls=%fused_computation.31 | convolution fusion | flops 3943759872 | bytes 18794752 | tf_op jit(solution)/shard_map/dot_general | solution.py:23
  407.0 2.2 reshape.1030
  411.3 2.5 fusion.30
  416.4 3.2 multiply_reduce_fusion.1
  419.6 68.2 %reduce-scatter.9.cloned.1.call-done = bf16[1,96,768]{2,1,0:T(8,128)(2,1)} async-done(((bf16[32,96,768]{2,1,0:T(8,128)(2,1)}), bf16[1,96,768]{2,1,0:T(8,128)(2,1)}) %reduce-scatter.9.cloned.1.call-update) | async-done | bytes 147472 | tf_op jit(solution)/shard_map/reduce_scatter | solution.py:198
  487.9 3.0 multiply_add_fusion
  492.7 41.8 %all-reduce.3 = (f32[2,768]{1,0:T(2,128)}, f32[2,768]{1,0:T(2,128)}, f32[2,768]{1,0:T(2,128)S(1)}, f32[2,27,64]{2,1,0:T(8,128)S(1)}, f32[768]{0:T(1024)}, /*index=5*/f32[3072]{0:T(1024)S(1)}, f32[768]{0:T(1024)}) all-reduce(f32[2,768]{1,0:T(2,128)S(1)} %pad_maximum_fusion.2, ...), channel_id=1, replica_groups=mesh['dp'=8,'tp'=4] {'dp','tp'}, use_global_device_ids=true, to_apply=%region_10.11 | all-reduce | flops 12672 | bytes 101376 | tf_op jit(solution)/shard_map/psum | solution.py:313
  536.5 51.7 %reduce-scatter.7.cloned.1.call-done = bf16[1,24,768]{2,1,0:T(8,128)(2,1)} async-done(((bf16[32,24,768]{2,1,0:T(8,128)(2,1)}), bf16[1,24,768]{2,1,0:T(8,128)(2,1)}) %reduce-scatter.7.cloned.1.call-update) | async-done | bytes 36880 | tf_op jit(solution)/shard_map/reduce_scatter | solution.py:198
  588.2 9.5 %all-gather.5 = bf16[1,192,768]{2,1,0:T(8,128)(2,1)S(1)} all-gather(bf16[1,24,768]{2,1,0:T(8,128)(2,1)} %reduce-scatter.7.cloned.1.call-done), channel_id=7, replica_groups=mesh['dp'=8,'tp'=4] {'dp'}, dimensions={1}, use_global_device_ids=true | all-gather | bytes 331776 | tf_op jit(solution)/shard_map/all_gather | solution.py:199
  598.6 101.2 %reduce-scatter.5.cloned.1.call-done = bf16[1,3,96,192]{3,2,1,0:T(8,128)(2,1)} async-done(((bf16[32,3,96,192]{3,2,1,0:T(8,128)(2,1)}), bf16[1,3,96,192]{3,2,1,0:T(8,128)(2,1)}) %reduce-scatter.5.cloned.1.call-update) | async-done | bytes 110608 | tf_op jit(solution)/shard_map/reduce_scatter | solution.py:198
  700.8 14.3 %all-gather.4 = bf16[1,3,768,192]{3,1,0,2:T(4,128)(2,1)S(1)} all-gather(bf16[1,3,96,192]{3,1,0,2:T(4,128)(2,1)S(1)} %copy.115), channel_id=6, replica_groups=mesh['dp'=8,'tp'=4] {'dp'}, dimensions={2}, use_global_device_ids=true | all-gather | bytes 995328 | tf_op jit(solution)/shard_map/all_gather | solution.py:199
  715.5 2.3 copy.120
  717.8 7.2 all-gather.27.cloned.1.call-done
  725.1 2.9 bitcast_convert_fusion.1
  728.0 23.0 %all-gather.25.cloned.1.call-done = bf16[1,768,768]{2,1,0:T(8,128)(2,1)} async-done(((bf16[1,96,768]{2,1,0:T(8,128)(2,1)}), bf16[1,768,768]{2,1,0:T(8,128)(2,1)}) %all-gather.25.cloned.1.call-update) | async-done | bytes 1179664 | tf_op jit(solution)/shard_map/all_gather | solution.py:199
  751.1 2.8 bitcast_convert_fusion.2
  (167 shorter events, 48.6 us)
Async XLA Ops:
  7.2 3.6 copy-start
  7.2 61.0 %all-gather.19.cloned.1.call-start = ((), (), s32[]{:S(2)}) async-start(), calls=%async_computation.9 | async-start | bytes 1216512 | tf_op jit(solution)/shard_map/all_gather | solution.py:187
  8.7 125.4 %all-gather.17.cloned.1.call-start = ((), (), s32[]{:S(2)}) async-start(), calls=%async_computation.8 | async-start | bytes 4866048 | tf_op jit(solution)/shard_map/all_gather | solution.py:187
  10.7 190.5 %all-gather.21.cloned.1.call-start = ((), (), s32[]{:S(2)}) async-start(), calls=%async_computation.10 | async-start | bytes 4866048 | tf_op jit(solution)/shard_map/all_gather | solution.py:187
  11.5 252.9 %all-gather.23.cloned.1.call-start = ((), (), s32[]{:S(2)}) async-start(), calls=%async_computation.11 | async-start | bytes 4866048 | tf_op jit(solution)/shard_map/all_gather | solution.py:187
  13.1 396.5 %reduce-scatter.11.cloned.1.call-start = ((), (), s32[]{:S(2)}) async-start(), calls=%async_computation.7 | async-start | bytes 4866048 | tf_op jit(solution)/shard_map/reduce_scatter | solution.py:198
  46.9 3.2 copy-start.9
  52.6 101.3 %copy-start.20 = (bf16[4,208,768]{2,1,0:T(8,128)(2,1)}, bf16[4,208,768]{2,1,0:T(8,128)(2,1)S(1)}, u32[]{:S(2)}) copy-start(bf16[4,208,768]{2,1,0:T(8,128)(2,1)S(1)} %add_convert_fusion.4) | copy-start | bytes 3833860
  151.6 2.3 copy-start.25
  151.7 2.3 copy-start.15
  151.7 4.5 copy-start.23
  158.7 40.6 %copy-start.2 = (bf16[832,768]{1,0:T(8,128)(2,1)}, bf16[832,768]{1,0:T(8,128)(2,1)S(1)}, u32[]{:S(2)}) copy-start(bf16[832,768]{1,0:T(8,128)(2,1)S(1)} %add_convert_fusion.3.q_ref) | copy-start | bytes 3833860
  158.7 39.3 %copy-start.5 = (f32[4,208,768]{2,1,0:T(8,128)S(1)}, f32[4,208,768]{2,1,0:T(8,128)}, u32[]{:S(2)}) copy-start(f32[4,208,768]{2,1,0:T(8,128)} %pad_convert_fusion) | copy-start | bytes 7667716
  158.7 39.3 %copy-start.26 = (bf16[4,8,24,768]{3,2,1,0:T(8,128)(2,1)S(1)}, bf16[4,8,24,768]{3,2,1,0:T(8,128)(2,1)}, u32[]{:S(2)}) copy-start(bf16[4,8,24,768]{3,2,1,0:T(8,128)(2,1)} %copy.107) | copy-start | bytes 3538948
  198.0 1.4 copy-start.3
  199.3 1.4 copy-start.11
  223.4 8.1 %copy-start.22 = (bf16[4,208,768]{2,1,0:T(8,128)(2,1)S(1)}, bf16[4,208,768]{2,1,0:T(8,128)(2,1)}, u32[]{:S(2)}) copy-start(bf16[4,208,768]{2,1,0:T(8,128)(2,1)} %get-tuple-element.130) | copy-start | bytes 3833860
  242.0 245.9 %reduce-scatter.9.cloned.1.call-start = ((), (), s32[]{:S(2)}) async-start(), calls=%async_computation.6 | async-start | bytes 4866048 | tf_op jit(solution)/shard_map/reduce_scatter | solution.py:198
  267.1 11.5 %copy-start.17 = (bf16[4,8,96,768]{3,2,1,0:T(8,128)(2,1)}, bf16[4,8,96,768]{3,2,1,0:T(8,128)(2,1)S(1)}, u32[]{:S(2)}) copy-start(bf16[4,8,96,768]{3,2,1,0:T(8,128)(2,1)S(1)} %copy.110) | copy-start | bytes 14155780
  267.1 13.8 %copy-start.12 = (f32[832,768]{1,0:T(8,128)S(1)}, f32[832,768]{1,0:T(8,128)}, u32[]{:S(2)}) copy-start(f32[832,768]{1,0:T(8,128)} %copy-done.11) | copy-start | bytes 7667716
  278.6 2.3 copy-start.30
  304.1 22.5 %copy-start.10 = (bf16[4,196,768]{2,1,0:T(8,128)(2,1)S(1)}, bf16[4,196,768]{2,1,0:T(8,128)(2,1)}, u32[]{:S(2)}) copy-start(bf16[4,196,768]{2,1,0:T(8,128)(2,1)} %copy-done.9) | copy-start | bytes 3612676
  304.1 284.1 %reduce-scatter.7.cloned.1.call-start = ((), (), s32[]{:S(2)}) async-start(), calls=%async_computation.5 | async-start | bytes 1216512 | tf_op jit(solution)/shard_map/reduce_scatter | solution.py:198
  316.6 10.0 %copy-start.13 = (f32[832,768]{1,0:T(8,128)S(1)}, f32[832,768]{1,0:T(8,128)}, u32[]{:S(2)}) copy-start(f32[832,768]{1,0:T(8,128)} %copy-done.11) | copy-start | bytes 7667716
  326.6 1.3 copy-start.4
  327.9 1.6 copy-start.14
  329.6 1.7 copy-start.27
  330.7 369.1 %reduce-scatter.5.cloned.1.call-start = ((), (), s32[]{:S(2)}) async-start(), calls=%async_computation.4 | async-start | bytes 4866048 | tf_op jit(solution)/shard_map/reduce_scatter | solution.py:198
  370.7 3.3 copy-start.19
  370.7 3.3 copy-start.21
  374.0 1.4 copy-start.18
  395.4 0.7 copy-start.29
  395.4 329.7 %all-gather.27.cloned.1.call-start = ((), (), s32[]{:S(2)}) async-start(), calls=%async_computation.13 | async-start | bytes 1327104 | tf_op jit(solution)/shard_map/all_gather | solution.py:199
  409.7 341.4 %all-gather.25.cloned.1.call-start = ((), (), s32[]{:S(2)}) async-start(), calls=%async_computation.12 | async-start | bytes 1327104 | tf_op jit(solution)/shard_map/all_gather | solution.py:199
  411.3 2.6 copy-start.24
  413.9 1.8 copy-start.6
  413.9 2.2 copy-start.8
  413.9 2.5 copy-start.16
  416.4 71.5 %copy-start.7 = (f32[4,208,768]{2,1,0:T(8,128)S(1)}, f32[4,208,768]{2,1,0:T(8,128)}, u32[]{:S(2)}) copy-start(f32[4,208,768]{2,1,0:T(8,128)} %pad_convert_fusion) | copy-start | bytes 7667716
  491.1 1.6 copy-start.28
  725.1 28.8 %copy-start.1 = (bf16[768,768]{1,0:T(8,128)(2,1)S(1)}, bf16[768,768]{1,0:T(8,128)(2,1)}, u32[]{:S(2)}) copy-start(bf16[768,768]{1,0:T(8,128)(2,1)} %param.25) | copy-start | bytes 3538948
Sparse Core Ops, SparseCore 0:
  11.4 56.7 all-gather.18
  71.6 62.4 all-gather.16
  136.9 62.3 all-gather.20
  202.0 62.3 all-gather.22
  269.7 105.7 reduce-scatter.10
  381.8 106.0 reduce-scatter.8
  493.0 95.1 reduce-scatter.6
  593.7 106.0 reduce-scatter.4
  701.9 23.1 all-gather.26
  727.0 24.0 all-gather.24

commit v2 on v1

v2 whole, which is shorter than its diff:
```python
import jax
import jax.numpy as jnp
from jax import lax
from jax.experimental import pallas as pl
from jax.experimental.pallas import tpu as pltpu
from jax.sharding import PartitionSpec as P

HEAD_DIM = 64
WIN = 14
GRID = 4
SLOTS = WIN * WIN
PAD = 208
LANES = 128
HALF = 64
CHUNK = 64
TILE = 256

bf16 = jnp.bfloat16
f32 = jnp.float32
neg_fill = -30000.0
pad_fill = -1e30
root_half = 0.7071067811865476
bell = 0.3989422804014327
VMEM_LIMIT = 64 << 20
MESH = pl.DeviceIdType.MESH


def dot(a, b, dims=((1,), (0,))):
    return lax.dot_general(a, b, (dims, ((), ())), preferred_element_type=f32)


NT = ((1,), (1,))
TN = ((0,), (0,))


def window_constants():
    slot = jnp.arange(PAD, dtype=jnp.int32)[:, None]
    lane = jnp.arange(HALF, dtype=jnp.int32)[None, :]
    place = jnp.where(lane % 32 < 16, slot // WIN, slot % WIN)
    hot = ((slot < SLOTS) & (lane % 16 == place)).astype(bf16)
    zero = jnp.zeros_like(hot)
    return jnp.concatenate([jnp.concatenate([hot, zero], 1), jnp.concatenate([zero, hot], 1)], 0), hot[:, :32].T


def position_matrices(rel_pos):
    flipped = rel_pos[:, ::-1, :]
    rows = jnp.pad(flipped, ((0, 0), (0, 32 - flipped.shape[1]), (0, 0))).reshape(HALF, HEAD_DIM)
    zero = jnp.zeros_like(rows)
    both = jnp.concatenate([jnp.concatenate([rows, zero], 1), jnp.concatenate([zero, rows], 1)], 0)
    return both * jnp.asarray(8.0, bf16), both.T


def stack_heads(pair, heads):
    if heads == 1:
        return pair
    lane = lax.broadcasted_iota(jnp.int32, pair.shape, 1)
    zero = jnp.zeros_like(pair)
    return jnp.concatenate([jnp.where(lane < HALF, pair, zero), jnp.where(lane < HALF, zero, pair)], axis=0)


def merge_heads(stacked, heads):
    if heads == 1:
        return stacked
    top, bottom = stacked[:PAD], stacked[PAD:]
    lane = lax.broadcasted_iota(jnp.int32, top.shape, 1)
    return jnp.where(lane < HALF, top, bottom)


def place_of_lane():
    lane = lax.broadcasted_iota(jnp.int32, (1, PAD), 1)
    row = lax.div(lane, WIN)
    return row, lane - row * WIN


def attend_forward_unit(q_ref, k_ref, v_ref, mix_ref, p_ref, fill_ref, rel_ref, hot_ref, scr_ref, blocks):
    places = place_of_lane()
    eighth = jnp.asarray(0.125, bf16)
    firsts, scores, biases = [], [], []
    count = 0
    for window, start, heads in blocks:
        firsts.append(count)
        lanes, rows = slice(start, start + LANES), slice(window * PAD, (window + 1) * PAD)
        left = jnp.concatenate([rel_ref[: heads * HALF], stack_heads(k_ref[rows, lanes], heads)], axis=0)
        both = dot(left, q_ref[rows, lanes] * eighth, NT)
        for head in range(heads):
            scr_ref[count + head] = both[head * HALF : (head + 1) * HALF]
        scores.append(both[heads * HALF :])
        count += heads
    for b, (window, start, heads) in enumerate(blocks):
        parts = []
        for head in range(heads):
            along = []
            for base, place in ((0, places[0]), (32, places[1])):
                picked = scr_ref[firsts[b] + head, base : base + 16, :]
                for at in range(WIN - 1):
                    first = base + WIN - 1 - at
                    picked = jnp.where(place == at, scr_ref[firsts[b] + head, first : first + 16, :], picked)
                along.append(picked)
            bias = jnp.concatenate(along, axis=0)
            high = bias.astype(bf16)
            parts += [high, (bias - high.astype(f32)).astype(bf16)]
        biases.append(jnp.concatenate(parts, axis=0))
    for b, (window, start, heads) in enumerate(blocks):
        scores[b] = scores[b] + dot(hot_ref[: heads * PAD, : heads * HALF], biases[b])
    for b, (window, start, heads) in enumerate(blocks):
        fill = fill_ref[window * PAD : (window + 1) * PAD]
        fill = jnp.concatenate([fill, fill[:, : PAD - LANES]], axis=1)
        for head in range(heads):
            one = scores[b][head * PAD : (head + 1) * PAD]
            one = jnp.where(fill == 0.0, one, fill)
            weights = jnp.exp(one - jnp.max(one, axis=0, keepdims=True))
            total = jnp.sum(weights, axis=0, keepdims=True)
            p_ref[firsts[b] + head] = (weights * (1.0 / total)).astype(bf16)
    for b, (window, start, heads) in enumerate(blocks):
        lanes, rows = slice(start, start + LANES), slice(window * PAD, (window + 1) * PAD)
        turned = v_ref[rows, lanes].T
        parts = [
            dot(turned[head * HALF : (head + 1) * HALF], p_ref[firsts[b] + head]).astype(bf16) for head in range(heads)
        ]
        if heads == 1:
            parts.append(jnp.zeros_like(parts[0]))
        mix_ref[rows, lanes] = jnp.concatenate(parts, axis=0).T


def attend_backward_unit(
    q_ref, k_ref, v_ref, d_ref, p_ref, dq_ref, dk_ref, dv_ref, table_ref, relt_ref, hott_ref, scr_ref, blocks
):
    places = place_of_lane()
    eighth = jnp.asarray(0.125, bf16)
    firsts, d_attn, d_scores, sums, offsets = [], [], [], [], []
    count = 0
    for window, start, heads in blocks:
        firsts.append(count)
        lanes, rows = slice(start, start + LANES), slice(window * PAD, (window + 1) * PAD)
        d_attn.append(dot(stack_heads(v_ref[rows, lanes], heads), d_ref[rows, lanes], NT))
        count += heads
    for b, (window, start, heads) in enumerate(blocks):
        lanes, rows = slice(start, start + LANES), slice(window * PAD, (window + 1) * PAD)
        soft = p_ref[firsts[b] : firsts[b] + heads].reshape(heads * PAD, PAD)
        dv_ref[rows, lanes] = merge_heads(dot(soft, d_ref[rows, lanes]), heads).astype(bf16)
    for b, (window, start, heads) in enumerate(blocks):
        parts = []
        for head in range(heads):
            soft = p_ref[firsts[b] + head].astype(f32)
            weighted = d_attn[b][head * PAD : (head + 1) * PAD] * soft
            inner = jnp.sum(weighted, axis=0, keepdims=True)
            parts.append((weighted - soft * inner).astype(bf16))
        d_scores.append(parts)
    for b, (window, start, heads) in enumerate(blocks):
        lanes, rows = slice(start, start + LANES), slice(window * PAD, (window + 1) * PAD)
        turned_k = k_ref[rows, lanes].T * eighth
        parts = []
        for head in range(heads):
            left = jnp.concatenate([turned_k[head * HALF : (head + 1) * HALF], hott_ref[...]], axis=0)
            both = dot(left, d_scores[b][head])
            for axis in range(2):
                scr_ref[firsts[b] + head, axis, 16:32, :] = both[HALF + 16 * axis : HALF + 16 * axis + 16]
            parts.append(both[:HALF])
        sums.append(parts)
    for b, (window, start, heads) in enumerate(blocks):
        spread = []
        for head in range(heads):
            for axis in range(2):
                picked = scr_ref[firsts[b] + head, axis, 16:48, :]
                for at in range(WIN - 1):
                    picked = jnp.where(places[axis] == at, scr_ref[firsts[b] + head, axis, 3 + at : 35 + at, :], picked)
                spread.append(picked)
        offsets.append(jnp.concatenate(spread, axis=0).astype(bf16))
    for b, (window, start, heads) in enumerate(blocks):
        lanes, rows = slice(start, start + LANES), slice(window * PAD, (window + 1) * PAD)
        right = dot(jnp.concatenate(d_scores[b] + [offsets[b]], axis=0), q_ref[rows, lanes])
        dk_ref[rows, lanes] = (merge_heads(right[: heads * PAD], heads) * 0.125).astype(bf16)
        table_ref[: heads * HALF] += right[heads * PAD :]
        extra = dot(relt_ref[:, : heads * HALF], offsets[b])
        turned = jnp.concatenate(sums[b] if heads == 2 else sums[b] + [jnp.zeros_like(sums[b][0])], axis=0) + extra
        turned = turned.astype(bf16)
        dq_ref[rows, lanes] = turned.T


class Place:
    def __init__(self, tp, dp):
        self.tp, self.dp = tp, dp
        self.d, self.me = lax.axis_index("dp"), lax.axis_index("tp")
        c, x, y = self.d % 2, (self.d // 2) % 2, (self.d // 4) % 2
        self.c = c
        self.core = self.d + 1 - 2 * c
        peer_x, peer_y = self.d + 2 - 4 * x, self.d + 4 - 8 * y
        self.x, self.y = peer_x, peer_y
        self.first = peer_x * (1 - c) + peer_y * c
        self.second = peer_y * (1 - c) + peer_x * c
        self.bit_one = x * (1 - c) + y * c
        self.bit_two = y * (1 - c) + x * c
        self.extra = []
        for bit in range(3, dp.bit_length() - 1):
            step = 1 << bit
            self.extra.append(self.d + step * (1 - 2 * ((self.d // step) % 2)))

    def block(self, one, two, c=None):
        c = self.c if c is None else c
        y = two * (1 - c) + one * c
        x = one * (1 - c) + two * c
        return 2 * y + x

    def flips(self):
        a, b = self.bit_one, self.bit_two
        return [self.block(a, b), self.block(1 - a, b), self.block(a, 1 - b), self.block(1 - a, 1 - b)]

    def other(self, step):
        return (self.me + step) % self.tp

    def greet_start(self):
        barrier = pltpu.get_barrier_semaphore()
        for peer in [self.core, self.x, self.y] + self.extra:
            pl.semaphore_signal(barrier, inc=1, device_id=(peer, self.me), device_id_type=MESH)

        def signal(step, carry):
            pl.semaphore_signal(barrier, inc=1, device_id=(self.d, self.other(step)), device_id_type=MESH)
            return carry

        lax.fori_loop(1, self.tp, signal, 0)

    def greet_wait(self):
        pl.semaphore_wait(pltpu.get_barrier_semaphore(), 3 + len(self.extra) + self.tp - 1)


def piece(ref, block, c):
    rows, columns = ref.shape[-2] // 4, ref.shape[-1] // 2
    lead = (slice(None),) * (len(ref.shape) - 2)
    return ref.at[
        lead + (pl.ds(pl.multiple_of(block * rows, rows), rows), pl.ds(pl.multiple_of(c * columns, columns), columns))
    ]


def remote(src, dst, send, recv, device):
    return pltpu.make_async_remote_copy(
        src_ref=src, dst_ref=dst, send_sem=send, recv_sem=recv, device_id=device, device_id_type=MESH
    )


class Spread:
    def __init__(self, place, ref, send, recv, at):
        self.place, self.ref, self.send, self.recv, self.at = place, ref, send, recv, at

    def copy(self, k, arriving):
        place = self.place
        flips = place.flips()
        me = place.me
        if k == 0:
            device, block, came = place.first, flips[0], flips[1]
            half = came_half = place.c
        elif k < 3:
            device, block, came = place.second, flips[k - 1], flips[k + 1]
            half = came_half = place.c
        else:
            device, block = place.core, flips[k - 3]
            came = flips[(0, 2, 1, 3)[k - 3]]
            half, came_half = place.c, 1 - place.c
        where, side = (came, came_half) if arriving else (block, half)
        view = piece(self.ref, where, side)
        index = tuple(self.at) + (k,)
        return remote(view, view, self.send.at[index], self.recv.at[index], (device, me))

    def start_own(self):
        for k in (0, 1, 3):
            self.copy(k, False).start()

    def after_first(self):
        self.copy(0, True).wait_recv()
        for k in (2, 4):
            self.copy(k, False).start()

    def after_second(self):
        for k in (1, 2):
            self.copy(k, True).wait_recv()
            self.copy(k + 4, False).start()

    def ready(self):
        for k in range(3, 7):
            self.copy(k, True).wait_recv()

    def sent(self):
        for k in range(7):
            self.copy(k, False).wait_send()


def repeat(count, fn, first=0):
    def step(i, carry):
        fn(i)
        return carry

    lax.fori_loop(first, count, step, 0)


def normal_rows(values):
    centre = jnp.mean(values, axis=-1, keepdims=True)
    centred = values - centre
    scale = lax.rsqrt(jnp.mean(centred * centred, axis=-1, keepdims=True) + 1e-06)
    return centred * scale, scale


def normal_back(gradient, normal, scale, gain):
    e = gradient * gain
    return scale * (
        e - jnp.mean(e, axis=-1, keepdims=True) - normal * jnp.mean(e * normal, axis=-1, keepdims=True)
    )


def block_kernel(tp, dp, names, *refs):
    r = dict(zip(names, refs))
    place = Place(tp, dp)
    me, c, one_bit, two_bit = place.me, place.c, place.bit_one, place.bit_two
    x, cot, fill, vec = r["x"], r["cot"], r["fill"], r["vec"]
    a, f, g, ga = r["a"], r["f"], r["g"], r["ga"]
    normed, q, k, v, mix = r["normed"], r["q"], r["k"], r["v"], r["mix"]
    middle, total, slide = r["middle"], r["total"], r["slide"]
    normed_two, turned_two, hid, dbs = r["normed_two"], r["turned_two"], r["hid"], r["dbs"]
    sums, bias = r["sums"], r["bias"]
    rows_all, width = x.shape
    part = a.shape[2]
    units = f.shape[3]
    windows = rows_all // PAD
    half_rows = rows_all // 2
    columns = width // TILE
    halves_of_rows = [slice(0, half_rows), slice(half_rows, rows_all)]
    blocks = []
    for window in range(windows // 2):
        for start in range(0, part, LANES):
            blocks.append((window, start, min(2, (part - start) // HALF)))

    weights = [
        (r["own_a"].at[0:3], lambda s: a.at[s, 0:3]),
        (r["own_a"].at[3:4], lambda s: a.at[s, 3:4]),
        (r["own_f"], lambda s: f.at[s]),
        (r["own_g"], lambda s: g.at[s]),
    ]
    own_copy = [
        pltpu.make_async_copy(src, dst, r["local"].at[i])
        for i, (src, dst) in enumerate(
            [(r["own_a"], a.at[me]), (r["own_f"], f.at[me]), (r["own_g"], g.at[me]), (r["own_bias"], bias.at[me])]
        )
    ]

    def z_copy(w, other, arriving):
        src, dst = weights[w]
        owner = other if arriving else me
        block = place.flips()[0]
        return remote(
            piece(src, block, c),
            piece(dst(owner), block, c),
            r["z_send"].at[w, other],
            r["z_recv"].at[w, owner],
            (place.d, other),
        )

    def bias_copy(other, arriving):
        owner = other if arriving else me
        return remote(r["own_bias"], bias.at[owner], r["b_send"].at[other], r["b_recv"].at[owner], (place.d, other))

    def spread(w, s):
        return Spread(place, weights[w][1](s), r["p_send"], r["p_recv"], (w, s))

    def send(w):
        repeat(tp, lambda j: z_copy(w, place.other(tp - j), False).start(), 1)

    def first(w, j):
        z_copy(w, place.other(j), True).wait_recv()
        spread(w, place.other(j)).start_own()

    def second(w, j):
        spread(w, place.other(j)).after_first()

    def third(w, j):
        spread(w, place.other(j)).after_second()

    def ready(w, j):
        spread(w, place.other(j)).ready()

    def sent(w, j):
        spread(w, place.other(j)).sent()
        z_copy(w, place.other(j), False).wait_send()

    grads = [ga, f, g]
    halves, quarters, eighths, arrived, final = ([r[name + str(w)] for w in range(3)] for name in ("h", "u", "e", "t", "o"))
    outs = [r["out_a"], r["out_f"], r["out_g"]]

    def rows_of(block, size):
        return pl.ds(pl.multiple_of(block * size, size), size)

    def lanes_of(w, side):
        count = grads[w].shape[-1] // 2
        return pl.ds(pl.multiple_of(side * count, count), count)

    def core_copy(w, s):
        return remote(
            grads[w].at[s, :, :, lanes_of(w, 1 - c)],
            halves[w].at[s],
            r["core_send"].at[w, s],
            r["core_recv"].at[w, s],
            (place.core, me),
        )

    def quarter_copy(w, s, two):
        size = eighths[w].shape[2]
        return remote(
            halves[w].at[s, :, rows_of(place.block(1 - one_bit, two), size)],
            quarters[w].at[s, :, two * size : (two + 1) * size],
            r["one_send"].at[w, s, two],
            r["one_recv"].at[w, s, two],
            (place.first, me),
        )

    def eighth_copy(w, s):
        size = eighths[w].shape[2]
        return remote(
            quarters[w].at[s, :, rows_of(1 - two_bit, size)],
            eighths[w].at[s],
            r["two_send"].at[w, s],
            r["two_recv"].at[w, s],
            (place.second, me),
        )

    def shard_copy(w, other, arriving):
        owner = other if arriving else me
        return remote(
            eighths[w].at[other], arrived[w].at[owner], r["s_send"].at[w, other], r["s_recv"].at[w, owner], (place.d, other)
        )

    def reduce_one(w, s):
        core_copy(w, s).start()

    def reduce_two(w, s):
        core_copy(w, s).wait_recv()
        size = eighths[w].shape[2]

        def add(block):
            rows = rows_of(block, size)
            halves[w][s, :, rows] += grads[w][s, :, rows, lanes_of(w, c)]

        for two in range(2):
            add(place.block(1 - one_bit, two))
            quarter_copy(w, s, two).start()
        for two in range(2):
            add(place.block(one_bit, two))

    def reduce_three(w, s):
        size = eighths[w].shape[2]
        for two in range(2):
            quarter_copy(w, s, two).wait_recv()

        def add(two):
            rows = rows_of(two, size)
            quarters[w][s, :, rows] += halves[w][s, :, rows_of(place.block(one_bit, two), size)]

        add(1 - two_bit)
        eighth_copy(w, s).start()
        add(two_bit)

    def reduce_four(w, j):
        s = place.other(j)
        eighth_copy(w, s).wait_recv()
        eighths[w][s] += quarters[w][s, :, rows_of(two_bit, eighths[w].shape[2])]
        if j > 0:
            shard_copy(w, s, False).start()

    def out_spread(w):
        return Spread(place, outs[w], r["q_send"], r["q_recv"], (w,))

    def reduce_five(w):
        repeat(tp, lambda j: shard_copy(w, place.other(j), True).wait_recv(), 1)
        arrived[w][me] = eighths[w][me]
        value = arrived[w][0].astype(f32)
        for s in range(1, tp):
            value += arrived[w][s].astype(f32)
        final[w][...] = value.astype(bf16)
        for i, peer in enumerate(place.extra):
            copy = remote(final[w], r["x" + str(w)].at[i], r["x_send"].at[w, i], r["x_recv"].at[w, i], (peer, me))
            copy.start()
            copy.wait()
            final[w][...] += r["x" + str(w)][i]
        put = pltpu.make_async_copy(final[w], piece(outs[w], place.flips()[0], c), r["put"].at[w])
        put.start()
        put.wait()
        out_spread(w).start_own()

    def reduce_done(w):
        out_spread(w).ready()
        out_spread(w).sent()

        def one(j):
            s = place.other(j)
            core_copy(w, s).wait_send()
            for two in range(2):
                quarter_copy(w, s, two).wait_send()
            eighth_copy(w, s).wait_send()

        repeat(tp, one)
        repeat(tp, lambda j: shard_copy(w, place.other(j), False).wait_send(), 1)

    levels = [place.core, place.x, place.y] + place.extra
    table = r["table"]
    small = [(sums, r["sums_in"], r["sums_z"], r["sums_out"]), (r["fold"], r["fold_in"], r["fold_z"], r["fold_out"])]

    def small_copy(i, level):
        return remote(
            small[i][0], small[i][1].at[level], r["v_send"].at[i, level], r["v_recv"].at[i, level], (levels[level], me)
        )

    def small_start(level):
        for i in range(2):
            small_copy(i, level).start()

    def small_level(level):
        for i in range(2):
            small_copy(i, level).wait()
            small[i][0][...] += small[i][1][level]
        if level + 1 < len(levels):
            small_start(level + 1)

    def small_shard(i, other, arriving):
        owner = other if arriving else me
        return remote(small[i][0], small[i][2].at[owner], r["vz_send"].at[i, other], r["vz_recv"].at[i, owner], (place.d, other))

    def small_across():
        for i in range(2):
            repeat(tp, lambda j: small_shard(i, place.other(j), False).start(), 1)

    def small_finish():
        for i in range(2):
            repeat(tp, lambda j: small_shard(i, place.other(j), True).wait_recv(), 1)
            small[i][2][me] = small[i][0][...]
            value = small[i][2][0]
            for s in range(1, tp):
                value += small[i][2][s]
            small[i][3][...] = value
            repeat(tp, lambda j: small_shard(i, place.other(j), False).wait_send(), 1)

    def chunk(i):
        return pl.ds(pl.multiple_of(i * CHUNK, CHUNK), CHUNK)

    chunks = rows_all // CHUNK

    def keep_rows(rows, count):
        keep = (fill[rows] == 0.0).astype(f32)
        return jnp.concatenate([keep] * (count // LANES), axis=1)

    def norm_one(i):
        rows = chunk(i)
        normal, _ = normal_rows(x[rows].astype(f32))
        normed[rows] = (normal * vec[0:1] + vec[1:2]).astype(bf16)

    def project(s):
        for t, target in enumerate((q, k, v)):
            for rows in halves_of_rows:
                value = dot(normed[rows], a[s, t], NT)
                if t != 1:
                    value = value + bias[s, 1 + t // 2 : 2 + t // 2, :part]
                target[s, rows, :part] = value.astype(bf16)

    def unit_view(ref, s, at):
        return ref.at[s, pl.ds(pl.multiple_of(at * half_rows, half_rows), half_rows)]

    def p_out(i):
        return pltpu.make_async_copy(r["p"].at[i % 2], r["p_hbm"].at[i], r["p_sem"].at[i % 2])

    def p_in(i):
        return pltpu.make_async_copy(r["p_hbm"].at[i], r["p"].at[i % 2], r["p_sem"].at[i % 2])

    def attend(i, s, at):
        attend_forward_unit(
            unit_view(q, s, at),
            unit_view(k, s, at),
            unit_view(v, s, at),
            unit_view(mix, s, at),
            r["p"].at[i % 2],
            fill.at[pl.ds(pl.multiple_of(at * half_rows, half_rows), half_rows)],
            r["rel"],
            r["hot"],
            r["scr_a"],
            blocks,
        )

    def attend_back(i, s, at):
        views = [unit_view(ref, s, at) for ref in (q, k, v)]
        attend_backward_unit(
            *views, unit_view(mix, s, at), r["p"].at[i % 2], *views, table, r["relt"], r["hott"], r["scr_b"], blocks
        )

    def mix_out(n):
        tile = pl.ds(pl.multiple_of(n * TILE, TILE), TILE)
        for rows in halves_of_rows:
            value = dot(mix[0, rows, :part], a[0, 3, :, tile])
            for s in range(1, tp):
                value = value + dot(mix[s, rows, :part], a[s, 3, :, tile])
            middle[rows, tile] = x[rows, tile].astype(f32) + keep_rows(rows, TILE) * (value + vec[4:5, tile])

    def norm_two(i):
        rows = chunk(i)
        value = middle[rows]
        normal, _ = normal_rows(value)
        normed_two[rows] = (normal * vec[2:3] + vec[3:4]).astype(bf16)
        total[rows] = value + keep_rows(rows, width) * vec[5:6]
        slide[rows] = jnp.zeros_like(value)

    def layers(s):
        def one(n):
            tile = pl.ds(pl.multiple_of(n * TILE, TILE), TILE)
            column = None
            for rows in halves_of_rows:
                before = dot(normed_two[rows], f[s, 0, :, tile]) + bias[s, 0:1, tile]
                keep = keep_rows(rows, TILE)
                phi = 0.5 * (1.0 + lax.erf(before * root_half))
                hid[rows, tile] = (before * phi * keep).astype(bf16)
                slope = phi + before * (jnp.exp(-0.5 * before * before) * bell)
                down = (slope * (dot(cot[rows], g[s, 0, tile, :], NT) * keep)).astype(bf16)
                dbs[rows, tile] = down
                part_sum = jnp.sum(down.astype(f32), axis=0, keepdims=True)
                column = part_sum if column is None else column + part_sum
            r["layer_sum"][s, 0:1, tile] = column

        repeat(units // TILE, one)

    def layers_add(s):
        def one(n):
            tile = pl.ds(pl.multiple_of(n * TILE, TILE), TILE)
            for rows in halves_of_rows:
                total[rows, tile] += dot(hid[rows], g[s, 0, :, tile])
                slide[rows, tile] += dot(dbs[rows], f[s, 0, tile, :], NT)

        repeat(columns, one)

    def layers_grad(s):
        def one(n):
            tile = pl.ds(pl.multiple_of(n * TILE, TILE), TILE)
            g[s, 0, tile, :] = dot(hid[:, tile], cot[...], TN).astype(bf16)
            f[s, 0, :, tile] = dot(turned_two[...], dbs[:, tile]).astype(bf16)

        repeat(units // TILE, one)

    def middle_back(i):
        rows = chunk(i)
        hid[rows, :width] = total[rows].astype(bf16)
        keep = keep_rows(rows, width)
        gradient = slide[rows]
        normal, scale = normal_rows(middle[rows])
        outer = cot[rows].astype(f32)
        down = outer + normal_back(gradient, normal, scale, vec[2:3])
        slide[rows] = down
        masked = down * keep
        dbs[rows, :width] = masked.astype(bf16)
        total[rows] = jnp.zeros_like(down)
        add = lambda at, value: sums.__setitem__(
            (slice(at, at + 1), slice(None)), sums[at : at + 1] + jnp.sum(value, axis=0, keepdims=True)
        )
        add(1, gradient * normal)
        add(3, gradient)
        add(4, masked)
        add(5, outer * keep)

    def mix_back(s):
        ga[s, 3] = dot(mix[s, :, :part], dbs[:, :width], TN).astype(bf16)
        for rows in halves_of_rows:
            mix[s, rows, :part] = dot(dbs[rows, :width], a[s, 3], NT).astype(bf16)

    def project_back(s):
        for t, source in enumerate((q, k, v)):
            ga[s, t] = dot(source[s, :, :part], normed[...], TN).astype(bf16)
        for i, source in ((0, q), (1, v)):
            value = jnp.sum(source[s, :, :part].astype(f32), axis=0, keepdims=True)
            r["head_sum"][s, i : i + 1, :part] = value

        def one(n):
            tile = pl.ds(pl.multiple_of(n * TILE, TILE), TILE)
            for rows in halves_of_rows:
                total[rows, tile] += (
                    dot(q[s, rows, :part], a[s, 0, :, tile])
                    + dot(k[s, rows, :part], a[s, 1, :, tile])
                    + dot(v[s, rows, :part], a[s, 2, :, tile])
                )

        repeat(columns, one)

    def input_back(i):
        rows = chunk(i)
        gradient = total[rows]
        normal, scale = normal_rows(x[rows].astype(f32))
        middle[rows] = slide[rows] + normal_back(gradient, normal, scale, vec[0:1])
        sums[0:1] = sums[0:1] + jnp.sum(gradient * normal, axis=0, keepdims=True)
        sums[2:3] = sums[2:3] + jnp.sum(gradient, axis=0, keepdims=True)

    def run(events, index):
        for at, steps in events.items():

            @pl.when(index == at)
            def _(steps=steps):
                for fn, *args in steps:
                    fn(*args)

    everyone = list(range(1, tp))
    last = tp - 1
    each = lambda fn, w: [(fn, w, j) for j in everyone]

    for copy in own_copy:
        copy.start()
    place.greet_start()
    repeat(chunks, norm_one)
    lead = part - part % LANES
    if lead < part:
        for ref in (q, k, v, mix):
            for s in range(tp):
                ref[s, :, lead:] = jnp.zeros((rows_all, LANES), bf16)
    sums[...] = jnp.zeros_like(sums)
    table[...] = jnp.zeros_like(table)
    r["scr_b"][...] = jnp.zeros_like(r["scr_b"])
    place.greet_wait()
    send(0)
    repeat(tp, lambda j: bias_copy(place.other(tp - j), False).start(), 1)
    send(1)
    own_copy[0].wait()
    own_copy[3].wait()

    before_project, before_unit = gather_events(
        tp, dict(send=send, first=first, second=second, third=third, ready=ready, bias=lambda: repeat(tp, lambda j: bias_copy(place.other(j), True).wait_recv(), 1))
    )

    def forward_unit(i):
        j, at = i // 2, i % 2
        s = place.other(j)

        @pl.when(at == 0)
        def _():
            run(before_project, j)
            project(s)

        run(before_unit, i)

        @pl.when(i >= 2)
        def _():
            p_out(i - 2).wait()

        attend(i, s, at)
        p_out(i).start()

    unit_count = 2 * tp
    repeat(unit_count, forward_unit)
    p_out(unit_count - 2).wait()
    p_out(unit_count - 1).wait()
    for j in everyone:
        ready(1, j)
    repeat(columns, mix_out)
    repeat(chunks, norm_two)
    turned_two[...] = normed_two[...].T
    own_copy[1].wait()
    own_copy[2].wait()

    stages = layer_events(tp, dict(send=send, first=first, second=second, third=third, ready=ready, sent=sent, one=reduce_one, two=reduce_two, three=reduce_three, four=reduce_four, other=place.other))

    def layer_step(j):
        s = place.other(j)
        run(stages[0], j)
        layers(s)
        run(stages[1], j)
        layers_add(s)
        run(stages[2], j)
        layers_grad(s)
        run(stages[3], j)

    repeat(tp, layer_step)

    repeat(chunks, middle_back)
    put_out = pltpu.make_async_copy(hid.at[:, :width], r["out"], r["local"].at[1])
    put_out.start()
    back = back_events(tp, dict(sent=sent, one=reduce_one, two=reduce_two, three=reduce_three, four=reduce_four, five=reduce_five, after_first=lambda w: out_spread(w).after_first(), after_second=lambda w: out_spread(w).after_second(), other=place.other))
    run({0: back["start"]}, 0)
    p_in(0).start()
    repeat(tp, lambda j: mix_back(place.other(j)))

    def backward_unit(i):
        j, at = i // 2, i % 2
        s = place.other(j)
        run(back["unit"], i)

        @pl.when(i + 1 < unit_count)
        def _():
            p_in(i + 1).start()

        p_in(i).wait()
        attend_back(i, s, at)

        @pl.when(at == 1)
        def _():
            project_back(s)
            run(back["shard"], j)

    repeat(unit_count, backward_unit)
    repeat(chunks, input_back)
    put_in = pltpu.make_async_copy(middle, r["grad_x"], r["local"].at[2])
    put_in.start()
    for s in range(tp):
        for n in range(units // width):
            at = 8 + s * (units // width) + n
            sums[at : at + 1] = r["layer_sum"][s, 0:1, n * width : (n + 1) * width]
        sums[16 + s : 17 + s, :part] = r["head_sum"][s, 0:1, :part]
        sums[16 + s : 17 + s, width // 2 : width // 2 + part] = r["head_sum"][s, 1:2, :part]
    r["fold"][...] = table[:HALF, :HALF] + table[HALF:, HALF:]
    small_start(0)
    two, three, four = reduce_two, reduce_three, reduce_four
    s = place.other(last)
    two(0, s)
    small_level(0)
    three(0, s)
    small_level(1)
    four(0, last)
    for level in range(2, len(levels)):
        small_level(level)
    small_across()
    reduce_five(0)
    out_spread(0).after_first()
    small_finish()
    out_spread(0).after_second()
    for w in (2, 1, 0):
        reduce_done(w)
    for j in everyone:
        sent(0, j)
        sent(1, j)
    repeat(tp, lambda j: bias_copy(place.other(tp - j), False).wait_send(), 1)
    put_out.wait()
    put_in.wait()


def gather_events(tp, do):
    every = list(range(1, tp))
    project, unit = {}, {}
    at = lambda table, key, *step: table.setdefault(key, []).append(step)
    unit_of = lambda i: min(i, 2 * tp - 1)
    at(unit, 0, do["first"], 0, 1)
    at(unit, 1, do["second"], 0, 1)
    for j in every[1:]:
        at(unit, 1, do["first"], 0, j)
    at(project, 1, do["third"], 0, 1)
    for j in every[1:]:
        at(project, 1, do["second"], 0, j)
    at(project, 1, do["bias"])
    at(project, 1, do["ready"], 0, 1)
    for j in every[1:]:
        at(unit, unit_of(2), do["third"], 0, j)
    at(unit, unit_of(2), do["send"], 2)
    for j in every:
        at(unit, unit_of(3), do["first"], 1, j)
    for j in every[1:]:
        at(project, j, do["ready"], 0, j)
    for j in every:
        at(unit, unit_of(4), do["second"], 1, j)
    at(unit, unit_of(4), do["send"], 3)
    for j in every:
        at(unit, unit_of(5), do["third"], 1, j)
        at(unit, unit_of(5), do["first"], 2, j)
    for j in every:
        at(unit, unit_of(6), do["second"], 2, j)
    for j in every:
        at(unit, unit_of(7), do["third"], 2, j)
        at(unit, unit_of(7), do["first"], 3, j)
    return project, unit


def layer_events(tp, do):
    every = list(range(1, tp))
    stages = [{}, {}, {}, {}]
    at = lambda stage, key, *step: stages[stage].setdefault(key, []).append(step)
    for j in every:
        at(0, 0, do["second"], 3, j)
    for j in every:
        at(1, 0, do["third"], 3, j)
    for j in every:
        at(0, j, do["ready"], 2, j)
        at(0, j, do["ready"], 3, j)
        at(2, j, do["sent"], 2, j)
        at(2, j, do["sent"], 3, j)
    for j in range(tp):
        for w in (2, 1):
            at(3, j, do["one"], w, do["other"](j))
    for j in every:
        for w in (2, 1):
            at(1, j, do["two"], w, do["other"](j - 1))
        for w in (2, 1):
            at(3, j, do["three"], w, do["other"](j - 1))
    for j in every[1:]:
        for w in (2, 1):
            at(2, j, do["four"], w, j - 2)
    return stages


def back_events(tp, do):
    unit, shard, start = {}, {}, []
    at = lambda table, key, *step: table.setdefault(key, []).append(step)
    last = tp - 1
    for w in (2, 1):
        start.append((do["two"], w, do["other"](last)))
    for w in (2, 1):
        if last > 0:
            at(unit, 0, do["four"], w, last - 1)
    for w in (2, 1):
        at(unit, 0, do["three"], w, do["other"](last))
    for w in (2, 1):
        at(unit, 1, do["four"], w, last)
    for w in (2, 1):
        at(unit, 2, do["five"], w)
    for w in (2, 1):
        at(unit, 3, do["after_first"], w)
    for w in (2, 1):
        at(unit, 3, do["after_second"], w)
    for j in range(tp):
        at(shard, j, do["one"], 0, do["other"](j))
        if j > 0:
            at(unit, 2 * j, do["two"], 0, do["other"](j - 1))
            at(unit, 2 * j + 1, do["three"], 0, do["other"](j - 1))
            at(shard, j, do["four"], 0, j - 1)
    return dict(unit=unit, shard=shard, start=start)


def whole_block(tp, dp, x, cot, fill, vec, own_a, own_f, own_g, own_bias, rel, relt, hot, hott):
    rows, width = x.shape
    part = own_a.shape[1]
    units = own_f.shape[2]
    heads = (rows // PAD // 2) * (part // HEAD_DIM)
    wide = -(-part // LANES) * LANES
    unit_count = 2 * tp
    any_space = pl.BlockSpec(memory_space=pl.ANY)
    vmem = pl.BlockSpec(memory_space=pltpu.VMEM)
    dma = pltpu.SemaphoreType.DMA
    inputs = [
        ("x", x, vmem),
        ("cot", cot, vmem),
        ("fill", fill, vmem),
        ("vec", vec, vmem),
        ("own_a", own_a, any_space),
        ("own_f", own_f, any_space),
        ("own_g", own_g, any_space),
        ("own_bias", own_bias, any_space),
        ("rel", rel, vmem),
        ("relt", relt, vmem),
        ("hot", hot, vmem),
        ("hott", hott, vmem),
    ]
    shape = jax.ShapeDtypeStruct
    outputs = [
        ("out", shape((rows, width), bf16), any_space),
        ("grad_x", shape((rows, width), f32), any_space),
        ("out_a", shape(own_a.shape, bf16), any_space),
        ("out_f", shape(own_f.shape, bf16), any_space),
        ("out_g", shape(own_g.shape, bf16), any_space),
        ("sums_out", shape((24, width), f32), vmem),
        ("fold_out", shape((HALF, HALF), f32), vmem),
        ("p_hbm", shape((unit_count, heads, PAD, PAD), bf16), any_space),
    ]
    buffer = lambda dims, kind: pltpu.VMEM(tuple(dims), kind)
    scratch = [
        ("a", buffer((tp,) + own_a.shape, bf16)),
        ("f", buffer((tp,) + own_f.shape, bf16)),
        ("g", buffer((tp,) + own_g.shape, bf16)),
        ("ga", buffer((tp,) + own_a.shape, bf16)),
        ("bias", buffer((tp,) + own_bias.shape, f32)),
        ("normed", buffer((rows, width), bf16)),
    ]
    scratch += [(name, buffer((tp, rows, wide), bf16)) for name in ("q", "k", "v", "mix")]
    scratch += [("p", buffer((2, heads, PAD, PAD), bf16))]
    scratch += [(name, buffer((rows, width), f32)) for name in ("middle", "total", "slide")]
    scratch += [("normed_two", buffer((rows, width), bf16)), ("turned_two", buffer((width, rows), bf16))]
    scratch += [(name, buffer((rows, units), bf16)) for name in ("hid", "dbs")]
    scratch += [
        ("sums", buffer((24, width), f32)),
        ("table", buffer((LANES, LANES), f32)),
        ("fold", buffer((HALF, HALF), f32)),
        ("layer_sum", buffer((tp, 8, units), f32)),
        ("head_sum", buffer((tp, 8, wide), f32)),
        ("scr_a", buffer((heads, HALF, PAD), f32)),
        ("scr_b", buffer((heads, 2, 48, PAD), f32)),
    ]
    levels = dp.bit_length() - 1
    more = levels - 3
    for w, own in enumerate((own_a, own_f, own_g)):
        n, count, lanes = own.shape[0], own.shape[1], own.shape[2] // 2
        scratch += [
            ("h" + str(w), buffer((tp, n, count, lanes), bf16)),
            ("u" + str(w), buffer((tp, n, count // 2, lanes), bf16)),
            ("e" + str(w), buffer((tp, n, count // 4, lanes), bf16)),
            ("t" + str(w), buffer((tp, n, count // 4, lanes), bf16)),
            ("o" + str(w), buffer((n, count // 4, lanes), bf16)),
        ]
        if more:
            scratch += [("x" + str(w), buffer((more, n, count // 4, lanes), bf16))]
    for name, dims in (("sums", (24, width)), ("fold", (HALF, HALF))):
        scratch += [(name + "_in", buffer((levels,) + dims, f32)), (name + "_z", buffer((tp,) + dims, f32))]
    semaphores = dict(local=(4,), p_sem=(2,), put=(3,))
    for name, dims in dict(
        z=(4, tp), p=(4, tp, 7), b=(tp,), core=(3, tp), one=(3, tp, 2), two=(3, tp), s=(3, tp), q=(3, 7), x=(3, max(more, 1)), v=(2, levels), vz=(2, tp)
    ).items():
        semaphores[name + "_send"] = semaphores[name + "_recv"] = dims
    scratch += [(name, dma(dims)) for name, dims in semaphores.items()]
    names = [entry[0] for entry in inputs + outputs + scratch]
    return pl.pallas_call(
        lambda *refs: block_kernel(tp, dp, names, *refs),
        in_specs=[entry[2] for entry in inputs],
        out_specs=[entry[2] for entry in outputs],
        out_shape=[entry[1] for entry in outputs],
        scratch_shapes=[entry[1] for entry in scratch],
        compiler_params=pltpu.CompilerParams(collective_id=1, has_side_effects=True, vmem_limit_bytes=VMEM_LIMIT),
    )(*[entry[1] for entry in inputs])


def pad_windows(rows):
    windows = rows.shape[0] // SLOTS
    cut = rows.reshape((windows, SLOTS) + rows.shape[1:])
    return jnp.pad(cut, ((0, 0), (0, PAD - SLOTS), (0, 0))).reshape((windows * PAD,) + rows.shape[1:])


def cut_windows(rows):
    windows = rows.shape[0] // PAD
    return rows.reshape((windows, PAD) + rows.shape[1:])[:, :SLOTS].reshape((windows * SLOTS,) + rows.shape[1:])


def keep_slots(height, breadth, windows):
    first = lax.axis_index("tp") * windows
    window = (first + jnp.arange(windows, dtype=jnp.int32))[:, None]
    inside = jnp.arange(PAD, dtype=jnp.int32)[None, :]
    row_at = window // GRID * WIN + inside // WIN
    column_at = window % GRID * WIN + inside % WIN
    real = inside < SLOTS
    return (row_at < height) & (column_at < breadth) & real, real


def body(
    tokens,
    heights,
    widths,
    norm_gain,
    norm_bias,
    w_qkv,
    b_qv,
    rel_pos,
    w_proj,
    b_proj,
    w_fc1,
    b_fc1,
    w_fc2,
    b_fc2,
    cotangent,
):
    tp, dp = lax.axis_size("tp"), lax.axis_size("dp")
    width = tokens.shape[1]
    windows = tokens.shape[0] // SLOTS
    part, units = w_qkv.shape[2], w_fc1.shape[1]
    keep, real = keep_slots(heights[0], widths[0], windows)
    fill = jnp.where(keep, 0.0, jnp.where(real, neg_fill, pad_fill)).astype(f32)
    fill = jnp.broadcast_to(fill.reshape(-1, 1), (windows * PAD, LANES))
    vec = jnp.concatenate([norm_gain[0:1], norm_bias[0:1], norm_gain[1:2], norm_bias[1:2], b_proj[None], b_fc2[None]])
    vec = jnp.pad(vec.astype(f32), ((0, 2), (0, 0)))
    biases = jnp.concatenate([b_fc1[None].astype(f32), jnp.pad(b_qv.astype(f32), ((0, 0), (0, units - part)))])
    biases = jnp.pad(biases, ((0, 5), (0, 0)))
    turned = jnp.concatenate([w_qkv.transpose(0, 2, 1), w_proj[None]], axis=0)
    rel, relt = position_matrices(rel_pos)
    hot, hott = window_constants()
    out, grad_x, out_a, out_f, out_g, sums, fold, _ = whole_block(
        tp, dp, pad_windows(tokens), pad_windows(cotangent), fill, vec, turned, w_fc1[None], w_fc2[None], biases, rel, relt, hot, hott
    )
    me = lax.axis_index("tp")
    offsets = 2 * WIN - 1
    grad_rel = jnp.stack([fold[:offsets], fold[32 : 32 + offsets]])[:, ::-1, :]
    per = units // width
    mine = lax.dynamic_slice_in_dim(sums, 16 + me, 1, 0)
    return (
        cut_windows(out),
        cut_windows(grad_x),
        sums[0:2],
        sums[2:4],
        out_a[:3].transpose(0, 2, 1).astype(f32),
        jnp.concatenate([mine[:, :part], mine[:, width // 2 : width // 2 + part]]),
        grad_rel,
        out_a[3].astype(f32),
        sums[4],
        out_f[0].astype(f32),
        lax.dynamic_slice_in_dim(sums, 8 + me * per, per, 0).reshape(-1),
        out_g[0].astype(f32),
        sums[5],
    )


def solution(mesh):
    rows = P(("dp", "tp"), None)
    return jax.shard_map(
        body,
        mesh=mesh,
        in_specs=(
            rows,
            P("dp"),
            P("dp"),
            P(),
            P(),
            P(None, None, "tp"),
            P(None, "tp"),
            P(),
            P("tp", None),
            P(),
            P(None, "tp"),
            P("tp"),
            P("tp", None),
            P(),
            rows,
        ),
        out_specs=(
            rows,
            rows,
            P(),
            P(),
            P(None, None, "tp"),
            P(None, "tp"),
            P(),
            P("tp", None),
            P(),
            P(None, "tp"),
            P("tp"),
            P("tp", None),
            P(),
        ),
        check_vma=False,
    )
```

time: 773 us -> 266 us (0.34); the launches traced: 761 us -> 264 us
  waiting for transfers between devices: 353 us -> 0 us
  Pallas kernels: 69 us -> 230 us
  blocking collectives: 91.5 us -> 0 us
  local copies, waits for them, and re-layouts: 110 us -> 20.1 us
  matrix products: 84.7 us -> 0 us
  between operations: 16.6 us -> 2.19 us
  starting transfers between devices: 12.9 us -> 0 us
  other arithmetic: 23.5 us -> 11.6 us
    reduce_scatter x4 -> x0, waiting for transfers between devices: 221 us -> none  [spread_sum(): lax.psum_scatter(cut.reshape((dp * tp,) + cut.shape[2:]), ('dp', 'tp'), s...]
    pallas_call x2 -> x1, Pallas kernels: 69 us -> 230 us  [whole_block(): pl.pallas_call(lambda *refs: block_kernel(tp, dp, names, *refs), in_specs...]
    all_gather x6 -> x0, waiting for transfers between devices: 132 us -> none  [the longest x4 101 us: gather_shards(): pieces = lax.all_gather(piece, ('dp', 'tp'), axis=0, tiled=False)]
    dot_general x18 -> x0, matrix products: 84.7 us -> none  [dot(): return lax.dot_general(a, b, (dims, ((), ())), preferred_element_type=f32)]
    all_gather x4 -> x0, blocking collectives: 49.7 us -> none  [the longest x2 23.8 us: spread_sum(): return lax.all_gather(mine[0], 'dp', axis=split, tiled=True).astype(f32)]
    convert_element_type x9 -> x1, local copies, waits for them, and re-layouts: 43.6 us -> 0.01 us  [body(): b_fc1[None].astype(f32)]
    psum x1 -> x0, blocking collectives: 41.8 us -> none  [body(): lax.psum((jnp.stack([jnp.sum(d_normed * normal_one, axis=0), jnp.sum(d_no...]
    transpose x4 -> x1, local copies, waits for them, and re-layouts: 16.5 us -> 0.6 us  [window_constants(): hot[:, :32]]
  transfers between devices with their start and end apart: 10 -> 0, of which waited for: 8 -> 0; matrix products, arithmetic and copies ran while one was open for 27% -> 0% of each run, Pallas kernels for 9% -> 0%
where the time goes in v2:
time: 266 us; the launch traced here: 264 us
  Pallas kernels  230 us (86%)
  local copies, waits for them, and re-layouts  20.1 us (8%)
  other arithmetic  11.6 us (4%)
    pallas_call x1, Pallas kernels, whole_block(): pl.pallas_call(lambda *refs: block_kernel(tp, dp, names, *refs), in_specs...  230 us

profile of v2, /device:TPU:0, one launch (start us, length us, event | category | flops | bytes accessed | tf_op | source)
XLA Modules:
  0.0 264.2 jit_solution(7979873922170814941)
XLA Ops:
  0.6 0.0 copy-start.1
  2.1 0.1 fusion.13
  2.2 0.1 reshape.302
  2.3 0.9 broadcast_in_dim.90.refs_2_
  3.2 0.8 fusion.20
  4.0 0.7 broadcast_in_dim.91
  4.7 0.7 broadcast_in_dim.92
  5.4 0.6 pad_convert_fusion.1.refs_3_
  6.0 0.1 fusion.4
  6.1 0.1 fusion.2
  6.2 0.8 copy.36.refs_10_
  7.0 0.6 slice_bitcast_fusion.refs_11_
  7.6 0.7 copy.32
  8.3 0.1 copy.33
  8.4 0.7 fusion.8
  9.1 0.7 copy.35.refs_8_
  9.8 0.0 copy-done.1
  9.9 0.3 reshape.291
  10.1 0.0 copy-start.2
  10.1 1.1 pad.32
  11.3 0.6 copy-done.2
  11.9 0.3 reshape.293
  12.1 0.0 copy-start.5
  12.2 0.0 copy-start.6
  12.2 1.1 pad.33
  13.3 0.4 copy-done.5
  13.7 0.2 copy-done.6
  13.8 1.1 pad_maximum_fusion.refs_4_
  15.0 0.0 copy-done.7
  15.0 0.0 copy-done.8
  15.0 0.6 pad_convert_fusion.refs_7_
  15.6 230.3 %shard_map.246 = (bf16[832,768]{1,0:T(8,128)(2,1)}, f32[832,768]{1,0:T(8,128)}, bf16[4,192,768]{2,1,0:T(8,128)(2,1)}, bf16[1,768,768]{2,1,0:T(8,128)(2,1)}, bf16...) custom-call(bf16[832,768]{1,0:T(8,128)(2,1)} %bitcast.32, ...), custom_call_target="tpu_custom_call" | custom-call | tf_op jit(solution)/shard_map/pallas_call | solution.py:1000
  245.9 0.8 constant_dynamic-slice_fusion
  246.7 0.6 pad_maximum_fusion.2
  247.3 0.7 slice_bitcast_fusion.2
  248.1 0.6 copy.37
  248.7 1.4 slice_reduce_fusion
  250.2 1.4 fusion.19
  251.6 2.7 %convert_bitcast_fusion = f32[3,768,192]{1,2,0:T(8,128)} fusion(bf16[4,192,768]{2,1,0:T(8,128)(2,1)} %get-tuple-element.23), kind=kLoop, calls=%fused_computation | loop fusion | flops 442368 | bytes 2654208 | tf_op jit(solution)/shard_map/convert_element_type | solution.py:1075
  254.2 1.8 bitcast_convert_fusion.2
  256.1 0.2 slice.70
  256.3 1.6 reshape.299
  257.8 1.4 slice.69
  259.2 1.2 reshape.297
  260.4 0.5 copy-done.4
  260.9 1.6 bitcast_convert_fusion
  262.5 0.1 copy-done.3
  262.6 1.6 bitcast_convert_fusion.1
  (19 shorter events, 0.2 us)
Async XLA Ops:
  0.6 9.2 %copy-start.1 = (bf16[784,768]{1,0:T(8,128)(2,1)S(1)}, bf16[784,768]{1,0:T(8,128)(2,1)}, u32[]{:S(2)}) copy-start(bf16[784,768]{1,0:T(8,128)(2,1)} %param.15) | copy-start | bytes 3612676
  10.1 1.7 copy-start.2
  12.1 1.5 copy-start.5
  12.2 1.7 copy-start.6
  13.3 1.7 copy-start.7
  13.3 1.7 copy-start.8
  251.6 4.5 %copy-start = (f32[832,768]{1,0:T(8,128)S(1)}, f32[832,768]{1,0:T(8,128)}, u32[]{:S(2)}) copy-start(f32[832,768]{1,0:T(8,128)} %get-tuple-element.21) | copy-start | bytes 7667716
  259.2 1.7 copy-start.4
  260.9 1.7 copy-start.3

commit v3 on v2

v3 whole, which is shorter than its diff:
```python
import jax
import jax.numpy as jnp
import ml_dtypes
import numpy as np
from jax import lax
from jax.experimental import pallas as pl
from jax.experimental.pallas import tpu as pltpu
from jax.sharding import PartitionSpec as P

HEAD_DIM = 64
WIN = 14
GRID = 4
SLOTS = WIN * WIN
PAD = 208
LANES = 128
HALF = 64
CHUNK = 64
ENDS = 16
PLACES = [
    ("start", 0, ("send", 0, 1), ("send", 0, 2), ("first", 0, 1), ("send", 0, 3)),
    ("project", 0, ("second", 0, 1), ("send", 1, 1)),
    ("unit", 0, ("first", 0, 2), ("third", 0, 1), ("first", 0, 3)),
    ("unit", 1, ("ready", 0, 1), ("send", 1, 3)),
    ("project", 1, ("bias_ready",), ("second", 0, 2)),
    ("unit", 2, ("second", 0, 3)),
    ("unit", 3, ("third", 0, 2), ("first", 1, 1)),
    ("project", 2, ("send", 1, 2), ("ready", 0, 2), ("third", 0, 3)),
    ("unit", 5, ("ready", 0, 3), ("first", 1, 3)),
    ("mid1", 0, ("second", 1, 1)),
    ("layers", 2, ("first", 1, 2)),
    ("add", 0, ("third", 1, 1)),
    ("grad", 0, ("second", 1, 3), ("z_sent", 1)),
    ("layers", 3, ("ready", 1, 1)),
    ("layers", 5, ("one", 1, 0), ("second", 1, 2)),
    ("add", 5, ("third", 1, 3)),
    ("grad", 3, ("two", 1, 0), ("third", 1, 2), ("sent", 1, 1)),
    ("layer3", 1, ("ready", 1, 3)),
    ("layers", 6, ("one", 1, 1), ("ready", 1, 2)),
    ("grad", 6, ("three", 1, 0), ("two", 1, 1), ("sent", 1, 2)),
    ("layers", 11, ("one", 1, 2)),
    ("add", 11, ("two", 1, 2)),
    ("grad", 9, ("sent", 1, 3)),
    ("layer3", 3, ("three", 1, 1)),
    ("down0", 0, ("one", 1, 3)),
    ("down2", 0, ("s0", 0), ("three", 1, 2), ("two", 1, 3)),
    ("back", 1, ("four", 1, 1)),
    ("shard", 0, ("one", 0, 0)),
    ("back", 2, ("s1", 0)),
    ("turn", 1, ("four", 1, 2), ("two", 0, 0)),
    ("shard", 1, ("one", 0, 1)),
    ("back", 4, ("three", 1, 3)),
    ("back", 5, ("two", 0, 1)),
    ("turn", 2, ("s2", 0)),
    ("back", 6, ("three", 0, 0), ("one", 0, 2)),
    ("turn", 3, ("two", 0, 2), ("four", 1, 3)),
    ("end0", 0, ("three", 0, 1), ("one", 0, 3)),
    ("end1", 0, ("four", 1, 0), ("three", 0, 2)),
    ("end2", 0, ("two", 0, 3), ("four", 0, 1)),
    ("end3", 0, ("five", 1)),
    ("end4", 0, ("four", 0, 2), ("three", 0, 3)),
    ("end5", 0, ("four", 0, 0), ("four", 0, 3), ("s0", 1)),
    ("end6", 0, ("s1", 1)),
    ("end7", 0, ("after_first", 1), ("s2", 1)),
    ("end8", 0, ("s3", 0), ("five", 0)),
    ("end9", 0, ("after_second", 1)),
    ("end11", 0, ("s4", 0), ("s3", 1)),
    ("end12", 0, ("after_first", 0), ("after_second", 0)),
    ("end13", 0, ("done", 1)),
    ("end14", 0, ("s4", 1)),
    ("end15", 0, ("done", 0)),
]
TILE = 256

bf16 = jnp.bfloat16
f32 = jnp.float32
neg_fill = -30000.0
pad_fill = -1e30
root_half = 0.7071067811865476
bell = 0.3989422804014327
VMEM_LIMIT = 64 << 20
MESH = pl.DeviceIdType.MESH


def dot(a, b, dims=((1,), (0,))):
    return lax.dot_general(a, b, (dims, ((), ())), preferred_element_type=f32)


NT = ((1,), (1,))
TN = ((0,), (0,))


def window_constants():
    slot = np.arange(PAD)[:, None]
    lane = np.arange(HALF)[None, :]
    place = np.where(lane % 32 < 16, slot // WIN, slot % WIN)
    hot = ((slot < SLOTS) & (lane % 16 == place)).astype(np.float32)
    zero = np.zeros_like(hot)
    both = np.concatenate([np.concatenate([hot, zero], 1), np.concatenate([zero, hot], 1)], 0)
    pick = np.zeros((LANES, HALF), np.float32)
    for offset in range(2 * WIN - 1):
        for head in range(2):
            for axis in range(2):
                pick[HALF * head + 32 * axis + offset, 32 * axis + 2 * WIN - 2 - offset] = 8.0
    narrow = lambda values: values.astype(ml_dtypes.bfloat16)
    return narrow(both), narrow(hot[:, :32].T.copy()), narrow(pick)


def stack_heads(pair, heads):
    if heads == 1:
        return pair
    lane = lax.broadcasted_iota(jnp.int32, pair.shape, 1)
    zero = jnp.zeros_like(pair)
    return jnp.concatenate([jnp.where(lane < HALF, pair, zero), jnp.where(lane < HALF, zero, pair)], axis=0)


def merge_heads(stacked, heads):
    if heads == 1:
        return stacked
    top, bottom = stacked[:PAD], stacked[PAD:]
    lane = lax.broadcasted_iota(jnp.int32, top.shape, 1)
    return jnp.where(lane < HALF, top, bottom)


def place_of_lane():
    lane = lax.broadcasted_iota(jnp.int32, (1, PAD), 1)
    row = lax.div(lane, WIN)
    return row, lane - row * WIN


def attend_forward_unit(q_ref, k_ref, v_ref, mix_ref, p_ref, fill_ref, rel_ref, hot_ref, scr_ref, blocks):
    places = place_of_lane()
    eighth = jnp.asarray(0.125, bf16)
    firsts, scores, biases = [], [], []
    count = 0
    for window, start, heads in blocks:
        firsts.append(count)
        lanes, rows = slice(start, start + LANES), slice(window * PAD, (window + 1) * PAD)
        left = jnp.concatenate([rel_ref[: heads * HALF], stack_heads(k_ref[rows, lanes], heads)], axis=0)
        both = dot(left, q_ref[rows, lanes] * eighth, NT)
        for head in range(heads):
            scr_ref[count + head] = both[head * HALF : (head + 1) * HALF]
        scores.append(both[heads * HALF :])
        count += heads
    for b, (window, start, heads) in enumerate(blocks):
        parts = []
        for head in range(heads):
            along = []
            for base, place in ((0, places[0]), (32, places[1])):
                picked = scr_ref[firsts[b] + head, base : base + 16, :]
                for at in range(WIN - 1):
                    first = base + WIN - 1 - at
                    picked = jnp.where(place == at, scr_ref[firsts[b] + head, first : first + 16, :], picked)
                along.append(picked)
            bias = jnp.concatenate(along, axis=0)
            high = bias.astype(bf16)
            parts += [high, (bias - high.astype(f32)).astype(bf16)]
        biases.append(jnp.concatenate(parts, axis=0))
    for b, (window, start, heads) in enumerate(blocks):
        scores[b] = scores[b] + dot(hot_ref[: heads * PAD, : heads * HALF], biases[b])
    for b, (window, start, heads) in enumerate(blocks):
        fill = fill_ref[window * PAD : (window + 1) * PAD]
        fill = jnp.concatenate([fill, fill[:, : PAD - LANES]], axis=1)
        for head in range(heads):
            one = scores[b][head * PAD : (head + 1) * PAD]
            one = jnp.where(fill == 0.0, one, fill)
            weights = jnp.exp(one - jnp.max(one, axis=0, keepdims=True))
            total = jnp.sum(weights, axis=0, keepdims=True)
            p_ref[firsts[b] + head] = (weights * (1.0 / total)).astype(bf16)
    for b, (window, start, heads) in enumerate(blocks):
        lanes, rows = slice(start, start + LANES), slice(window * PAD, (window + 1) * PAD)
        turned = v_ref[rows, lanes].T
        parts = [
            dot(turned[head * HALF : (head + 1) * HALF], p_ref[firsts[b] + head]).astype(bf16) for head in range(heads)
        ]
        if heads == 1:
            parts.append(jnp.zeros_like(parts[0]))
        mix_ref[rows, lanes] = jnp.concatenate(parts, axis=0).T


def attend_backward_unit(
    q_ref, k_ref, v_ref, d_ref, p_ref, dq_ref, dk_ref, dv_ref, table_ref, relt_ref, hott_ref, scr_ref, blocks
):
    places = place_of_lane()
    eighth = jnp.asarray(0.125, bf16)
    firsts, d_attn, d_scores, sums, offsets = [], [], [], [], []
    count = 0
    for window, start, heads in blocks:
        firsts.append(count)
        lanes, rows = slice(start, start + LANES), slice(window * PAD, (window + 1) * PAD)
        d_attn.append(dot(stack_heads(v_ref[rows, lanes], heads), d_ref[rows, lanes], NT))
        count += heads
    for b, (window, start, heads) in enumerate(blocks):
        lanes, rows = slice(start, start + LANES), slice(window * PAD, (window + 1) * PAD)
        soft = p_ref[firsts[b] : firsts[b] + heads].reshape(heads * PAD, PAD)
        dv_ref[rows, lanes] = merge_heads(dot(soft, d_ref[rows, lanes]), heads).astype(bf16)
    for b, (window, start, heads) in enumerate(blocks):
        parts = []
        for head in range(heads):
            soft = p_ref[firsts[b] + head].astype(f32)
            weighted = d_attn[b][head * PAD : (head + 1) * PAD] * soft
            inner = jnp.sum(weighted, axis=0, keepdims=True)
            parts.append((weighted - soft * inner).astype(bf16))
        d_scores.append(parts)
    for b, (window, start, heads) in enumerate(blocks):
        lanes, rows = slice(start, start + LANES), slice(window * PAD, (window + 1) * PAD)
        turned_k = k_ref[rows, lanes].T * eighth
        parts = []
        for head in range(heads):
            left = jnp.concatenate([turned_k[head * HALF : (head + 1) * HALF], hott_ref[...]], axis=0)
            both = dot(left, d_scores[b][head])
            for axis in range(2):
                scr_ref[firsts[b] + head, axis, 16:32, :] = both[HALF + 16 * axis : HALF + 16 * axis + 16]
            parts.append(both[:HALF])
        sums.append(parts)
    for b, (window, start, heads) in enumerate(blocks):
        spread = []
        for head in range(heads):
            for axis in range(2):
                picked = scr_ref[firsts[b] + head, axis, 16:48, :]
                for at in range(WIN - 1):
                    picked = jnp.where(places[axis] == at, scr_ref[firsts[b] + head, axis, 3 + at : 35 + at, :], picked)
                spread.append(picked)
        offsets.append(jnp.concatenate(spread, axis=0).astype(bf16))
    for b, (window, start, heads) in enumerate(blocks):
        lanes, rows = slice(start, start + LANES), slice(window * PAD, (window + 1) * PAD)
        right = dot(jnp.concatenate(d_scores[b] + [offsets[b]], axis=0), q_ref[rows, lanes])
        dk_ref[rows, lanes] = (merge_heads(right[: heads * PAD], heads) * 0.125).astype(bf16)
        table_ref[: heads * HALF] += right[heads * PAD :]
        extra = dot(relt_ref[:, : heads * HALF], offsets[b])
        turned = jnp.concatenate(sums[b] if heads == 2 else sums[b] + [jnp.zeros_like(sums[b][0])], axis=0) + extra
        turned = turned.astype(bf16)
        dq_ref[rows, lanes] = turned.T


class Place:
    def __init__(self, tp, dp):
        self.tp, self.dp = tp, dp
        self.d, self.me = lax.axis_index("dp"), lax.axis_index("tp")
        c, x, y = self.d % 2, (self.d // 2) % 2, (self.d // 4) % 2
        self.c = c
        self.core = self.d + 1 - 2 * c
        peer_x, peer_y = self.d + 2 - 4 * x, self.d + 4 - 8 * y
        self.x, self.y = peer_x, peer_y
        self.first = peer_x * (1 - c) + peer_y * c
        self.second = peer_y * (1 - c) + peer_x * c
        self.bit_one = x * (1 - c) + y * c
        self.bit_two = y * (1 - c) + x * c
        self.extra = []
        for bit in range(3, dp.bit_length() - 1):
            step = 1 << bit
            self.extra.append(self.d + step * (1 - 2 * ((self.d // step) % 2)))

    def flips(self):
        a, b = self.bit_one, self.bit_two
        return [2 * a + b, 2 * (1 - a) + b, 2 * a + 1 - b, 2 * (1 - a) + 1 - b]

    def other(self, step):
        return (self.me + step) % self.tp

    def greet_start(self):
        barrier = pltpu.get_barrier_semaphore()
        for peer in [self.core, self.x, self.y] + self.extra:
            pl.semaphore_signal(barrier, inc=1, device_id=(peer, self.me), device_id_type=MESH)

        def signal(step, carry):
            pl.semaphore_signal(barrier, inc=1, device_id=(self.d, self.other(step)), device_id_type=MESH)
            return carry

        lax.fori_loop(1, self.tp, signal, 0)

    def greet_wait(self):
        pl.semaphore_wait(pltpu.get_barrier_semaphore(), 3 + len(self.extra) + self.tp - 1)


def piece(ref, block, c):
    rows, columns = ref.shape[-2] // 4, ref.shape[-1] // 2
    lead = (slice(None),) * (len(ref.shape) - 2)
    return ref.at[
        lead + (pl.ds(pl.multiple_of(block * rows, rows), rows), pl.ds(pl.multiple_of(c * columns, columns), columns))
    ]


def remote(src, dst, send, recv, device):
    return pltpu.make_async_remote_copy(
        src_ref=src, dst_ref=dst, send_sem=send, recv_sem=recv, device_id=device, device_id_type=MESH
    )


class Spread:
    def __init__(self, place, ref, send, recv, at):
        self.place, self.ref, self.send, self.recv, self.at = place, ref, send, recv, at

    def copy(self, k, arriving):
        place = self.place
        flips = place.flips()
        index = tuple(self.at) + (k,)
        if k == 3:
            columns = self.ref.shape[-1] // 2
            side = 1 - place.c if arriving else place.c
            lead = (slice(None),) * (len(self.ref.shape) - 1)
            view = self.ref.at[lead + (pl.ds(pl.multiple_of(side * columns, columns), columns),)]
            device = place.core
        else:
            device, block, came = (
                (place.first, flips[0], flips[1]) if k == 0 else (place.second, flips[k - 1], flips[k + 1])
            )
            view = piece(self.ref, came if arriving else block, place.c)
        return remote(view, view, self.send.at[index], self.recv.at[index], (device, place.me))

    def start_own(self):
        for k in (0, 1):
            self.copy(k, False).start()

    def after_first(self):
        self.copy(0, True).wait_recv()
        self.copy(2, False).start()

    def after_second(self):
        for k in (1, 2):
            self.copy(k, True).wait_recv()
        self.copy(3, False).start()

    def ready(self):
        self.copy(3, True).wait_recv()

    def sent(self):
        for k in range(4):
            self.copy(k, False).wait_send()


def repeat(count, fn, first=0):
    def step(i, carry):
        fn(i)
        return carry

    lax.fori_loop(first, count, step, 0)


def normal_rows(values):
    centre = jnp.mean(values, axis=-1, keepdims=True)
    centred = values - centre
    scale = lax.rsqrt(jnp.mean(centred * centred, axis=-1, keepdims=True) + 1e-06)
    return centred * scale, scale


def normal_back(gradient, normal, scale, gain):
    e = gradient * gain
    return scale * (
        e - jnp.mean(e, axis=-1, keepdims=True) - normal * jnp.mean(e * normal, axis=-1, keepdims=True)
    )


def block_kernel(tp, dp, names, *refs):
    r = dict(zip(names, refs))
    place = Place(tp, dp)
    me, c, one_bit, two_bit = place.me, place.c, place.bit_one, place.bit_two
    x, cot, fill, vec = r["x"], r["cot"], r["fill"], r["vec"]
    rel, relt = r["rel"], r["relt"]
    a, b, ga = r["a"], r["b"], r["ga"]
    normed, q, k, v, mix = r["normed"], r["q"], r["k"], r["v"], r["mix"]
    middle, total, slide = r["middle"], r["total"], r["slide"]
    normed_two, turned_two, hid, dbs = r["normed_two"], r["turned_two"], r["hid"], r["dbs"]
    early, late, bias = r["early"], r["late"], r["bias"]
    rows_all, width = x.shape
    part = a.shape[2]
    pieces = b.shape[1] // 2
    units = pieces * width
    windows = rows_all // PAD
    half_rows = rows_all // 2
    columns = width // TILE
    tiles = units // TILE
    halves_of_rows = [slice(0, half_rows), slice(half_rows, rows_all)]
    blocks = []
    for window in range(windows // 2):
        for start in range(0, part, LANES):
            blocks.append((window, start, min(2, (part - start) // HALF)))

    weights = [a, b]
    own_copy = [pltpu.make_async_copy(r["own_a"], a.at[me], r["local"].at[0])]
    own_copy.append(pltpu.make_async_copy(r["own_f"], b.at[me, 0:pieces], r["local"].at[1]))
    own_copy.append(pltpu.make_async_copy(r["own_g"], b.at[me, pieces:], r["local"].at[2]))
    own_copy.append(pltpu.make_async_copy(r["x_in"], hid.at[: r["x_in"].shape[0], :width], r["local"].at[3]))
    own_copy.append(pltpu.make_async_copy(r["cot_in"], dbs.at[: r["x_in"].shape[0], :width], r["local"].at[4]))

    def z_copy(w, other, arriving):
        owner = other if arriving else me
        view = piece(weights[w].at[owner], place.flips()[0], c)
        return remote(view, view, r["z_send"].at[w, other], r["z_recv"].at[w, owner], (place.d, other))

    def bias_copy(other, arriving):
        owner = other if arriving else me
        return remote(bias.at[owner], bias.at[owner], r["b_send"].at[other], r["b_recv"].at[owner], (place.d, other))

    def spread(w, s):
        return Spread(place, weights[w].at[s], r["p_send"], r["p_recv"], (w, s))

    def send(w, j):
        z_copy(w, place.other(tp - j), False).start()

    def first(w, j):
        z_copy(w, place.other(j), True).wait_recv()
        spread(w, place.other(j)).start_own()

    def second(w, j):
        spread(w, place.other(j)).after_first()

    def third(w, j):
        spread(w, place.other(j)).after_second()

    def ready(w, j):
        spread(w, place.other(j)).ready()

    def sent(w, j):
        spread(w, place.other(j)).sent()

    def z_sent(w):
        repeat(tp, lambda j: z_copy(w, place.other(j), False).wait_send(), 1)

    grads = [ga, b]
    halves, quarters, eighths, arrived, final = ([r[name + str(w)] for w in range(2)] for name in ("h", "u", "e", "t", "o"))
    outs = [r["out_a"], r["out_b"]]

    def rows_of(block, size):
        return pl.ds(pl.multiple_of(block * size, size), size)

    def lanes_of(w, side):
        count = grads[w].shape[-1] // 2
        return pl.ds(pl.multiple_of(side * count, count), count)

    def core_copy(w, s):
        return remote(
            grads[w].at[s, :, :, lanes_of(w, 1 - c)],
            halves[w].at[s],
            r["core_send"].at[w, s],
            r["core_recv"].at[w, s],
            (place.core, me),
        )

    def quarter_copy(w, s):
        size = quarters[w].shape[2]
        return remote(
            halves[w].at[s, :, rows_of(1 - one_bit, size)],
            quarters[w].at[s],
            r["one_send"].at[w, s],
            r["one_recv"].at[w, s],
            (place.first, me),
        )

    def eighth_copy(w, s):
        size = eighths[w].shape[2]
        return remote(
            quarters[w].at[s, :, rows_of(1 - two_bit, size)],
            eighths[w].at[s],
            r["two_send"].at[w, s],
            r["two_recv"].at[w, s],
            (place.second, me),
        )

    def shard_copy(w, other, arriving):
        owner = other if arriving else me
        return remote(
            eighths[w].at[other], arrived[w].at[owner], r["s_send"].at[w, other], r["s_recv"].at[w, owner], (place.d, other)
        )

    def reduce_one(w, s):
        core_copy(w, s).start()

    def reduce_two(w, s):
        core_copy(w, s).wait_recv()
        size = quarters[w].shape[2]

        def add(block):
            rows = rows_of(block, size)
            halves[w][s, :, rows] += grads[w][s, :, rows, lanes_of(w, c)]

        add(1 - one_bit)
        quarter_copy(w, s).start()
        add(one_bit)

    def reduce_three(w, s):
        size = eighths[w].shape[2]
        quarter_copy(w, s).wait_recv()

        def add(two):
            rows = rows_of(two, size)
            quarters[w][s, :, rows] += halves[w][s, :, rows_of(2 * one_bit + two, size)]

        add(1 - two_bit)
        eighth_copy(w, s).start()
        add(two_bit)

    def reduce_four(w, j):
        s = place.other(j)
        eighth_copy(w, s).wait_recv()
        eighths[w][s] += quarters[w][s, :, rows_of(two_bit, eighths[w].shape[2])]
        if j > 0:
            shard_copy(w, s, False).start()

    def out_spread(w):
        return Spread(place, outs[w], r["q_send"], r["q_recv"], (w,))

    def reduce_five(w):
        repeat(tp, lambda j: shard_copy(w, place.other(j), True).wait_recv(), 1)
        arrived[w][me] = eighths[w][me]
        value = arrived[w][0].astype(f32)
        for s in range(1, tp):
            value += arrived[w][s].astype(f32)
        final[w][...] = value.astype(bf16)
        for i, peer in enumerate(place.extra):
            copy = remote(final[w], r["x" + str(w)].at[i], r["x_send"].at[w, i], r["x_recv"].at[w, i], (peer, me))
            copy.start()
            copy.wait()
            final[w][...] += r["x" + str(w)][i]
        put = pltpu.make_async_copy(final[w], piece(outs[w], place.flips()[0], c), r["put"].at[w])
        put.start()
        put.wait()
        out_spread(w).start_own()

    def reduce_done(w):
        out_spread(w).ready()
        out_spread(w).sent()

        def one(j):
            s = place.other(j)
            core_copy(w, s).wait_send()
            quarter_copy(w, s).wait_send()
            eighth_copy(w, s).wait_send()

        repeat(tp, one)
        repeat(tp, lambda j: shard_copy(w, place.other(j), False).wait_send(), 1)

    levels = [place.core, place.x, place.y] + place.extra
    table = r["table"]
    small = [[r["early"]], [r["late"], r["fold"]]]
    small_in = [[r["early_in"]], [r["late_in"], r["fold_in"]]]
    small_z = [[r["early_z"]], [r["late_z"], r["fold_z"]]]
    small_out = [[r["early_out"]], [r["late_out"], r["fold_out"]]]

    def small_copy(group, i, level):
        at = group + i
        return remote(
            small[group][i],
            small_in[group][i].at[level],
            r["v_send"].at[at, level],
            r["v_recv"].at[at, level],
            (levels[level], me),
        )

    def small_start(group):
        for i in range(len(small[group])):
            small_copy(group, i, 0).start()

    def small_level(group, level):
        for i in range(len(small[group])):
            small_copy(group, i, level).wait()
            small[group][i][...] += small_in[group][i][level]
            if level + 1 < len(levels):
                small_copy(group, i, level + 1).start()

    def small_shard(group, i, other, arriving):
        owner = other if arriving else me
        at = group + i
        return remote(
            small[group][i], small_z[group][i].at[owner], r["vz_send"].at[at, other], r["vz_recv"].at[at, owner], (place.d, other)
        )

    def small_across(group):
        for level in range(2, len(levels)):
            small_level(group, level)
        for i in range(len(small[group])):
            repeat(tp, lambda j: small_shard(group, i, place.other(j), False).start(), 1)

    def small_finish(group):
        for i in range(len(small[group])):
            repeat(tp, lambda j: small_shard(group, i, place.other(j), True).wait_recv(), 1)
            landed = small_z[group][i]
            landed[me] = small[group][i][...]
            value = landed[0]
            for s in range(1, tp):
                value += landed[s]
            small_out[group][i][...] = value

    def small_sent():
        for group in range(2):
            for i in range(len(small[group])):
                repeat(tp, lambda j: small_shard(group, i, place.other(j), False).wait_send(), 1)

    def chunk(i):
        return pl.ds(pl.multiple_of(i * CHUNK, CHUNK), CHUNK)

    chunks = rows_all // CHUNK

    def keep_rows(rows, count):
        keep = (fill[rows] == 0.0).astype(f32)
        return jnp.concatenate([keep] * (count // LANES), axis=1)

    def fill_rows(i):
        row = i * CHUNK + lax.broadcasted_iota(jnp.int32, (CHUNK, LANES), 0)
        window = sum((row >= PAD * at).astype(jnp.int32) for at in range(1, windows))
        inside = row - PAD * window
        down = (inside * 4682) >> 16
        across = inside - WIN * down
        window = me * windows + window
        lower = window // GRID if GRID & (GRID - 1) else window >> (GRID.bit_length() - 1)
        kept = (lower * WIN + down < r["heights"][0]) & ((window - lower * GRID) * WIN + across < r["widths"][0])
        value = jnp.where(kept, 0.0, neg_fill)
        fill[chunk(i)] = jnp.where(inside < SLOTS, value, pad_fill).astype(f32)

    def norm_one(i):
        rows = chunk(i)
        normal, _ = normal_rows(x[rows].astype(f32))
        normed[rows] = (normal * vec[0:1] + vec[2:3]).astype(bf16)

    def project(s):
        for t, target in enumerate((q, k, v)):
            for rows in halves_of_rows:
                value = dot(normed[rows], a[s, t], NT)
                if t != 1:
                    value = value + bias[s, t // 2 : 1 + t // 2, :part]
                target[s, rows, :part] = value.astype(bf16)

    def unit_view(ref, s, at):
        return ref.at[s, pl.ds(pl.multiple_of(at * half_rows, half_rows), half_rows)]

    def p_out(i):
        return pltpu.make_async_copy(r["p"].at[i % 2], r["p_hbm"].at[i], r["p_sem"].at[i % 2])

    def p_in(i):
        return pltpu.make_async_copy(r["p_hbm"].at[i], r["p"].at[i % 2], r["p_sem"].at[i % 2])

    def attend(i, s, at):
        attend_forward_unit(
            unit_view(q, s, at),
            unit_view(k, s, at),
            unit_view(v, s, at),
            unit_view(mix, s, at),
            r["p"].at[i % 2],
            fill.at[pl.ds(pl.multiple_of(at * half_rows, half_rows), half_rows)],
            rel,
            r["hot"],
            r["scr_a"],
            blocks,
        )

    def attend_back(i, s, at):
        views = [unit_view(ref, s, at) for ref in (q, k, v)]
        attend_backward_unit(
            *views, unit_view(mix, s, at), r["p"].at[i % 2], *views, table, relt, r["hott"], r["scr_b"], blocks
        )

    def mix_out(n):
        tile = pl.ds(pl.multiple_of(n * TILE, TILE), TILE)
        for rows in halves_of_rows:
            value = dot(mix[0, rows, :part], a[0, 3, :, tile])
            for s in range(1, tp):
                value = value + dot(mix[s, rows, :part], a[s, 3, :, tile])
            middle[rows, tile] = x[rows, tile].astype(f32) + keep_rows(rows, TILE) * (value + vec[4:5, tile])

    def norm_two(i):
        rows = chunk(i)
        value = middle[rows]
        normal, _ = normal_rows(value)
        normed_two[rows] = (normal * vec[1:2] + vec[3:4]).astype(bf16)
        total[rows] = value + keep_rows(rows, width) * vec[5:6]
        slide[rows] = jnp.zeros_like(value)

    def tile_of(n):
        inner = n if pieces == 1 else n % columns
        block = 0 if pieces == 1 else n // columns
        return pl.ds(pl.multiple_of(n * TILE, TILE), TILE), block, pl.ds(pl.multiple_of(inner * TILE, TILE), TILE)

    def layers(s, j):
        def one(n):
            run("layers", j * tiles + n)
            tile, block, inner = tile_of(n)
            column = None
            for rows in halves_of_rows:
                before = dot(normed_two[rows], b[s, block, :, inner]) + bias[s, pl.ds(2 + block, 1), inner]
                keep = keep_rows(rows, TILE)
                phi = 0.5 * (1.0 + lax.erf(before * root_half))
                hid[rows, tile] = (before * phi * keep).astype(bf16)
                slope = phi + before * (jnp.exp(-0.5 * before * before) * bell)
                down = (slope * (dot(cot[rows], b[s, pieces + block, inner, :], NT) * keep)).astype(bf16)
                dbs[rows, tile] = down
                part_sum = jnp.sum(down.astype(f32), axis=0, keepdims=True)
                column = part_sum if column is None else column + part_sum
            early[pl.ds(4 + s * pieces + block, 1), inner] = column

        repeat(tiles, one)

    def layers_add(s, j):
        def one(n):
            run("add", j * columns + n)
            tile = pl.ds(pl.multiple_of(n * TILE, TILE), TILE)
            for rows in halves_of_rows:
                for i in range(pieces):
                    part_of = slice(i * width, (i + 1) * width)
                    total[rows, tile] += dot(hid[rows, part_of], b[s, pieces + i, :, tile])
                    slide[rows, tile] += dot(dbs[rows, part_of], b[s, i, tile, :], NT)

        repeat(columns, one)

    def layers_grad(s, j):
        def one(n):
            run("grad", j * tiles + n)
            tile, block, inner = tile_of(n)
            b[s, pieces + block, inner, :] = dot(hid[:, tile], cot[...], TN).astype(bf16)
            b[s, block, :, inner] = dot(turned_two[...], dbs[:, tile]).astype(bf16)

        repeat(tiles, one)

    def middle_back(i):
        rows = chunk(i)
        hid[rows, :width] = total[rows].astype(bf16)
        keep = keep_rows(rows, width)
        gradient = slide[rows]
        normal, scale = normal_rows(middle[rows])
        outer = cot[rows].astype(f32)
        down = outer + normal_back(gradient, normal, scale, vec[1:2])
        slide[rows] = down
        masked = down * keep
        dbs[rows, :width] = masked.astype(bf16)
        total[rows] = jnp.zeros_like(down)
        for at, value in enumerate((gradient * normal, gradient, masked, outer * keep)):
            early[at : at + 1] = early[at : at + 1] + jnp.sum(value, axis=0, keepdims=True)

    def mix_back(s):
        ga[s, 3] = dot(mix[s, :, :part], dbs[:, :width], TN).astype(bf16)
        for rows in halves_of_rows:
            mix[s, rows, :part] = dot(dbs[rows, :width], a[s, 3], NT).astype(bf16)

    def project_back(s):
        for t, source in enumerate((q, k, v)):
            ga[s, t] = dot(source[s, :, :part], normed[...], TN).astype(bf16)
        for i, source in ((0, q), (1, v)):
            value = jnp.sum(source[s, :, :part].astype(f32), axis=0, keepdims=True)
            first_lane = i * (width // 2)
            late[pl.ds(2 + s, 1), first_lane : first_lane + part] = value

        def one(n):
            tile = pl.ds(pl.multiple_of(n * TILE, TILE), TILE)
            for rows in halves_of_rows:
                total[rows, tile] += (
                    dot(q[s, rows, :part], a[s, 0, :, tile])
                    + dot(k[s, rows, :part], a[s, 1, :, tile])
                    + dot(v[s, rows, :part], a[s, 2, :, tile])
                )

        repeat(columns, one)

    def input_back(i):
        rows = chunk(i)
        gradient = total[rows]
        normal, scale = normal_rows(x[rows].astype(f32))
        middle[rows] = slide[rows] + normal_back(gradient, normal, scale, vec[0:1])
        late[0:1] = late[0:1] + jnp.sum(gradient * normal, axis=0, keepdims=True)
        late[1:2] = late[1:2] + jnp.sum(gradient, axis=0, keepdims=True)

    plan = make_plan(tp, tiles, columns)

    def run(name, index=0):
        for at, steps in sorted(plan.get(name, {}).items()):

            @pl.when(index == at)
            def _(steps=steps):
                for fn, *args in steps:
                    do[fn](*args)

    def bias_ready():
        repeat(tp, lambda j: bias_copy(place.other(j), True).wait_recv(), 1)

    do = dict(
        send=send,
        first=first,
        second=second,
        third=third,
        ready=ready,
        sent=sent,
        bias_ready=bias_ready,
        one=lambda w, j: reduce_one(w, place.other(j)),
        two=lambda w, j: reduce_two(w, place.other(j)),
        three=lambda w, j: reduce_three(w, place.other(j)),
        four=reduce_four,
        z_sent=z_sent,
        five=reduce_five,
        after_first=lambda w: out_spread(w).after_first(),
        after_second=lambda w: out_spread(w).after_second(),
        s0=small_start,
        s1=lambda group: small_level(group, 0),
        s2=lambda group: small_level(group, 1),
        s3=small_across,
        s4=small_finish,
        done=reduce_done,
    )

    place.greet_start()
    for copy in own_copy:
        copy.start()
    bias[me] = vec[8:16]
    for copy in own_copy:
        copy.wait()
    place.greet_wait()
    run("start")
    repeat(tp, lambda j: bias_copy(place.other(tp - j), False).start(), 1)
    slots = r["x_in"].shape[0] // windows
    for window in range(windows):
        for staged, target in ((hid, x), (dbs, cot)):
            target[window * PAD : window * PAD + slots] = staged[window * slots : (window + 1) * slots, :width]
            target[window * PAD + slots : (window + 1) * PAD] = jnp.zeros((PAD - slots, width), bf16)
    repeat(chunks, norm_one)
    repeat(chunks, fill_rows)
    picked = dot(r["pick"][...], r["offsets"][...])
    lane = lax.broadcasted_iota(jnp.int32, picked.shape, 1)
    head = lax.broadcasted_iota(jnp.int32, picked.shape, 0)
    picked = jnp.where((lane < HALF) == (head < HALF), picked, 0.0)
    rel[...] = picked.astype(bf16)
    relt[...] = (picked * 0.125).T.astype(bf16)
    lead = part - part % LANES
    if lead < part:
        for ref in (q, k, v, mix):
            for s in range(tp):
                ref[s, :, lead:] = jnp.zeros((rows_all, LANES), bf16)
    for ref in (early, late, table, r["scr_b"]):
        ref[...] = jnp.zeros_like(ref)

    def forward_unit(i):
        j, at = i // 2, i % 2
        s = place.other(j)

        @pl.when(at == 0)
        def _():
            run("project", j)
            project(s)

        run("unit", i)

        @pl.when(i >= 2)
        def _():
            p_out(i - 2).wait()

        attend(i, s, at)
        p_out(i).start()

    unit_count = 2 * tp
    repeat(unit_count, forward_unit)
    run("mid")
    p_out(unit_count - 2).wait()
    p_out(unit_count - 1).wait()
    repeat(columns, mix_out)
    run("mid1")
    repeat(chunks, norm_two)
    turned_two[...] = normed_two[...].T

    def layer_step(j):
        s = place.other(j)
        layers(s, j)
        layers_add(s, j)
        layers_grad(s, j)
        run("layer3", j)

    repeat(tp, layer_step)

    run("down0")
    repeat(chunks, middle_back)
    for window in range(windows):
        normed_two[window * slots : (window + 1) * slots] = hid[window * PAD : window * PAD + slots, :width]
    put_out = pltpu.make_async_copy(normed_two.at[: windows * slots], r["out"], r["local"].at[1])
    put_out.start()
    run("down1")
    p_in(0).start()
    repeat(tp, lambda j: mix_back(place.other(j)))
    run("down2")

    def backward_unit(i):
        j, at = i // 2, i % 2
        s = place.other(j)
        run("back", i)

        @pl.when(i + 1 < unit_count)
        def _():
            p_in(i + 1).start()

        p_in(i).wait()
        attend_back(i, s, at)

        @pl.when(at == 1)
        def _():
            run("turn", j)
            project_back(s)
            run("shard", j)

    repeat(unit_count, backward_unit)
    for at in range(4):
        run("end" + str(at))
        repeat(chunks * (at + 1) // 4, input_back, chunks * at // 4)
    for window in range(windows):
        total[window * slots : (window + 1) * slots] = middle[window * PAD : window * PAD + slots]
    put_in = pltpu.make_async_copy(total.at[: windows * slots], r["grad_x"], r["local"].at[2])
    put_in.start()
    r["fold"][:, :HALF] = table[:32, :HALF] + table[HALF : HALF + 32, HALF:]
    r["fold"][:, HALF:] = table[32:HALF, :HALF] + table[HALF + 32 :, HALF:]
    for at in range(4, ENDS):
        run("end" + str(at))
    for j in range(1, tp):
        sent(0, j)
    z_sent(0)
    small_sent()
    repeat(tp, lambda j: bias_copy(place.other(tp - j), False).wait_send(), 1)
    put_out.wait()
    put_in.wait()


def make_plan(tp, tiles, columns):
    plan = {}
    if PLACES and (tp, tiles, columns) == (4, 3, 3):
        for place, index, *steps in PLACES:
            plan.setdefault(place, {})[index] = steps
        return plan

    def at(place, index, *step):
        if place in ("layer0", "layer1", "layer2"):
            place, count = dict(layer0=("layers", tiles), layer1=("add", columns), layer2=("grad", tiles))[place]
            index *= count
        plan.setdefault(place, {}).setdefault(index, []).append(step)

    others = list(range(1, tp))
    arrivals = [(w, j) for w in (0, 1) for j in others]
    order = [("unit", 1)]
    for j in others:
        order += [("project", j), ("unit", 2 * j), ("unit", 2 * j + 1)]
    order.append(("mid", 0))
    order += [("layer" + str(stage), j) for j in range(tp) for stage in range(4)]
    slots = len(arrivals) + 2
    own_end = order.index(("layer3", 0))
    marks = [s * own_end // (slots - 1) for s in range(slots)]
    need = {0: "project", 1: "layer0"}
    limit = len(order) - 1
    for slot in reversed(range(slots)):
        if slot >= 2:
            w, j = arrivals[slot - 2]
            limit = min(limit, order.index((need[w], j)))
        limit = min(limit, marks[slot])
        marks = marks[:slot] + [limit] + marks[slot + 1 :]
    for ahead in range(min(2, len(arrivals))):
        at("start", 0, "send", *arrivals[ahead])
    for slot in range(slots):
        for name, behind in (("third", 2), ("second", 1), ("first", 0)):
            if 0 <= slot - behind < len(arrivals):
                at(*order[marks[slot]], name, *arrivals[slot - behind])
        if slot + 2 < len(arrivals):
            at(*order[marks[slot]], "send", *arrivals[slot + 2])
    if tp > 1:
        at("project", 1, "bias_ready")
        at("layer2", 0, "z_sent", 1)
    for j in others:
        at("project", j, "ready", 0, j)
        at("layer0", j, "ready", 1, j)
        at("layer2", j, "sent", 1, j)

    last = tp - 1
    for j in range(tp):
        at("layer3", j, "one", 1, j)
    for j in range(tp):
        at(*(("layer1", j + 1) if j < last else ("down1", 0)), "two", 1, j)
    for j in range(tp):
        at(*(("layer1", j + 2) if j + 2 <= last else ("down1", 0) if j < last else ("shard", 0)), "three", 1, j)
    for j in range(tp):
        where = ("layer1", j + 3) if j + 3 <= last else ("down1", 0) if j + 2 <= last else ("back", 1) if j < last else ("turn", min(1, last))
        at(*where, "four", 1, j)
    late = lambda n: ("shard", n) if n <= last else ("end0", 0)
    at(*late(1), "five", 1)
    at(*late(2), "after_first", 1)
    at(*late(3), "after_second", 1)

    for j in range(tp):
        at("shard", j, "one", 0, j)
    for j in range(tp):
        at(*(("back", 2 * j + 3) if j < last else ("end4", 0)), "two", 0, j)
    for j in range(tp):
        at(*(("shard", j + 1) if j < last else ("end6", 0)), "three", 0, j)
    for j in range(tp):
        at(*(("back", 2 * j + 5) if j + 2 <= last else ("end0", 0) if j < last else ("end7", 0)), "four", 0, j)
    for group, places in enumerate((("down2", "end0", "end1", "end2", "end3"), ("end4", "end5", "end6", "end7", "end8"))):
        for step, place in enumerate(places):
            at(place, 0, "s" + str(step), group)
    at("end9", 0, "five", 0)
    at("end9", 0, "after_first", 0)
    at("end10", 0, "after_second", 0)
    at("end11", 0, "done", 1)
    at("end11", 0, "done", 0)
    return plan


def whole_block(tp, dp, x, cot, heights, widths, vec, own_a, own_f, own_g, offsets):
    width = x.shape[1]
    windows = x.shape[0] // SLOTS
    rows = windows * PAD
    part = own_a.shape[1]
    pieces = own_f.shape[0]
    units = pieces * width
    heads = (windows // 2) * (part // HEAD_DIM)
    wide = -(-part // LANES) * LANES
    unit_count = 2 * tp
    hot, hott, pick = window_constants()
    scalar = pl.BlockSpec(memory_space=pltpu.SMEM)
    any_space = pl.BlockSpec(memory_space=pl.ANY)
    vmem = pl.BlockSpec(memory_space=pltpu.VMEM)
    dma = pltpu.SemaphoreType.DMA
    inputs = [
        ("x_in", x, any_space),
        ("cot_in", cot, any_space),
        ("heights", heights, scalar),
        ("widths", widths, scalar),
        ("vec", vec, vmem),
        ("own_a", own_a, any_space),
        ("own_f", own_f, any_space),
        ("own_g", own_g, any_space),
        ("offsets", offsets, vmem),
        ("hot", hot, vmem),
        ("hott", hott, vmem),
        ("pick", pick, vmem),
    ]
    shape = jax.ShapeDtypeStruct
    outputs = [
        ("out", shape(x.shape, bf16), any_space),
        ("grad_x", shape(x.shape, f32), any_space),
        ("out_a", shape(own_a.shape, bf16), any_space),
        ("out_b", shape((2 * pieces, width, width), bf16), any_space),
        ("early_out", shape((8, width), f32), vmem),
        ("late_out", shape((8, width), f32), vmem),
        ("fold_out", shape((32, LANES), f32), vmem),
        ("p_hbm", shape((unit_count, heads, PAD, PAD), bf16), any_space),
    ]
    buffer = lambda dims, kind: pltpu.VMEM(tuple(dims), kind)
    scratch = [
        ("a", buffer((tp,) + own_a.shape, bf16)),
        ("b", buffer((tp, 2 * pieces, width, width), bf16)),
        ("ga", buffer((tp,) + own_a.shape, bf16)),
        ("bias", buffer((tp, 8, width), f32)),
        ("x", buffer((rows, width), bf16)),
        ("cot", buffer((rows, width), bf16)),
        ("fill", buffer((rows, LANES), f32)),
        ("rel", buffer((LANES, LANES), bf16)),
        ("relt", buffer((LANES, LANES), bf16)),
        ("normed", buffer((rows, width), bf16)),
    ]
    scratch += [(name, buffer((tp, rows, wide), bf16)) for name in ("q", "k", "v", "mix")]
    scratch += [("p", buffer((2, heads, PAD, PAD), bf16))]
    scratch += [(name, buffer((rows, width), f32)) for name in ("middle", "total", "slide")]
    scratch += [("normed_two", buffer((rows, width), bf16)), ("turned_two", buffer((width, rows), bf16))]
    scratch += [(name, buffer((rows, units), bf16)) for name in ("hid", "dbs")]
    scratch += [
        ("early", buffer((8, width), f32)),
        ("late", buffer((8, width), f32)),
        ("table", buffer((LANES, LANES), f32)),
        ("fold", buffer((32, LANES), f32)),
        ("scr_a", buffer((heads, HALF, PAD), f32)),
        ("scr_b", buffer((heads, 2, 48, PAD), f32)),
    ]
    levels = dp.bit_length() - 1
    more = levels - 3
    for w, own in enumerate((own_a.shape, (2 * pieces, width, width))):
        n, count, lanes = own[0], own[1], own[2] // 2
        scratch += [
            ("h" + str(w), buffer((tp, n, count, lanes), bf16)),
            ("u" + str(w), buffer((tp, n, count // 2, lanes), bf16)),
            ("e" + str(w), buffer((tp, n, count // 4, lanes), bf16)),
            ("t" + str(w), buffer((tp, n, count // 4, lanes), bf16)),
            ("o" + str(w), buffer((n, count // 4, lanes), bf16)),
        ]
        if more:
            scratch += [("x" + str(w), buffer((more, n, count // 4, lanes), bf16))]
    for name, dims in (("early", (8, width)), ("late", (8, width)), ("fold", (32, LANES))):
        scratch += [(name + "_in", buffer((levels,) + dims, f32)), (name + "_z", buffer((tp,) + dims, f32))]
    semaphores = dict(local=(5,), p_sem=(2,), put=(2,))
    for name, dims in dict(
        z=(2, tp), p=(2, tp, 4), b=(tp,), core=(2, tp), one=(2, tp), two=(2, tp), s=(2, tp), q=(2, 4), x=(2, max(more, 1)), v=(3, levels), vz=(3, tp)
    ).items():
        semaphores[name + "_send"] = semaphores[name + "_recv"] = dims
    scratch += [(name, dma(dims)) for name, dims in semaphores.items()]
    names = [entry[0] for entry in inputs + outputs + scratch]
    return pl.pallas_call(
        lambda *refs: block_kernel(tp, dp, names, *refs),
        in_specs=[entry[2] for entry in inputs],
        out_specs=[entry[2] for entry in outputs],
        out_shape=[entry[1] for entry in outputs],
        scratch_shapes=[entry[1] for entry in scratch],
        compiler_params=pltpu.CompilerParams(collective_id=1, has_side_effects=True, vmem_limit_bytes=VMEM_LIMIT),
    )(*[entry[1] for entry in inputs])


def body(
    tokens,
    heights,
    widths,
    norm_gain,
    norm_bias,
    w_qkv,
    b_qv,
    rel_pos,
    w_proj,
    b_proj,
    w_fc1,
    b_fc1,
    w_fc2,
    b_fc2,
    cotangent,
):
    tp, dp = lax.axis_size("tp"), lax.axis_size("dp")
    width = tokens.shape[1]
    part, units = w_qkv.shape[2], w_fc1.shape[1]
    blocks = units // width
    pad = lambda values, rows, lanes=0: jnp.pad(values, ((0, rows), (0, lanes)))
    vec = [norm_gain, norm_bias, b_proj[None], pad(b_fc2[None], 2), pad(b_qv, 0, width - part)]
    vec = jnp.concatenate(vec + [pad(b_fc1.reshape(blocks, width), 6 - blocks)]).astype(f32)
    offsets = jnp.pad(rel_pos, ((0, 0), (0, 32 - rel_pos.shape[1]), (0, 0))).reshape(HALF, HEAD_DIM)
    offsets = jnp.concatenate([offsets, offsets], axis=1)
    turned = jnp.concatenate([w_qkv.transpose(0, 2, 1), w_proj[None]], axis=0)
    first = w_fc1[None] if blocks == 1 else w_fc1.reshape(width, blocks, width).transpose(1, 0, 2)
    out, grad_x, out_a, out_b, early, late, fold, _ = whole_block(
        tp, dp, tokens, cotangent, heights, widths, vec, turned, first, w_fc2.reshape(blocks, width, width), offsets
    )
    me = lax.axis_index("tp")
    count = 2 * WIN - 1
    grad_rel = jnp.stack([fold[:count, :HALF], fold[:count, HALF:]])[:, ::-1, :]
    mine = lax.dynamic_slice_in_dim(late, 2 + me, 1, 0)
    return (
        out,
        grad_x,
        jnp.stack([late[0], early[0]]),
        jnp.stack([late[1], early[1]]),
        out_a[:3].transpose(0, 2, 1).astype(f32),
        jnp.concatenate([mine[:, :part], mine[:, width // 2 : width // 2 + part]]),
        grad_rel,
        out_a[3].astype(f32),
        early[2],
        out_b[:blocks].transpose(1, 0, 2).reshape(width, units).astype(f32),
        lax.dynamic_slice_in_dim(early, 4 + me * blocks, blocks, 0).reshape(-1),
        out_b[blocks:].reshape(units, width).astype(f32),
        early[3],
    )


def solution(mesh):
    rows = P(("dp", "tp"), None)
    return jax.shard_map(
        body,
        mesh=mesh,
        in_specs=(
            rows,
            P("dp"),
            P("dp"),
            P(),
            P(),
            P(None, None, "tp"),
            P(None, "tp"),
            P(),
            P("tp", None),
            P(),
            P(None, "tp"),
            P("tp"),
            P("tp", None),
            P(),
            rows,
        ),
        out_specs=(
            rows,
            rows,
            P(),
            P(),
            P(None, None, "tp"),
            P(None, "tp"),
            P(),
            P("tp", None),
            P(),
            P(None, "tp"),
            P("tp"),
            P("tp", None),
            P(),
        ),
        check_vma=False,
    )
```

time: 266 us -> 200 us (0.75)
  Pallas kernels: 230 us -> 175 us
  local copies, waits for them, and re-layouts: 20.1 us -> 10.3 us
    pallas_call x1, Pallas kernels: 230 us -> 175 us  [whole_block(): pl.pallas_call(lambda *refs: block_kernel(tp, dp, names, *refs), in_specs...]
    slice x5 -> x1, local copies, waits for them, and re-layouts: 5.22 us -> 1.67 us  [body(): early[3]]
where the time goes in v3:
time: 200 us
  Pallas kernels  175 us (88%)
  other arithmetic  12.5 us (6%)
  local copies, waits for them, and re-layouts  10.3 us (5%)
    pallas_call x1, Pallas kernels, whole_block(): pl.pallas_call(lambda *refs: block_kernel(tp, dp, names, *refs), in_specs...  175 us
    unnamed x14, local copies, waits for them, and re-layouts  4.19 us

profile of v3, /device:TPU:0, one launch (start us, length us, event | category | flops | bytes accessed | tf_op | source)
XLA Modules:
  0.0 199.7 jit_solution(4564363135131611393)
XLA Ops:
  1.9 0.7 broadcast_in_dim.12
  2.6 0.7 broadcast_in_dim.13
  3.3 0.7 pad.17
  4.0 0.7 reshape.45
  4.7 0.8 concatenate.12
  5.5 0.0 copy-start.4
  5.5 0.6 convert_element_type.35.refs_4_
  6.1 2.4 %pad_maximum_fusion.refs_5_ = bf16[4,192,768]{2,1,0:T(8,128)(2,1)} fusion(bf16[1,192,768]{2,1,0:T(8,128)(2,1)} %bitcast.23, bf16[3,192,768]{2,1,0:T(8,128)(2,1)} %bitcast.22), kind=kLoop, calls=%fused_computation.1 | loop fusion | flops 589824 | bytes 2359296 | tf_op jit(solution)/shard_map/concatenate | solution.py:1118
  8.5 0.0 copy-done.4
  8.5 0.7 pad_maximum_fusion.2.refs_8_
  9.2 174.9 %shard_map.273 = (bf16[784,768]{1,0:T(8,128)(2,1)}, f32[784,768]{1,0:T(8,128)}, bf16[4,192,768]{2,1,0:T(8,128)(2,1)}, bf16[2,768,768]{2,1,0:T(8,128)(2,1)}, f32[...) custom-call(bf16[784,768]{1,0:T(8,128)(2,1)} %refs_0_.1, ...), custom_call_target="tpu_custom_call" | custom-call | tf_op jit(solution)/shard_map/pallas_call | solution.py:1082
  184.1 1.7 slice_reduce_fusion
  185.8 0.6 pad_maximum_fusion.3
  186.4 0.6 pad_maximum_fusion.4
  187.0 0.0 copy-start.3
  187.0 0.0 copy-start.1
  187.0 2.7 %convert_bitcast_fusion = f32[3,768,192]{1,2,0:T(8,128)} fusion(bf16[4,192,768]{2,1,0:T(8,128)(2,1)} %get-tuple-element.24), kind=kLoop, calls=%fused_computation | loop fusion | flops 442368 | bytes 2654208 | tf_op jit(solution)/shard_map/convert_element_type | solution.py:1132
  189.7 0.8 constant_dynamic-slice_fusion
  190.5 0.6 pad_maximum_fusion.5
  191.0 0.0 copy-done.3
  191.0 0.1 slice_bitcast_fusion.1
  191.2 0.6 copy.32
  191.8 1.8 bitcast_convert_fusion.2
  193.6 0.0 copy-done.1
  193.6 0.0 copy-start.2
  193.6 2.5 %bitcast_convert_fusion = (f32[768,768]{1,0:T(8,128)}, f32[768,768]{1,0:T(8,128)}) fusion(bf16[2,768,768]{2,1,0:T(8,128)(2,1)S(1)} %copy-done.1), kind=kLoop, calls=%fused_computation.2 | loop fusion | flops 1179648 | bytes 7077888 | tf_op jit(solution)/shard_map/convert_element_type | solution.py:1139
  196.2 0.0 copy-done.2
  196.2 0.0 copy-start
  196.2 1.0 copy.38
  197.2 1.1 copy-done
  198.3 1.4 copy.39
  (6 shorter events, 0.1 us)
Async XLA Ops:
  5.5 3.0 %copy-start.4 = (bf16[2,27,64]{2,0,1:T(2,128)(2,1)S(1)}, bf16[2,27,64]{2,0,1:T(2,128)(2,1)}, u32[]{:S(2)}) copy-start(bf16[2,27,64]{2,0,1:T(2,128)(2,1)} %param.25) | copy-start | bytes 20740
  187.0 4.1 %copy-start.3 = (f32[32,128]{1,0:T(8,128)S(1)}, f32[32,128]{1,0:T(8,128)}, u32[]{:S(2)}) copy-start(f32[32,128]{1,0:T(8,128)} %get-tuple-element.25) | copy-start | bytes 49156
  187.0 6.6 %copy-start.1 = (bf16[2,768,768]{2,1,0:T(8,128)(2,1)S(1)}, bf16[2,768,768]{2,1,0:T(8,128)(2,1)}, u32[]{:S(2)}) copy-start(bf16[2,768,768]{2,1,0:T(8,128)(2,1)} %get-tuple-element.26) | copy-start | bytes 7077892
  193.6 2.5 %copy-start.2 = (bf16[784,768]{1,0:T(8,128)(2,1)S(1)}, bf16[784,768]{1,0:T(8,128)(2,1)}, u32[]{:S(2)}) copy-start(bf16[784,768]{1,0:T(8,128)(2,1)} %get-tuple-element.68) | copy-start | bytes 3612676
  196.2 2.1 %copy-start = (f32[784,768]{1,0:T(8,128)S(1)}, f32[784,768]{1,0:T(8,128)}, u32[]{:S(2)}) copy-start(f32[784,768]{1,0:T(8,128)} %get-tuple-element.69) | copy-start | bytes 7225348

commit v4 on v3

--- a/solution.py
+++ b/solution.py
@@ -15,59 +15,53 @@
 LANES = 128
 HALF = 64
 CHUNK = 64
-ENDS = 16
+ENDS = 20
 PLACES = [
-    ("start", 0, ("send", 0, 1), ("send", 0, 2), ("first", 0, 1), ("send", 0, 3)),
-    ("project", 0, ("second", 0, 1), ("send", 1, 1)),
-    ("unit", 0, ("first", 0, 2), ("third", 0, 1), ("first", 0, 3)),
-    ("unit", 1, ("ready", 0, 1), ("send", 1, 3)),
-    ("project", 1, ("bias_ready",), ("second", 0, 2)),
-    ("unit", 2, ("second", 0, 3)),
-    ("unit", 3, ("third", 0, 2), ("first", 1, 1)),
-    ("project", 2, ("send", 1, 2), ("ready", 0, 2), ("third", 0, 3)),
-    ("unit", 5, ("ready", 0, 3), ("first", 1, 3)),
+    ("start", 0, ("send", 0, 1)),
+    ("warm", 0, ("send", 0, 2), ("first", 0, 1), ("send", 0, 3), ("second", 0, 1)),
+    ("warm", 1, ("send", 1, 1), ("first", 0, 2)),
+    ("project", 0, ("first", 0, 3)),
+    ("unit", 0, ("send", 1, 3), ("third", 0, 1)),
+    ("project", 1, ("bias_ready",), ("ready", 0, 1), ("second", 0, 2)),
+    ("unit", 3, ("second", 0, 3), ("third", 0, 2)),
+    ("project", 2, ("first", 1, 1), ("send", 1, 2), ("ready", 0, 2)),
+    ("unit", 4, ("third", 0, 3)),
+    ("project", 3, ("first", 1, 3), ("ready", 0, 3)),
     ("mid1", 0, ("second", 1, 1)),
-    ("layers", 2, ("first", 1, 2)),
+    ("layers", 0, ("first", 1, 2)),
     ("add", 0, ("third", 1, 1)),
-    ("grad", 0, ("second", 1, 3), ("z_sent", 1)),
+    ("grad", 0, ("z_sent", 1)),
+    ("layer3", 0, ("second", 1, 2), ("one", 1, 0)),
     ("layers", 3, ("ready", 1, 1)),
-    ("layers", 5, ("one", 1, 0), ("second", 1, 2)),
-    ("add", 5, ("third", 1, 3)),
-    ("grad", 3, ("two", 1, 0), ("third", 1, 2), ("sent", 1, 1)),
-    ("layer3", 1, ("ready", 1, 3)),
-    ("layers", 6, ("one", 1, 1), ("ready", 1, 2)),
-    ("grad", 6, ("three", 1, 0), ("two", 1, 1), ("sent", 1, 2)),
-    ("layers", 11, ("one", 1, 2)),
-    ("add", 11, ("two", 1, 2)),
+    ("add", 4, ("second", 1, 3)),
+    ("grad", 3, ("third", 1, 2), ("two", 1, 0), ("sent", 1, 1)),
+    ("layer3", 1, ("ready", 1, 2)),
+    ("layers", 6, ("one", 1, 1)),
+    ("layers", 8, ("third", 1, 3)),
+    ("add", 7, ("two", 1, 1)),
+    ("grad", 6, ("sent", 1, 2)),
+    ("layer3", 2, ("one", 1, 2), ("ready", 1, 3)),
+    ("add", 10, ("two", 1, 2), ("three", 1, 1)),
     ("grad", 9, ("sent", 1, 3)),
-    ("layer3", 3, ("three", 1, 1)),
-    ("down0", 0, ("one", 1, 3)),
-    ("down2", 0, ("s0", 0), ("three", 1, 2), ("two", 1, 3)),
-    ("back", 1, ("four", 1, 1)),
+    ("layer3", 3, ("one", 1, 3)),
+    ("down0", 1, ("two", 1, 3)),
+    ("down2", 0, ("three", 1, 2)),
+    ("back", 0, ("s0", 0), ("four", 1, 1)),
+    ("turn", 0, ("three", 1, 3)),
     ("shard", 0, ("one", 0, 0)),
-    ("back", 2, ("s1", 0)),
-    ("turn", 1, ("four", 1, 2), ("two", 0, 0)),
-    ("shard", 1, ("one", 0, 1)),
-    ("back", 4, ("three", 1, 3)),
-    ("back", 5, ("two", 0, 1)),
-    ("turn", 2, ("s2", 0)),
-    ("back", 6, ("three", 0, 0), ("one", 0, 2)),
-    ("turn", 3, ("two", 0, 2), ("four", 1, 3)),
-    ("end0", 0, ("three", 0, 1), ("one", 0, 3)),
-    ("end1", 0, ("four", 1, 0), ("three", 0, 2)),
-    ("end2", 0, ("two", 0, 3), ("four", 0, 1)),
-    ("end3", 0, ("five", 1)),
-    ("end4", 0, ("four", 0, 2), ("three", 0, 3)),
-    ("end5", 0, ("four", 0, 0), ("four", 0, 3), ("s0", 1)),
-    ("end6", 0, ("s1", 1)),
-    ("end7", 0, ("after_first", 1), ("s2", 1)),
-    ("end8", 0, ("s3", 0), ("five", 0)),
-    ("end9", 0, ("after_second", 1)),
-    ("end11", 0, ("s4", 0), ("s3", 1)),
-    ("end12", 0, ("after_first", 0), ("after_second", 0)),
-    ("end13", 0, ("done", 1)),
-    ("end14", 0, ("s4", 1)),
-    ("end15", 0, ("done", 0)),
+    ("after", 0, ("four", 1, 2), ("three", 1, 0)),
+    ("back", 3, ("s1", 0), ("two", 0, 0)),
+    ("back", 4, ("four", 1, 3), ("one", 0, 1)),
+    ("turn", 2, ("s2", 0), ("two", 0, 1)),
+    ("shard", 2, ("one", 0, 2)),
+    ("after", 2, ("four", 1, 0)),
+    ("back", 6, ("two", 0, 2)),
+    ("turn", 3, ("three", 0, 1), ("three", 0, 0)),
+    ("shard", 3, ("one", 0, 3), ("three", 0, 2)),
+    ("end0", 0, ("s3", 0), ("two", 0, 3), ("five", 1), ("four", 0, 1)),
+    ("end1", 0, ("four", 0, 0)),
+    ("end2", 0, ("s4", 0), ("four", 0, 2)),
+    ("end4", 0, ("s0", 1), ("s1", 1), ("three", 0, 3), ("s2", 1), ("after_first", 1), ("s3", 1), ("four", 0, 3), ("five", 0), ("after_second", 1), ("s4", 1), ("done", 1), ("after_first", 0), ("after_second", 0), ("done", 0)),
 ]
 TILE = 256
 
@@ -362,6 +356,7 @@
     normed_two, turned_two, hid, dbs = r["normed_two"], r["turned_two"], r["hid"], r["dbs"]
     early, late, bias = r["early"], r["late"], r["bias"]
     rows_all, width = x.shape
+    held_units = r["p"].shape[0]
     part = a.shape[2]
     pieces = b.shape[1] // 2
     units = pieces * width
@@ -376,7 +371,8 @@
             blocks.append((window, start, min(2, (part - start) // HALF)))
 
     weights = [a, b]
-    own_copy = [pltpu.make_async_copy(r["own_a"], a.at[me], r["local"].at[0])]
+    own_copy = [pltpu.make_async_copy(r["own_a"], a.at[me, 0:3], r["local"].at[0])]
+    own_copy.append(pltpu.make_async_copy(r["own_p"], a.at[me, 3:4], r["local"].at[5]))
     own_copy.append(pltpu.make_async_copy(r["own_f"], b.at[me, 0:pieces], r["local"].at[1]))
     own_copy.append(pltpu.make_async_copy(r["own_g"], b.at[me, pieces:], r["local"].at[2]))
     own_copy.append(pltpu.make_async_copy(r["x_in"], hid.at[: r["x_in"].shape[0], :width], r["local"].at[3]))
@@ -623,10 +619,10 @@
         return ref.at[s, pl.ds(pl.multiple_of(at * half_rows, half_rows), half_rows)]
 
     def p_out(i):
-        return pltpu.make_async_copy(r["p"].at[i % 2], r["p_hbm"].at[i], r["p_sem"].at[i % 2])
+        return pltpu.make_async_copy(r["p"].at[i % held_units], r["p_hbm"].at[i], r["p_sem"].at[i % held_units])
 
     def p_in(i):
-        return pltpu.make_async_copy(r["p_hbm"].at[i], r["p"].at[i % 2], r["p_sem"].at[i % 2])
+        return pltpu.make_async_copy(r["p_hbm"].at[i], r["p"].at[i % held_units], r["p_sem"].at[i % held_units])
 
     def attend(i, s, at):
         attend_forward_unit(
@@ -634,7 +630,7 @@
             unit_view(k, s, at),
             unit_view(v, s, at),
             unit_view(mix, s, at),
-            r["p"].at[i % 2],
+            r["p"].at[i % held_units],
             fill.at[pl.ds(pl.multiple_of(at * half_rows, half_rows), half_rows)],
             rel,
             r["hot"],
@@ -645,7 +641,7 @@
     def attend_back(i, s, at):
         views = [unit_view(ref, s, at) for ref in (q, k, v)]
         attend_backward_unit(
-            *views, unit_view(mix, s, at), r["p"].at[i % 2], *views, table, relt, r["hott"], r["scr_b"], blocks
+            *views, unit_view(mix, s, at), r["p"].at[i % held_units], *views, table, relt, r["hott"], r["scr_b"], blocks
         )
 
     def mix_out(n):
@@ -729,9 +725,13 @@
         for rows in halves_of_rows:
             mix[s, rows, :part] = dot(dbs[rows, :width], a[s, 3], NT).astype(bf16)
 
+    def project_grad(s):
+        turned = jnp.concatenate([source[s, :, :part].T for source in (q, k, v)], axis=0)
+        for n in range(columns):
+            tile = slice(n * TILE, (n + 1) * TILE)
+            ga[s, 0:3, :, tile] = dot(turned, normed[:, tile]).astype(bf16).reshape(3, part, TILE)
+
     def project_back(s):
-        for t, source in enumerate((q, k, v)):
-            ga[s, t] = dot(source[s, :, :part], normed[...], TN).astype(bf16)
         for i, source in ((0, q), (1, v)):
             value = jnp.sum(source[s, :, :part].astype(f32), axis=0, keepdims=True)
             first_lane = i * (width // 2)
@@ -756,9 +756,14 @@
         late[0:1] = late[0:1] + jnp.sum(gradient * normal, axis=0, keepdims=True)
         late[1:2] = late[1:2] + jnp.sum(gradient, axis=0, keepdims=True)
 
+    last = tp - 1
     plan = make_plan(tp, tiles, columns)
 
     def run(name, index=0):
+        if isinstance(index, int):
+            for fn, *args in plan.get(name, {}).get(index, []):
+                do[fn](*args)
+            return
         for at, steps in sorted(plan.get(name, {}).items()):
 
             @pl.when(index == at)
@@ -769,6 +774,7 @@
     def bias_ready():
         repeat(tp, lambda j: bias_copy(place.other(j), True).wait_recv(), 1)
 
+    turn_of = lambda w, j: last - j if w == 0 else j
     do = dict(
         send=send,
         first=first,
@@ -777,10 +783,10 @@
         ready=ready,
         sent=sent,
         bias_ready=bias_ready,
-        one=lambda w, j: reduce_one(w, place.other(j)),
-        two=lambda w, j: reduce_two(w, place.other(j)),
-        three=lambda w, j: reduce_three(w, place.other(j)),
-        four=reduce_four,
+        one=lambda w, j: reduce_one(w, place.other(turn_of(w, j))),
+        two=lambda w, j: reduce_two(w, place.other(turn_of(w, j))),
+        three=lambda w, j: reduce_three(w, place.other(turn_of(w, j))),
+        four=lambda w, j: reduce_four(w, turn_of(w, j)),
         z_sent=z_sent,
         five=reduce_five,
         after_first=lambda w: out_spread(w).after_first(),
@@ -796,20 +802,40 @@
     place.greet_start()
     for copy in own_copy:
         copy.start()
+    vec[...] = jnp.zeros_like(vec)
+    for at, name in ((0, "gain"), (2, "shift")):
+        vec[at : at + 2] = r[name][...].astype(f32)
+    vec[4] = r["b_proj"][...].astype(f32)
+    vec[5] = r["b_fc2"][...].astype(f32)
+    vec[8:10, :part] = r["b_qv"][...].astype(f32)
+    for i in range(pieces):
+        vec[10 + i] = r["b_fc1"][i * width : (i + 1) * width].astype(f32)
     bias[me] = vec[8:16]
+    offsets = r["offsets"]
+    offsets[...] = jnp.zeros_like(offsets)
+    for at in range(2 * WIN - 1):
+        pair = r["rel_pos"][at].astype(f32)
+        for axis in range(2):
+            offsets[32 * axis + at : 32 * axis + at + 1, :HEAD_DIM] = pair[axis : axis + 1]
+    offsets[...] = offsets[...] + pltpu.roll(offsets[...], HALF, 1)
     for copy in own_copy:
         copy.wait()
     place.greet_wait()
     run("start")
     repeat(tp, lambda j: bias_copy(place.other(tp - j), False).start(), 1)
     slots = r["x_in"].shape[0] // windows
-    for window in range(windows):
-        for staged, target in ((hid, x), (dbs, cot)):
+
+    def unpack_rows(staged, target):
+        for window in range(windows):
             target[window * PAD : window * PAD + slots] = staged[window * slots : (window + 1) * slots, :width]
             target[window * PAD + slots : (window + 1) * PAD] = jnp.zeros((PAD - slots, width), bf16)
+
+    unpack_rows(hid, x)
+    run("warm", 0)
     repeat(chunks, norm_one)
+    run("warm", 1)
     repeat(chunks, fill_rows)
-    picked = dot(r["pick"][...], r["offsets"][...])
+    picked = dot(r["pick"][...], offsets[...].astype(bf16))
     lane = lax.broadcasted_iota(jnp.int32, picked.shape, 1)
     head = lax.broadcasted_iota(jnp.int32, picked.shape, 0)
     picked = jnp.where((lane < HALF) == (head < HALF), picked, 0.0)
@@ -834,22 +860,24 @@
 
         run("unit", i)
 
-        @pl.when(i >= 2)
+        @pl.when(i >= held_units)
         def _():
-            p_out(i - 2).wait()
+            p_out(i - held_units).wait()
 
         attend(i, s, at)
-        p_out(i).start()
+
+        @pl.when(i < unit_count - held_units)
+        def _():
+            p_out(i).start()
 
     unit_count = 2 * tp
     repeat(unit_count, forward_unit)
     run("mid")
-    p_out(unit_count - 2).wait()
-    p_out(unit_count - 1).wait()
     repeat(columns, mix_out)
     run("mid1")
     repeat(chunks, norm_two)
     turned_two[...] = normed_two[...].T
+    unpack_rows(dbs, cot)
 
     def layer_step(j):
         s = place.other(j)
@@ -860,34 +888,40 @@
 
     repeat(tp, layer_step)
 
-    run("down0")
-    repeat(chunks, middle_back)
+    for at in range(2):
+        run("down0", at)
+        repeat(chunks * (at + 1) // 2, middle_back, chunks * at // 2)
     for window in range(windows):
         normed_two[window * slots : (window + 1) * slots] = hid[window * PAD : window * PAD + slots, :width]
     put_out = pltpu.make_async_copy(normed_two.at[: windows * slots], r["out"], r["local"].at[1])
     put_out.start()
     run("down1")
-    p_in(0).start()
     repeat(tp, lambda j: mix_back(place.other(j)))
     run("down2")
 
     def backward_unit(i):
         j, at = i // 2, i % 2
-        s = place.other(j)
+        s = place.other(last - j)
+        unit = 2 * (last - j) + at
         run("back", i)
 
-        @pl.when(i + 1 < unit_count)
+        @pl.when(unit < unit_count - held_units)
         def _():
-            p_in(i + 1).start()
-
-        p_in(i).wait()
-        attend_back(i, s, at)
+            p_in(unit).wait()
+
+        attend_back(unit, s, at)
+
+        @pl.when(unit >= held_units)
+        def _():
+            p_in(unit - held_units).start()
 
         @pl.when(at == 1)
         def _():
             run("turn", j)
+            project_grad(s)
+            run("shard", j)
             project_back(s)
-            run("shard", j)
+            run("after", j)
 
     repeat(unit_count, backward_unit)
     for at in range(4):
@@ -991,7 +1025,7 @@
     return plan
 
 
-def whole_block(tp, dp, x, cot, heights, widths, vec, own_a, own_f, own_g, offsets):
+def whole_block(tp, dp, x, cot, heights, widths, gain, shift, b_qv, b_proj, b_fc1, b_fc2, rel_pos, own_a, own_p, own_f, own_g):
     width = x.shape[1]
     windows = x.shape[0] // SLOTS
     rows = windows * PAD
@@ -1001,6 +1035,7 @@
     heads = (windows // 2) * (part // HEAD_DIM)
     wide = -(-part // LANES) * LANES
     unit_count = 2 * tp
+    held_units = 4 if dp <= 8 else 2
     hot, hott, pick = window_constants()
     scalar = pl.BlockSpec(memory_space=pltpu.SMEM)
     any_space = pl.BlockSpec(memory_space=pl.ANY)
@@ -1011,11 +1046,17 @@
         ("cot_in", cot, any_space),
         ("heights", heights, scalar),
         ("widths", widths, scalar),
-        ("vec", vec, vmem),
+        ("gain", gain, vmem),
+        ("shift", shift, vmem),
+        ("b_qv", b_qv, vmem),
+        ("b_proj", b_proj, vmem),
+        ("b_fc1", b_fc1, vmem),
+        ("b_fc2", b_fc2, vmem),
+        ("rel_pos", rel_pos, vmem),
         ("own_a", own_a, any_space),
+        ("own_p", own_p, any_space),
         ("own_f", own_f, any_space),
         ("own_g", own_g, any_space),
-        ("offsets", offsets, vmem),
         ("hot", hot, vmem),
         ("hott", hott, vmem),
         ("pick", pick, vmem),
@@ -1024,28 +1065,30 @@
     outputs = [
         ("out", shape(x.shape, bf16), any_space),
         ("grad_x", shape(x.shape, f32), any_space),
-        ("out_a", shape(own_a.shape, bf16), any_space),
+        ("out_a", shape((4, part, width), bf16), any_space),
         ("out_b", shape((2 * pieces, width, width), bf16), any_space),
         ("early_out", shape((8, width), f32), vmem),
         ("late_out", shape((8, width), f32), vmem),
         ("fold_out", shape((32, LANES), f32), vmem),
-        ("p_hbm", shape((unit_count, heads, PAD, PAD), bf16), any_space),
+        ("p_hbm", shape((max(unit_count - held_units, 1), heads, PAD, PAD), bf16), any_space),
     ]
     buffer = lambda dims, kind: pltpu.VMEM(tuple(dims), kind)
     scratch = [
-        ("a", buffer((tp,) + own_a.shape, bf16)),
+        ("a", buffer((tp, 4, part, width), bf16)),
         ("b", buffer((tp, 2 * pieces, width, width), bf16)),
-        ("ga", buffer((tp,) + own_a.shape, bf16)),
+        ("ga", buffer((tp, 4, part, width), bf16)),
         ("bias", buffer((tp, 8, width), f32)),
         ("x", buffer((rows, width), bf16)),
         ("cot", buffer((rows, width), bf16)),
         ("fill", buffer((rows, LANES), f32)),
+        ("vec", buffer((16, width), f32)),
+        ("offsets", buffer((HALF, LANES), f32)),
         ("rel", buffer((LANES, LANES), bf16)),
         ("relt", buffer((LANES, LANES), bf16)),
         ("normed", buffer((rows, width), bf16)),
     ]
     scratch += [(name, buffer((tp, rows, wide), bf16)) for name in ("q", "k", "v", "mix")]
-    scratch += [("p", buffer((2, heads, PAD, PAD), bf16))]
+    scratch += [("p", buffer((held_units, heads, PAD, PAD), bf16))]
     scratch += [(name, buffer((rows, width), f32)) for name in ("middle", "total", "slide")]
     scratch += [("normed_two", buffer((rows, width), bf16)), ("turned_two", buffer((width, rows), bf16))]
     scratch += [(name, buffer((rows, units), bf16)) for name in ("hid", "dbs")]
@@ -1059,7 +1102,7 @@
     ]
     levels = dp.bit_length() - 1
     more = levels - 3
-    for w, own in enumerate((own_a.shape, (2 * pieces, width, width))):
+    for w, own in enumerate(((4, part, width), (2 * pieces, width, width))):
         n, count, lanes = own[0], own[1], own[2] // 2
         scratch += [
             ("h" + str(w), buffer((tp, n, count, lanes), bf16)),
@@ -1072,7 +1115,7 @@
             scratch += [("x" + str(w), buffer((more, n, count // 4, lanes), bf16))]
     for name, dims in (("early", (8, width)), ("late", (8, width)), ("fold", (32, LANES))):
         scratch += [(name + "_in", buffer((levels,) + dims, f32)), (name + "_z", buffer((tp,) + dims, f32))]
-    semaphores = dict(local=(5,), p_sem=(2,), put=(2,))
+    semaphores = dict(local=(6,), p_sem=(held_units,), put=(2,))
     for name, dims in dict(
         z=(2, tp), p=(2, tp, 4), b=(tp,), core=(2, tp), one=(2, tp), two=(2, tp), s=(2, tp), q=(2, 4), x=(2, max(more, 1)), v=(3, levels), vz=(3, tp)
     ).items():
@@ -1087,6 +1130,86 @@
         scratch_shapes=[entry[1] for entry in scratch],
         compiler_params=pltpu.CompilerParams(collective_id=1, has_side_effects=True, vmem_limit_bytes=VMEM_LIMIT),
     )(*[entry[1] for entry in inputs])
+
+
+def finish_kernel(
+    a_ref, b_ref, o_ref, x_ref, early, late, fold, qkv, proj, fc1, fc2, o, x, gain, shift, qv, rel, b_proj, b_fc1, b_fc2, *scratch
+):
+    a, b, wide_qkv, wide_proj, wide_fc1, wide_fc2, held_o, held_x, sem_in, sem_out = scratch
+    pieces = b.shape[0] // 2
+    width = b.shape[1]
+    part = a.shape[1]
+    me = lax.axis_index("tp")
+    loads = [pltpu.make_async_copy(b_ref.at[i], b.at[i], sem_in.at[i]) for i in range(2 * pieces)]
+    loads += [pltpu.make_async_copy(a_ref.at[i], a.at[i], sem_in.at[2 * pieces + i]) for i in range(4)]
+    loads.append(pltpu.make_async_copy(o_ref, held_o, sem_in.at[2 * pieces + 4]))
+    loads.append(pltpu.make_async_copy(x_ref, held_x, sem_in.at[2 * pieces + 5]))
+    for copy in loads:
+        copy.start()
+    stores = []
+
+    def store(value, out):
+        copy = pltpu.make_async_copy(value, out, sem_out.at[len(stores)])
+        copy.start()
+        stores.append(copy)
+
+    count = 2 * WIN - 1
+    gain[0:1], gain[1:2] = late[0:1], early[0:1]
+    shift[0:1], shift[1:2] = late[1:2], early[1:2]
+    mine = late[pl.ds(2 + me, 1), :]
+    qv[0:1], qv[1:2] = mine[:, :part], mine[:, width // 2 : width // 2 + part]
+    for at in range(count):
+        for axis in range(2):
+            rel[at, axis : axis + 1, :] = fold[count - 1 - at : count - at, axis * HALF : (axis + 1) * HALF]
+    b_proj[...] = early[2]
+    b_fc2[...] = early[3]
+    for i in range(pieces):
+        b_fc1[i * width : (i + 1) * width] = early[pl.ds(4 + me * pieces + i, 1), :].reshape(width)
+    for i in range(pieces):
+        loads[i].wait()
+        wide_fc1[:, i * width : (i + 1) * width] = b[i].astype(f32)
+    store(wide_fc1, fc1)
+    for i in range(pieces):
+        loads[pieces + i].wait()
+        wide_fc2[i * width : (i + 1) * width, :] = b[pieces + i].astype(f32)
+    store(wide_fc2, fc2)
+    for t in range(3):
+        loads[2 * pieces + t].wait()
+        wide_qkv[t] = a[t].astype(f32)
+        store(wide_qkv.at[t], qkv.at[t])
+    loads[2 * pieces + 3].wait()
+    wide_proj[...] = a[3].astype(f32)
+    store(wide_proj, proj)
+    loads[2 * pieces + 4].wait()
+    store(held_o, o)
+    loads[2 * pieces + 5].wait()
+    store(held_x, x)
+    for copy in stores:
+        copy.wait()
+
+
+def finish(out_a, out_b, out, grad_x, early, late, fold):
+    part, width = out_a.shape[1:]
+    pieces = out_b.shape[0] // 2
+    units = pieces * width
+    any_space = pl.BlockSpec(memory_space=pl.ANY)
+    vmem = pl.BlockSpec(memory_space=pltpu.VMEM)
+    large = [(3, part, width), (part, width), (width, units), (units, width)]
+    small = [(2, width), (2, width), (2, part), (2 * WIN - 1, 2, HEAD_DIM), (width,), (units,), (width,)]
+    shape = jax.ShapeDtypeStruct
+    return pl.pallas_call(
+        finish_kernel,
+        in_specs=[any_space] * 4 + [vmem] * 3,
+        out_specs=[any_space] * 6 + [vmem] * 7,
+        out_shape=[shape(dims, f32) for dims in large]
+        + [shape(out.shape, bf16), shape(grad_x.shape, f32)]
+        + [shape(dims, f32) for dims in small],
+        scratch_shapes=[pltpu.VMEM(out_a.shape, bf16), pltpu.VMEM(out_b.shape, bf16)]
+        + [pltpu.VMEM(dims, f32) for dims in large]
+        + [pltpu.VMEM(out.shape, bf16), pltpu.VMEM(grad_x.shape, f32)]
+        + [pltpu.SemaphoreType.DMA((2 * pieces + 6,)), pltpu.SemaphoreType.DMA((8,))],
+        compiler_params=pltpu.CompilerParams(vmem_limit_bytes=VMEM_LIMIT),
+    )(out_a, out_b, out, grad_x, early, late, fold)
 
 
 def body(
@@ -1110,34 +1233,43 @@
     width = tokens.shape[1]
     part, units = w_qkv.shape[2], w_fc1.shape[1]
     blocks = units // width
-    pad = lambda values, rows, lanes=0: jnp.pad(values, ((0, rows), (0, lanes)))
-    vec = [norm_gain, norm_bias, b_proj[None], pad(b_fc2[None], 2), pad(b_qv, 0, width - part)]
-    vec = jnp.concatenate(vec + [pad(b_fc1.reshape(blocks, width), 6 - blocks)]).astype(f32)
-    offsets = jnp.pad(rel_pos, ((0, 0), (0, 32 - rel_pos.shape[1]), (0, 0))).reshape(HALF, HEAD_DIM)
-    offsets = jnp.concatenate([offsets, offsets], axis=1)
-    turned = jnp.concatenate([w_qkv.transpose(0, 2, 1), w_proj[None]], axis=0)
     first = w_fc1[None] if blocks == 1 else w_fc1.reshape(width, blocks, width).transpose(1, 0, 2)
     out, grad_x, out_a, out_b, early, late, fold, _ = whole_block(
-        tp, dp, tokens, cotangent, heights, widths, vec, turned, first, w_fc2.reshape(blocks, width, width), offsets
+        tp,
+        dp,
+        tokens,
+        cotangent,
+        heights,
+        widths,
+        norm_gain,
+        norm_bias,
+        b_qv,
+        b_proj,
+        b_fc1,
+        b_fc2,
+        rel_pos.transpose(1, 0, 2),
+        w_qkv.transpose(0, 2, 1),
+        w_proj[None],
+        first,
+        w_fc2.reshape(blocks, width, width),
     )
-    me = lax.axis_index("tp")
-    count = 2 * WIN - 1
-    grad_rel = jnp.stack([fold[:count, :HALF], fold[:count, HALF:]])[:, ::-1, :]
-    mine = lax.dynamic_slice_in_dim(late, 2 + me, 1, 0)
+    qkv, proj, fc1, fc2, out, grad_x, gain, shift, qv, rel, proj_bias, fc1_bias, fc2_bias = finish(
+        out_a, out_b, out, grad_x, early, late, fold
+    )
     return (
         out,
         grad_x,
-        jnp.stack([late[0], early[0]]),
-        jnp.stack([late[1], early[1]]),
-        out_a[:3].transpose(0, 2, 1).astype(f32),
-        jnp.concatenate([mine[:, :part], mine[:, width // 2 : width // 2 + part]]),
-        grad_rel,
-        out_a[3].astype(f32),
-        early[2],
-        out_b[:blocks].transpose(1, 0, 2).reshape(width, units).astype(f32),
-        lax.dynamic_slice_in_dim(early, 4 + me * blocks, blocks, 0).reshape(-1),
-        out_b[blocks:].reshape(units, width).astype(f32),
-        early[3],
+        gain,
+        shift,
+        qkv.transpose(0, 2, 1),
+        qv,
+        rel.transpose(1, 0, 2),
+        proj,
+        proj_bias,
+        fc1,
+        fc1_bias,
+        fc2,
+        fc2_bias,
     )
 
 

time: 200 us -> 173 us (0.86)
  other arithmetic: 12.5 us -> 0 us
  local copies, waits for them, and re-layouts: 10.3 us -> 0 us
  Pallas kernels: 175 us -> 170 us
    pallas_call x1, Pallas kernels: 175 us -> 162 us  [whole_block(): pl.pallas_call(lambda *refs: block_kernel(tp, dp, names, *refs), in_specs...]
    pallas_call x0 -> x1, Pallas kernels: none -> 7.77 us  [finish(): pl.pallas_call(finish_kernel, in_specs=[any_space] * 4 + [vmem] * 3, out_...]
    convert_element_type x4 -> x0, other arithmetic: 7.65 us -> none  [the longest x1 2.67 us: body(): out_a[:3].transpose(0, 2, 1).astype(f32)]
    unnamed x14 -> x0, local copies, waits for them, and re-layouts: 4.19 us -> none
    concatenate x3 -> x0, other arithmetic: 3.65 us -> none  [the longest x1 2.38 us: body(): turned = jnp.concatenate([w_qkv.transpose(0, 2, 1), w_proj[None]], axis=0)]
    slice x2 -> x0, local copies, waits for them, and re-layouts: 2.46 us -> none  [the longest x1 1.67 us: body(): early[3]]
where the time goes in v4:
time: 173 us; the launch traced here: 172 us
  Pallas kernels  170 us (98%)
  between operations  2.11 us (1%)
    pallas_call x1, Pallas kernels, whole_block(): pl.pallas_call(lambda *refs: block_kernel(tp, dp, names, *refs), in_specs...  162 us
    pallas_call x1, Pallas kernels, finish(): pl.pallas_call(finish_kernel, in_specs=[any_space] * 4 + [vmem] * 3, out_...  7.77 us

profile of v4, /device:TPU:0, one launch (start us, length us, event | category | flops | bytes accessed | tf_op | source)
XLA Modules:
  0.0 172.1 jit_solution(5334799662436993323)
XLA Ops:
  1.9 162.2 %shard_map.273 = (bf16[784,768]{1,0:T(8,128)(2,1)}, f32[784,768]{1,0:T(8,128)}, bf16[4,192,768]{2,1,0:T(8,128)(2,1)}, bf16[2,768,768]{2,1,0:T(8,128)(2,1)}, f32[...) custom-call(bf16[784,768]{1,0:T(8,128)(2,1)} %refs_0_.1, ...), custom_call_target="tpu_custom_call" | custom-call | tf_op jit(solution)/shard_map/pallas_call | solution.py:1125
  164.1 7.8 %shard_map.274 = (f32[3,192,768]{2,1,0:T(8,128)}, f32[192,768]{1,0:T(8,128)}, f32[768,768]{1,0:T(8,128)}, f32[768,768]{1,0:T(8,128)}, bf16[784,768]{1,0:T(8,128)...) custom-call(bf16[4,192,768]{2,1,0:T(8,128)(2,1)} %get-tuple-element., ...), custom_call_target="tpu_custom_call" | custom-call | tf_op jit(solution)/shard_map/pallas_call | solution.py:1200

commit v5 on v4

--- a/solution.py
+++ b/solution.py
@@ -14,7 +14,7 @@
 PAD = 208
 LANES = 128
 HALF = 64
-CHUNK = 64
+CHUNK = 32
 ENDS = 20
 PLACES = [
     ("start", 0, ("send", 0, 1)),

time: 173 us -> 185 us (1.069)
  Pallas kernels: 170 us -> 182 us
    pallas_call x1, Pallas kernels: 162 us -> 174 us  [whole_block(): pl.pallas_call(lambda *refs: block_kernel(tp, dp, names, *refs), in_specs...]
where the time goes in v5:
time: 185 us; the launch traced here: 184 us
  Pallas kernels  182 us (98%)
  between operations  2.11 us (1%)
    pallas_call x1, Pallas kernels, whole_block(): pl.pallas_call(lambda *refs: block_kernel(tp, dp, names, *refs), in_specs...  174 us
    pallas_call x1, Pallas kernels, finish(): pl.pallas_call(finish_kernel, in_specs=[any_space] * 4 + [vmem] * 3, out_...  7.77 us

profile of v5, /device:TPU:0, one launch (start us, length us, event | category | flops | bytes accessed | tf_op | source)
XLA Modules:
  0.0 183.8 jit_solution(6847458031565571453)
XLA Ops:
  1.9 173.9 %shard_map.273 = (bf16[784,768]{1,0:T(8,128)(2,1)}, f32[784,768]{1,0:T(8,128)}, bf16[4,192,768]{2,1,0:T(8,128)(2,1)}, bf16[2,768,768]{2,1,0:T(8,128)(2,1)}, f32[...) custom-call(bf16[784,768]{1,0:T(8,128)(2,1)} %refs_0_.1, ...), custom_call_target="tpu_custom_call" | custom-call | tf_op jit(solution)/shard_map/pallas_call | solution.py:1125
  175.9 7.8 %shard_map.274 = (f32[3,192,768]{2,1,0:T(8,128)}, f32[192,768]{1,0:T(8,128)}, f32[768,768]{1,0:T(8,128)}, f32[768,768]{1,0:T(8,128)}, bf16[784,768]{1,0:T(8,128)...) custom-call(bf16[4,192,768]{2,1,0:T(8,128)(2,1)} %get-tuple-element., ...), custom_call_target="tpu_custom_call" | custom-call | tf_op jit(solution)/shard_map/pallas_call | solution.py:1200
